TPU v7x, 32 devices: a whole 2x2x4 slice. The times are simulated.
32 devices in a mesh: gx: 4 (over z), gy: 2 (over x), gz: 4 (over y, core).
Axes of the slice: x: 2, y: 2, z: 4, core: 2. Of those that a mesh axis runs over, the one named last changes fastest.
Arguments:
- populations: float32 [19, 16, 16, 512], P(None, 'gx', 'gy', 'gz'), may hold values from -0.1 to 0.7
- solid_class: int32 [16, 16, 512], P('gx', 'gy', 'gz'), may hold values from 0 to 3
- part_offset: float32 [512, 3, 128], P(('gx', 'gy', 'gz')), may hold values from -0.5 to 0.5
- part_velocity: float32 [512, 3, 128], P(('gx', 'gy', 'gz')), may hold values from -0.75 to 0.75
- part_drag: float32 [512, 128], P(('gx', 'gy', 'gz')), may hold values from 0.1 to 0.9
- part_cell: int32 [512, 128], P(('gx', 'gy', 'gz')), may hold values from 0 to 4095
- block_rows: int32 [512], P(('gx', 'gy', 'gz')), may hold values from 1 to 128, as said below
- block_dest: int32 [512, 1], P(('gx', 'gy', 'gz')), may hold values from 0 to 3; in each aligned block of 16 rows (0 to 15, 16 to 31, ...) at most 8 rows name the same one
Outputs:
- fluid_velocity: float32 [3, 16, 16, 512], P(None, 'gx', 'gy', 'gz')
- particle_velocity: float32 [1024, 3, 128], P(('gx', 'gy', 'gz'))
Inputs may be any that keep to these rules, and one draw needn't show every extreme that they name: Rows 0 to block_rows - 1 of a block hold particles; the first block of every device is full. `block_dest`: among the 16 blocks of one device no target is named more than 8 times, and on some devices one target is named exactly 8 times. `part_cell`: local index (p * 8 + q) * 128 + s of the cell in the target brick.
All inputs are finite; a program needn't handle non-finite values.
Results may differ from a plain program's by a relative error of at most 0.0003.
Values sent between devices are 32-bit elements; how exact they have to be, the bound alone decides.
A program may use at most 128 MiB of HBM per device.

v0:
```python
import jax
import jax.numpy as jnp
from jax import lax
from jax.sharding import PartitionSpec as P

STEPS = 2


directions = (
    (0, 0, 0),
    (1, 0, 0),
    (-1, 0, 0),
    (0, 1, 0),
    (0, -1, 0),
    (0, 0, 1),
    (0, 0, -1),
    (1, 1, 0),
    (-1, -1, 0),
    (1, -1, 0),
    (-1, 1, 0),
    (1, 0, 1),
    (-1, 0, -1),
    (1, 0, -1),
    (-1, 0, 1),
    (0, 1, 1),
    (0, -1, -1),
    (0, 1, -1),
    (0, -1, 1),
)
weights = (1.0 / 3.0,) + (1.0 / 18.0,) * 6 + (1.0 / 36.0,) * 12
opposite = (0, 2, 1, 4, 3, 6, 5, 8, 7, 10, 9, 12, 11, 14, 13, 16, 15, 18, 17)
relax_rate = 1.25
speed_unit = 0.05


def with_halo(cells, sides, width):
    for axis, dim in sides:
        count = lax.axis_size(axis)
        head = lax.slice_in_dim(cells, 0, width, axis=dim)
        tail = lax.slice_in_dim(cells, cells.shape[dim] - width, cells.shape[dim], axis=dim)
        cells = jnp.concatenate(
            [
                lax.ppermute(tail, axis, [(i, (i + 1) % count) for i in range(count)]),
                cells,
                lax.ppermute(head, axis, [((i + 1) % count, i) for i in range(count)]),
            ],
            axis=dim,
        )
    return cells


def project(vector, direction):
    summed = None
    for d in range(3):
        if direction[d] != 0:
            signed = vector[d] if direction[d] > 0 else -vector[d]
            summed = signed if summed is None else summed + signed
    return summed


def moments(fields):
    density = fields[0]
    for i in range(1, 19):
        density = density + fields[i]
    components = []
    for d in range(3):
        summed = None
        for i in range(1, 19):
            if directions[i][d] != 0:
                signed = fields[i] if directions[i][d] > 0 else -fields[i]
                summed = signed if summed is None else summed + signed
        components.append(summed)
    return (density, jnp.stack(components))


def collide(fields, density, velocity, cell_force, gray_fraction):
    flow_square = velocity[0] * velocity[0] + velocity[1] * velocity[1] + velocity[2] * velocity[2]
    post_list = []
    for i in range(19):
        baseline = density - 1.5 * flow_square
        if i > 0:
            along_flow = project(velocity, directions[i])
            along_force = project(cell_force, directions[i])
            baseline = baseline + 3.0 * along_flow + 4.5 * along_flow * along_flow
        equilibrium = weights[i] * baseline
        relaxed = fields[i] + relax_rate * (equilibrium - fields[i])
        if i > 0:
            relaxed = relaxed + 3.0 * weights[i] * along_force
        post_list.append((1.0 - gray_fraction) * relaxed + gray_fraction * fields[opposite[i]])
    return post_list


def corner_table(places, offset, extents):
    options = []
    for d in range(3):
        displace = offset[:, d, :]
        step_sign = jnp.where(displace >= 0.0, 1, -1).astype(jnp.int32)
        options.append(
            ((places[d], 1.0 - jnp.abs(displace)), (places[d] + step_sign, jnp.abs(displace)))
        )
    corners = []
    for a in options[0]:
        for b in options[1]:
            for c in options[2]:
                flat_index = ((a[0] * extents[1] + b[0]) * extents[2] + c[0]).astype(jnp.int32)
                corners.append((flat_index, a[1] * b[1] * c[1]))
    return corners


def fold_ghost(widened, dim):
    length = widened.shape[dim] - 4
    folded = lax.slice_in_dim(widened, 2, length + 2, axis=dim)
    lower = lax.slice_in_dim(widened, 0, 1, axis=dim)
    upper = lax.slice_in_dim(widened, length + 3, length + 4, axis=dim)
    lower_pad = [(0, 0)] * 4
    upper_pad = [(0, 0)] * 4
    lower_pad[dim] = (0, length - 1)
    upper_pad[dim] = (length - 1, 0)
    return folded + jnp.pad(lower, lower_pad) + jnp.pad(upper, upper_pad)


def move_layers(layers, moving, widened, dim):
    for k, i in enumerate(moving):
        extent = layers[i].shape[dim]
        start = 1 - directions[i][dim]
        layers[i] = lax.slice_in_dim(widened[k], start, start + extent, axis=dim)
    return layers


def propagate_by_axis(post_list):
    layers = list(post_list)
    moving = [i for i in range(19) if directions[i][0] != 0]
    widened = with_halo(jnp.stack([layers[i] for i in moving]), (("gx", 1),), 1)
    layers = move_layers(layers, moving, widened, 0)
    moving = [i for i in range(19) if directions[i][1] != 0]
    widened = with_halo(jnp.stack([layers[i] for i in moving]), (("gy", 2),), 1)
    layers = move_layers(layers, moving, widened, 1)
    moving = [i for i in range(19) if directions[i][2] != 0]
    widened = with_halo(jnp.stack([layers[i] for i in moving]), (("gz", 3),), 1)
    layers = move_layers(layers, moving, widened, 2)
    return layers


def per_device(
    populations,
    solid_class,
    part_offset,
    part_velocity,
    part_drag,
    part_cell,
    block_rows,
    block_dest,
):
    size_x, size_y, size_z = (populations.shape[1], populations.shape[2], populations.shape[3])
    rows_block = part_cell.shape[1]
    block_count = block_dest.shape[0]
    peers = lax.axis_size("gx")
    capacity = 2 * block_count // peers
    slot_count = peers * capacity
    destination = block_dest[:, 0]
    onehot = (destination[:, None] == jnp.arange(peers, dtype=jnp.int32)[None, :]).astype(jnp.int32)
    before = jnp.cumsum(onehot, axis=0) - onehot
    block_rank = jnp.sum(before * onehot, axis=1)
    slot_index = destination * capacity + block_rank
    match = slot_index[None, :] == jnp.arange(slot_count, dtype=jnp.int32)[:, None]
    filled = jnp.any(match, axis=1)
    source = jnp.sum(jnp.where(match, jnp.arange(block_count, dtype=jnp.int32)[None, :], 0), axis=1)
    floats = jnp.concatenate([part_offset, part_velocity, part_drag[:, None, :]], axis=1)
    send_floats = jnp.where(filled[:, None, None], jnp.take(floats, source, axis=0), 0.0)
    send_cells = jnp.where(filled[:, None], jnp.take(part_cell, source, axis=0), 0)
    send_rows = jnp.where(filled, jnp.take(block_rows, source, axis=0), 0)
    got_floats, got_cells, got_rows = (
        lax.all_to_all(send_floats, "gx", split_axis=0, concat_axis=0, tiled=True),
        lax.all_to_all(send_cells, "gx", split_axis=0, concat_axis=0, tiled=True),
        lax.all_to_all(send_rows, "gx", split_axis=0, concat_axis=0, tiled=True),
    )
    offset = got_floats[:, 0:3, :]
    velocity = got_floats[:, 3:6, :]
    drag_rate = got_floats[:, 6, :]
    live_rows = jnp.arange(rows_block, dtype=jnp.int32)[None, :] < got_rows[:, None]
    p = got_cells // (size_y * size_z) + 1
    q = got_cells // size_z % size_y + 1
    s = got_cells % size_z + 1
    corners = corner_table((p, q, s), offset, (size_x + 2, size_y + 2, size_z + 2))
    gray_fraction = solid_class.astype(jnp.float32) * 0.25
    fields = populations
    for repeat in range(STEPS):
        density, flow = moments(fields)
        rim_field = with_halo(flow, (("gx", 1), ("gy", 2), ("gz", 3)), 1)
        flattened = rim_field.reshape(3, -1)
        sampled = jnp.zeros_like(velocity)
        for flat_index, weight in corners:
            sampled = sampled + weight[:, None, :] * jnp.moveaxis(flattened[:, flat_index], 0, 1)
        drag_force = jnp.where(
            live_rows[:, None, :], drag_rate[:, None, :] * (sampled - velocity), 0.0
        )
        velocity = velocity + drag_force
        ghosts = jnp.zeros_like(flattened)
        for flat_index, weight in corners:
            ghosts = ghosts.at[:, flat_index].add(
                jnp.moveaxis(-weight[:, None, :] * drag_force, 1, 0)
            )
        ghosts = ghosts.reshape(3, size_x + 2, size_y + 2, size_z + 2)
        widened = with_halo(ghosts, (("gx", 1), ("gy", 2), ("gz", 3)), 1)
        cell_force = fold_ghost(fold_ghost(fold_ghost(widened, 1), 2), 3)
        post_list = collide(fields, density, flow, cell_force, gray_fraction)
        fields = jnp.stack(propagate_by_axis(post_list))
    density, flow = moments(fields)
    fluid_velocity = flow / speed_unit
    particle_velocity = jnp.where(live_rows[:, None, :], velocity / speed_unit, 0.0)
    return (fluid_velocity, particle_velocity)


def solution(mesh):
    in_specs = (
        P(None, "gx", "gy", "gz"),
        P("gx", "gy", "gz"),
        P(("gx", "gy", "gz"), None, None),
        P(("gx", "gy", "gz"), None, None),
        P(("gx", "gy", "gz"), None),
        P(("gx", "gy", "gz"), None),
        P(("gx", "gy", "gz")),
        P(("gx", "gy", "gz"), None),
    )
    out_specs = (P(None, "gx", "gy", "gz"), P(("gx", "gy", "gz"), None, None))
    return jax.shard_map(
        per_device, mesh=mesh, in_specs=in_specs, out_specs=out_specs, check_vma=False
    )
```

profile of v0, /device:TPU:0, one launch (start us, length us, event | category | flops | bytes accessed | tf_op | source)
XLA Modules:
  0.0 919.2 jit_solution(7450403598556893674)
XLA Ops:
  3.3 3.1 collective-permute-start
  6.4 2.1 collective-permute-start.1
  13.1 3.2 all-to-all-start.2
  23.6 5.1 all-to-all-start.1
  32.0 2.7 collective-permute-done.4
  35.9 2.8 copy.364
  38.8 5.6 all-to-all-start
  44.5 5.5 all-to-all-done
  50.3 12.9 %gather_fusion.3 = f32[4096,3]{1,0:T(8,128)S(1)} fusion(f32[3,7800]{0,1:T(8,128)} %copy.364, s32[4096]{0:T(1024)S(1)} %get-tuple-element.199), kind=kCustom, calls=%fused_computation.3 | custom fusion | bytes 114688 | tf_op jit(solution)/shard_map/gather | solution.py:193
  63.8 12.9 %gather_fusion.4 = f32[4096,3]{1,0:T(8,128)S(1)} fusion(f32[3,7800]{0,1:T(8,128)} %copy.364, s32[4096]{0:T(1024)S(1)} %get-tuple-element.34), kind=kCustom, calls=%fused_computation.4 | custom fusion | bytes 114688 | tf_op jit(solution)/shard_map/gather | solution.py:193
  77.3 12.9 %gather_fusion.5 = f32[4096,3]{1,0:T(8,128)S(1)} fusion(f32[3,7800]{0,1:T(8,128)} %copy.364, s32[4096]{0:T(1024)S(1)} %get-tuple-element.188), kind=kCustom, calls=%fused_computation.5 | custom fusion | bytes 114688 | tf_op jit(solution)/shard_map/gather | solution.py:193
  90.9 12.9 %gather_fusion.6 = f32[4096,3]{1,0:T(8,128)S(1)} fusion(f32[3,7800]{0,1:T(8,128)} %copy.364, s32[4096]{0:T(1024)S(1)} %get-tuple-element.186), kind=kCustom, calls=%fused_computation.6 | custom fusion | bytes 114688 | tf_op jit(solution)/shard_map/gather | solution.py:193
  104.4 12.9 %gather_fusion.8 = f32[4096,3]{1,0:T(8,128)S(1)} fusion(f32[3,7800]{0,1:T(8,128)} %copy.364, s32[4096]{0:T(1024)S(1)} %get-tuple-element.180), kind=kCustom, calls=%fused_computation.8 | custom fusion | bytes 114688 | tf_op jit(solution)/shard_map/gather | solution.py:193
  118.0 12.9 %gather_fusion.9 = f32[4096,3]{1,0:T(8,128)S(1)} fusion(f32[3,7800]{0,1:T(8,128)} %copy.364, s32[4096]{0:T(1024)S(1)} %get-tuple-element.182), kind=kCustom, calls=%fused_computation.9 | custom fusion | bytes 114688 | tf_op jit(solution)/shard_map/gather | solution.py:193
  131.5 12.9 %gather_fusion.10 = f32[4096,3]{1,0:T(8,128)S(1)} fusion(f32[3,7800]{0,1:T(8,128)} %copy.364, s32[4096]{0:T(1024)S(1)} %get-tuple-element.184), kind=kCustom, calls=%fused_computation.10 | custom fusion | bytes 114688 | tf_op jit(solution)/shard_map/gather | solution.py:193
  145.0 12.9 %gather_fusion.7 = f32[4096,3]{1,0:T(8,128)S(1)} fusion(f32[3,7800]{0,1:T(8,128)} %copy.364, s32[4096]{0:T(1024)S(1)} %get-tuple-element.40), kind=kCustom, calls=%fused_computation.7 | custom fusion | bytes 114688 | tf_op jit(solution)/shard_map/gather | solution.py:193
  165.4 2.1 copy.429
  169.4 2.0 copy.431
  174.1 29.1 %scatter_custom_fusion = f32[3,7800]{0,1:T(8,128)} fusion(s32[4096]{0:T(1024)S(1)} %get-tuple-element.200, f32[4096,3]{1,0:T(8,128)} %bitcast.1092, f32[]{:T(128)} %constant.123.clone.1), kind=kCustom, calls=%fused_computation.37 | custom fusion | flops 12288 | bytes 94112 | tf_op jit(solution)/shard_map/scatter-add | solution.py:200
  203.2 30.3 %scatter_fusion = f32[3,7800]{0,1:T(8,128)} fusion(f32[3,7800]{0,1:T(8,128)} %scatter_custom_fusion, s32[4096]{0:T(1024)S(1)} %get-tuple-element.35, f32[4096,3]{1,0:T(8,128)} %bitcast.1073), kind=kCustom, calls=%fused_computation.20 | custom fusion | flops 12288 | bytes 163840 | tf_op jit(solution)/shard_map/scatter-add | solution.py:200
  233.5 30.2 %scatter_fusion.1 = f32[3,7800]{0,1:T(8,128)} fusion(f32[3,7800]{0,1:T(8,128)} %scatter_fusion, s32[4096]{0:T(1024)S(1)} %get-tuple-element.189, f32[4096,3]{1,0:T(8,128)} %bitcast.1072), kind=kCustom, calls=%fused_computation.21 | custom fusion | flops 12288 | bytes 163840 | tf_op jit(solution)/shard_map/scatter-add | solution.py:200
  263.7 30.2 %scatter_fusion.2 = f32[3,7800]{0,1:T(8,128)} fusion(f32[3,7800]{0,1:T(8,128)} %scatter_fusion.1, s32[4096]{0:T(1024)S(1)} %get-tuple-element.187, f32[4096,3]{1,0:T(8,128)} %bitcast.1070), kind=kCustom, calls=%fused_computation.22 | custom fusion | flops 12288 | bytes 163840 | tf_op jit(solution)/shard_map/scatter-add | solution.py:200
  293.9 30.2 %scatter_fusion.3 = f32[3,7800]{0,1:T(8,128)} fusion(f32[3,7800]{0,1:T(8,128)} %scatter_fusion.2, s32[4096]{0:T(1024)S(1)} %get-tuple-element.41, f32[4096,3]{1,0:T(8,128)} %bitcast.1068), kind=kCustom, calls=%fused_computation.23 | custom fusion | flops 12288 | bytes 163840 | tf_op jit(solution)/shard_map/scatter-add | solution.py:200
  324.1 30.2 %scatter_fusion.4 = f32[3,7800]{0,1:T(8,128)} fusion(f32[3,7800]{0,1:T(8,128)} %scatter_fusion.3, s32[4096]{0:T(1024)S(1)} %get-tuple-element.181, f32[4096,3]{1,0:T(8,128)} %bitcast.1066), kind=kCustom, calls=%fused_computation.24 | custom fusion | flops 12288 | bytes 163840 | tf_op jit(solution)/shard_map/scatter-add | solution.py:200
  354.3 30.4 %scatter_fusion.5 = f32[3,7800]{0,1:T(8,128)} fusion(f32[3,7800]{0,1:T(8,128)} %scatter_fusion.4, s32[4096]{0:T(1024)S(1)} %get-tuple-element.183, f32[4096,3]{1,0:T(8,128)} %bitcast.1067), kind=kCustom, calls=%fused_computation.25 | custom fusion | flops 12288 | bytes 163840 | tf_op jit(solution)/shard_map/scatter-add | solution.py:200
  384.7 29.9 %scatter_fusion.6 = f32[3,7800]{0,1:T(8,128)} fusion(f32[3,7800]{0,1:T(8,128)} %scatter_fusion.5, s32[4096]{0:T(1024)S(1)} %get-tuple-element.185, f32[4096,3]{1,0:T(8,128)S(1)} %bitcast.1064), kind=kCustom, calls=%fused_computation.26 | custom fusion | flops 12288 | bytes 163840 | tf_op jit(solution)/shard_map/scatter-add | solution.py:200
  414.6 2.9 copy.392
  417.9 7.0 collective-permute-start.7
  424.9 2.1 collective-permute-done.6
  433.3 3.8 collective-permute-done.10
  439.9 2.7 collective-permute-start.13
  442.6 2.2 collective-permute-done.12
  445.3 2.6 collective-permute-start.14
  453.8 4.7 collective-permute-done.16
  459.8 3.0 collective-permute-start.19
  470.6 3.9 collective-permute-done.22
  474.9 2.8 copy.393
  477.7 12.9 %gather_fusion.11 = f32[4096,3]{1,0:T(8,128)S(1)} fusion(f32[3,7800]{0,1:T(8,128)} %copy.393, s32[4096]{0:T(1024)S(1)} %get-tuple-element.199), kind=kCustom, calls=%fused_computation.11 | custom fusion | bytes 114688 | tf_op jit(solution)/shard_map/gather | solution.py:193
  490.7 16.3 %gather_fusion.12 = f32[4096,3]{1,0:T(8,128)} fusion(f32[3,7800]{0,1:T(8,128)} %copy.393, s32[4096]{0:T(1024)S(1)} %get-tuple-element.34), kind=kCustom, calls=%fused_computation.12 | custom fusion | bytes 114688 | tf_op jit(solution)/shard_map/gather | solution.py:193
  507.0 16.3 %gather_fusion.13 = f32[4096,3]{1,0:T(8,128)} fusion(f32[3,7800]{0,1:T(8,128)} %copy.393, s32[4096]{0:T(1024)S(1)} %get-tuple-element.188), kind=kCustom, calls=%fused_computation.13 | custom fusion | bytes 114688 | tf_op jit(solution)/shard_map/gather | solution.py:193
  523.3 16.3 %gather_fusion.14 = f32[4096,3]{1,0:T(8,128)} fusion(f32[3,7800]{0,1:T(8,128)} %copy.393, s32[4096]{0:T(1024)S(1)} %get-tuple-element.186), kind=kCustom, calls=%fused_computation.14 | custom fusion | bytes 114688 | tf_op jit(solution)/shard_map/gather | solution.py:193
  539.6 16.3 %gather_fusion.16 = f32[4096,3]{1,0:T(8,128)} fusion(f32[3,7800]{0,1:T(8,128)} %copy.393, s32[4096]{0:T(1024)S(1)} %get-tuple-element.180), kind=kCustom, calls=%fused_computation.16 | custom fusion | bytes 114688 | tf_op jit(solution)/shard_map/gather | solution.py:193
  555.9 16.3 %gather_fusion.17 = f32[4096,3]{1,0:T(8,128)} fusion(f32[3,7800]{0,1:T(8,128)} %copy.393, s32[4096]{0:T(1024)S(1)} %get-tuple-element.182), kind=kCustom, calls=%fused_computation.17 | custom fusion | bytes 114688 | tf_op jit(solution)/shard_map/gather | solution.py:193
  572.2 16.4 %gather_fusion.15 = f32[4096,3]{1,0:T(8,128)} fusion(f32[3,7800]{0,1:T(8,128)} %copy.393, s32[4096]{0:T(1024)S(1)} %get-tuple-element.40), kind=kCustom, calls=%fused_computation.15 | custom fusion | bytes 114688 | tf_op jit(solution)/shard_map/gather | solution.py:193
  588.6 16.3 %gather_fusion.18 = f32[4096,3]{1,0:T(8,128)} fusion(f32[3,7800]{0,1:T(8,128)} %copy.393, s32[4096]{0:T(1024)S(1)} %get-tuple-element.184), kind=kCustom, calls=%fused_computation.18 | custom fusion | bytes 114688 | tf_op jit(solution)/shard_map/gather | solution.py:193
  605.6 2.4 copy.435
  608.6 2.4 copy.437
  611.6 2.4 copy.440
  614.8 2.3 copy.441
  618.6 29.3 %scatter_custom_fusion.8 = f32[3,7800]{0,1:T(8,128)} fusion(s32[4096]{0:T(1024)} %copy-done.51, f32[4096,3]{1,0:T(8,128)S(1)} %bitcast.1093, f32[]{:T(128)} %constant.123.clone.1), kind=kCustom, calls=%fused_computation.35 | custom fusion | flops 12288 | bytes 94112 | tf_op jit(solution)/shard_map/scatter-add | solution.py:200
  651.8 2.1 copy.445
  660.6 30.2 %scatter_fusion.7 = f32[3,7800]{0,1:T(8,128)} fusion(f32[3,7800]{0,1:T(8,128)} %scatter_custom_fusion.8, s32[4096]{0:T(1024)S(1)} %copy-done.16, f32[4096,3]{1,0:T(8,128)} %bitcast.1075), kind=kCustom, calls=%fused_computation.28 | custom fusion | flops 12288 | bytes 163840 | tf_op jit(solution)/shard_map/scatter-add | solution.py:200
  690.8 30.2 %scatter_fusion.8 = f32[3,7800]{0,1:T(8,128)} fusion(f32[3,7800]{0,1:T(8,128)} %scatter_fusion.7, s32[4096]{0:T(1024)S(1)} %copy-done.14, f32[4096,3]{1,0:T(8,128)} %bitcast.1074), kind=kCustom, calls=%fused_computation.29 | custom fusion | flops 12288 | bytes 163840 | tf_op jit(solution)/shard_map/scatter-add | solution.py:200
  721.0 30.2 %scatter_fusion.9 = f32[3,7800]{0,1:T(8,128)} fusion(f32[3,7800]{0,1:T(8,128)} %scatter_fusion.8, s32[4096]{0:T(1024)S(1)} %copy-done.12, f32[4096,3]{1,0:T(8,128)} %bitcast.1071), kind=kCustom, calls=%fused_computation.30 | custom fusion | flops 12288 | bytes 163840 | tf_op jit(solution)/shard_map/scatter-add | solution.py:200
  751.2 30.3 %scatter_fusion.10 = f32[3,7800]{0,1:T(8,128)} fusion(f32[3,7800]{0,1:T(8,128)} %scatter_fusion.9, s32[4096]{0:T(1024)S(1)} %get-tuple-element.41, f32[4096,3]{1,0:T(8,128)} %bitcast.1069), kind=kCustom, calls=%fused_computation.31 | custom fusion | flops 12288 | bytes 163840 | tf_op jit(solution)/shard_map/scatter-add | solution.py:200
  781.6 30.2 %scatter_fusion.11 = f32[3,7800]{0,1:T(8,128)} fusion(f32[3,7800]{0,1:T(8,128)} %scatter_fusion.10, s32[4096]{0:T(1024)S(1)} %copy-done.10, f32[4096,3]{1,0:T(8,128)} %bitcast.1065), kind=kCustom, calls=%fused_computation.32 | custom fusion | flops 12288 | bytes 163840 | tf_op jit(solution)/shard_map/scatter-add | solution.py:200
  811.8 30.2 %scatter_fusion.12 = f32[3,7800]{0,1:T(8,128)} fusion(f32[3,7800]{0,1:T(8,128)} %scatter_fusion.11, s32[4096]{0:T(1024)S(1)} %copy-done.8, f32[4096,3]{1,0:T(8,128)} %bitcast.1063), kind=kCustom, calls=%fused_computation.33 | custom fusion | flops 12288 | bytes 163840 | tf_op jit(solution)/shard_map/scatter-add | solution.py:200
  842.0 29.9 %scatter_fusion.13 = f32[3,7800]{0,1:T(8,128)} fusion(f32[3,7800]{0,1:T(8,128)} %scatter_fusion.12, s32[4096]{0:T(1024)S(1)} %get-tuple-element.185, f32[4096,3]{1,0:T(8,128)S(1)} %bitcast.1062), kind=kCustom, calls=%fused_computation.34 | custom fusion | flops 12288 | bytes 163840 | tf_op jit(solution)/shard_map/scatter-add | solution.py:200
  871.9 2.9 copy.417
  875.2 10.3 %collective-permute-start.25 = (f32[3,1,10,130]{3,2,1,0:T(8,128)S(1)}, f32[3,1,10,130]{3,2,1,0:T(8,128)S(1)}, u32[]{:S(2)}, u32[]{:S(2)}) collective-permute-start(f32[3,1,10,130]{3,2,1,0:T(8,128)S(1)} %get-tuple-element.101), channel_id=1, source_target_pairs={{8,0},{16,8},{24,16},{0,24},{9,1},{17,9},{25,17},{1,25},{10,2},{18... | collective-permute-start | bytes 46808 | tf_op jit(solution)/shard_map/ppermute | solution.py:45
  885.5 2.1 collective-permute-done.24
  894.1 5.2 collective-permute-done.28
  901.7 2.9 collective-permute-start.31
  913.5 4.4 collective-permute-done.34
  (352 shorter events, 93.9 us)
Async XLA Ops:
  0.6 19.6 %copy-start = (s32[16,128]{1,0:T(8,128)S(1)}, s32[16,128]{1,0:T(8,128)}, u32[]{:S(2)}) copy-start(s32[16,128]{1,0:T(8,128)} %param.13) | copy-start | bytes 24580
  3.3 17.5 %collective-permute-start = (f32[3,1,8,128]{3,2,1,0:T(8,128)S(1)}, f32[3,1,8,128]{3,2,1,0:T(8,128)S(1)}, u32[]{:S(2)}, u32[]{:S(2)}) collective-permute-start(f32[3,1,8,128]{3,2,1,0:T(8,128)S(1)} %get-tuple-element.166), channel_id=1, source_target_pairs={{0,8},{8,16},{16,24},{24,0},{1,9},{9,17},{17,25},{25,1},{2,10},{10... | collective-permute-start | bytes 36872 | tf_op jit(solution)/shard_map/ppermute | solution.py:43
  6.4 14.4 %collective-permute-start.1 = (f32[3,1,8,128]{3,2,1,0:T(8,128)S(1)}, f32[3,1,8,128]{3,2,1,0:T(8,128)S(1)}, u32[]{:S(2)}, u32[]{:S(2)}) collective-permute-start(f32[3,1,8,128]{3,2,1,0:T(8,128)S(1)} %get-tuple-element.167), channel_id=1, source_target_pairs={{8,0},{16,8},{24,16},{0,24},{9,1},{17,9},{25,17},{1,25},{10,2},{18... | collective-permute-start | bytes 36872 | tf_op jit(solution)/shard_map/ppermute | solution.py:45
  13.1 10.5 %all-to-all-start.2 = ((s32[4,8,1]{1,2,0:T(1,128)}), s32[4,8,1]{1,2,0:T(1,128)S(1)}, u32[]{:S(2)}, u32[]{:S(2)}) async-start(s32[4,8,1]{1,2,0:T(1,128)} %bitcast.28), calls=%async_computation.2 | async-start | bytes 4096 | tf_op jit(solution)/shard_map/all_to_all | solution.py:175
  20.8 9.1 collective-permute-start.2
  22.5 7.4 collective-permute-start.3
  23.6 15.2 %all-to-all-start.1 = ((f32[32,7,128]{2,1,0:T(8,128)}), f32[32,7,128]{2,1,0:T(8,128)S(1)}, u32[]{:S(2)}, u32[]{:S(2)}) async-start(f32[32,7,128]{2,1,0:T(8,128)} %select_select_fusion), calls=%async_computation.1 | async-start | bytes 262144 | tf_op jit(solution)/shard_map/all_to_all | solution.py:173
  30.1 4.6 collective-permute-start.4
  30.1 5.3 collective-permute-start.5
  38.8 11.2 %all-to-all-start = ((s32[4,8,128]{2,1,0:T(8,128)}), s32[4,8,128]{2,1,0:T(8,128)S(1)}, u32[]{:S(2)}, u32[]{:S(2)}) async-start(s32[4,8,128]{2,1,0:T(8,128)} %fusion.395), calls=%async_computation | async-start | bytes 32768 | tf_op jit(solution)/shard_map/all_to_all | solution.py:174
  44.5 114.4 %copy-start.41 = (f32[32,1,128]{2,1,0:T(1,128)}, f32[32,1,128]{2,1,0:T(1,128)S(1)}, u32[]{:S(2)}) copy-start(f32[32,1,128]{2,1,0:T(1,128)S(1)} %get-tuple-element.125) | copy-start | bytes 49156
  50.2 123.9 %copy-start.51 = (s32[4096]{0:T(1024)}, s32[4096]{0:T(1024)S(1)}, u32[]{:S(2)}) copy-start(s32[4096]{0:T(1024)S(1)} %get-tuple-element.200) | copy-start | bytes 49156
  50.2 152.9 %copy-start.15 = (s32[4096]{0:T(1024)}, s32[4096]{0:T(1024)S(1)}, u32[]{:S(2)}) copy-start(s32[4096]{0:T(1024)S(1)} %get-tuple-element.35) | copy-start | bytes 49156
  50.2 183.3 %copy-start.13 = (s32[4096]{0:T(1024)}, s32[4096]{0:T(1024)S(1)}, u32[]{:S(2)}) copy-start(s32[4096]{0:T(1024)S(1)} %get-tuple-element.189) | copy-start | bytes 49156
  50.2 213.5 %copy-start.11 = (s32[4096]{0:T(1024)}, s32[4096]{0:T(1024)S(1)}, u32[]{:S(2)}) copy-start(s32[4096]{0:T(1024)S(1)} %get-tuple-element.187) | copy-start | bytes 49156
  50.2 273.9 %copy-start.9 = (s32[4096]{0:T(1024)}, s32[4096]{0:T(1024)S(1)}, u32[]{:S(2)}) copy-start(s32[4096]{0:T(1024)S(1)} %get-tuple-element.181) | copy-start | bytes 49156
  50.3 304.1 %copy-start.7 = (s32[4096]{0:T(1024)}, s32[4096]{0:T(1024)S(1)}, u32[]{:S(2)}) copy-start(s32[4096]{0:T(1024)S(1)} %get-tuple-element.183) | copy-start | bytes 49156
  158.6 4.7 copy-start.43
  158.6 4.7 copy-start.45
  158.6 4.7 copy-start.47
  158.6 4.7 copy-start.49
  158.7 4.6 copy-start.17
  158.7 4.6 copy-start.19
  158.7 4.6 copy-start.21
  417.6 20.3 %copy-start.54 = (pred[4]{0:T(512)(128)(4,1)S(1)}, pred[4]{0:T(512)(128)(4,1)}, u32[]{:S(2)}) copy-start(pred[4]{0:T(512)(128)(4,1)} %constant.140.clone.1) | copy-start | bytes 16
  417.9 9.1 collective-permute-start.6
  417.9 9.1 collective-permute-start.7
  427.1 3.9 collective-permute-start.8
  427.2 10.8 %copy-start.53 = (pred[8]{0:T(512)(128)(4,1)S(1)}, pred[8]{0:T(512)(128)(4,1)}, u32[]{:S(2)}) copy-start(pred[8]{0:T(512)(128)(4,1)} %constant.141.clone.1) | copy-start | bytes 28
  427.2 4.1 collective-permute-start.9
  431.4 6.8 copy-start.52
  431.4 6.9 copy-start.2
  431.4 6.9 copy-start.3
  431.5 5.6 collective-permute-start.10
  431.6 6.0 collective-permute-start.11
  438.7 6.1 collective-permute-start.12
  439.9 5.2 collective-permute-start.13
  445.3 4.5 collective-permute-start.14
  447.9 3.8 collective-permute-start.15
  452.0 6.5 collective-permute-start.16
  452.0 6.4 collective-permute-start.17
  459.0 5.5 collective-permute-start.18
  459.8 4.7 collective-permute-start.19
  464.6 3.7 collective-permute-start.20
  464.6 3.7 collective-permute-start.21
  468.5 5.9 collective-permute-start.22
  468.6 5.8 collective-permute-start.23
  659.9 30.9 %copy-start.14 = (s32[4096]{0:T(1024)S(1)}, s32[4096]{0:T(1024)}, u32[]{:S(2)}) copy-start(s32[4096]{0:T(1024)} %copy-done.13) | copy-start | bytes 49156
  659.9 61.1 %copy-start.12 = (s32[4096]{0:T(1024)S(1)}, s32[4096]{0:T(1024)}, u32[]{:S(2)}) copy-start(s32[4096]{0:T(1024)} %copy-done.11) | copy-start | bytes 49156
  660.6 121.0 %copy-start.10 = (s32[4096]{0:T(1024)S(1)}, s32[4096]{0:T(1024)}, u32[]{:S(2)}) copy-start(s32[4096]{0:T(1024)} %copy-done.9) | copy-start | bytes 49156
  690.8 121.0 %copy-start.8 = (s32[4096]{0:T(1024)S(1)}, s32[4096]{0:T(1024)}, u32[]{:S(2)}) copy-start(s32[4096]{0:T(1024)} %copy-done.7) | copy-start | bytes 49156
  875.1 12.4 %collective-permute-start.24 = (f32[3,1,10,130]{3,2,1,0:T(8,128)S(1)}, f32[3,1,10,130]{3,2,1,0:T(8,128)S(1)}, u32[]{:S(2)}, u32[]{:S(2)}) collective-permute-start(f32[3,1,10,130]{3,2,1,0:T(8,128)S(1)} %get-tuple-element.102), channel_id=1, source_target_pairs={{0,8},{8,16},{16,24},{24,0},{1,9},{9,17},{17,25},{25,1},{2,10},{10... | collective-permute-start | bytes 46808 | tf_op jit(solution)/shard_map/ppermute | solution.py:43
  875.2 12.4 %collective-permute-start.25 = (f32[3,1,10,130]{3,2,1,0:T(8,128)S(1)}, f32[3,1,10,130]{3,2,1,0:T(8,128)S(1)}, u32[]{:S(2)}, u32[]{:S(2)}) collective-permute-start(f32[3,1,10,130]{3,2,1,0:T(8,128)S(1)} %get-tuple-element.101), channel_id=1, source_target_pairs={{8,0},{16,8},{24,16},{0,24},{9,1},{17,9},{25,17},{1,25},{10,2},{18... | collective-permute-start | bytes 46808 | tf_op jit(solution)/shard_map/ppermute | solution.py:45
  887.6 4.0 collective-permute-start.26
  887.7 4.3 collective-permute-start.27
  892.3 7.0 collective-permute-start.28
  892.3 6.9 collective-permute-start.29
  900.6 5.9 collective-permute-start.30
  901.7 4.9 collective-permute-start.31
  906.9 3.8 collective-permute-start.32
  907.6 3.8 collective-permute-start.33
  909.0 10.0 %copy-start.1 = (s32[16,128]{1,0:T(8,128)S(1)}, s32[16,128]{1,0:T(8,128)}, u32[]{:S(2)}) copy-start(s32[16,128]{1,0:T(8,128)} %param.13) | copy-start | bytes 24580
  911.7 6.2 collective-permute-start.34
  911.8 6.2 collective-permute-start.35
  (30 other events, 94.9 us)
where the time goes:
time: 922 us; the launch traced here: 919 us
  other arithmetic  496 us (54%)
  local copies, waits for them, and re-layouts  295 us (32%)
  starting transfers between devices  72.3 us (8%)
  waiting for transfers between devices  54 us (6%)
    scatter-add x16, other arithmetic, per_device(): ghosts.at[:, flat_index]  481 us
    gather x32, local copies, waits for them, and re-layouts, per_device(): flattened[:, flat_index]  247 us
    ppermute x18, starting transfers between devices, with_halo(): lax.ppermute(head, axis, [((i + 1) % count, i) for i in range(count)])  46.5 us
    ppermute x18, waiting for transfers between devices, with_halo(): lax.ppermute(tail, axis, [(i, (i + 1) % count) for i in range(count)])  43.5 us
    transpose x16, local copies, waits for them, and re-layouts, per_device(): jnp.moveaxis(-weight[:, None, :] * drag_force, 1, 0)  27.9 us
  transfers between devices with their start and end apart: 39, of which 25 were waited for; matrix products, arithmetic and copies ran while one was open for 2% of the time, Pallas kernels for 0%

commit v1 on v0

--- a/solution.py
+++ b/solution.py
@@ -88,23 +88,6 @@
             relaxed = relaxed + 3.0 * weights[i] * along_force
         post_list.append((1.0 - gray_fraction) * relaxed + gray_fraction * fields[opposite[i]])
     return post_list
-
-
-def corner_table(places, offset, extents):
-    options = []
-    for d in range(3):
-        displace = offset[:, d, :]
-        step_sign = jnp.where(displace >= 0.0, 1, -1).astype(jnp.int32)
-        options.append(
-            ((places[d], 1.0 - jnp.abs(displace)), (places[d] + step_sign, jnp.abs(displace)))
-        )
-    corners = []
-    for a in options[0]:
-        for b in options[1]:
-            for c in options[2]:
-                flat_index = ((a[0] * extents[1] + b[0]) * extents[2] + c[0]).astype(jnp.int32)
-                corners.append((flat_index, a[1] * b[1] * c[1]))
-    return corners
 
 
 def fold_ghost(widened, dim):
@@ -181,25 +164,36 @@
     p = got_cells // (size_y * size_z) + 1
     q = got_cells // size_z % size_y + 1
     s = got_cells % size_z + 1
-    corners = corner_table((p, q, s), offset, (size_x + 2, size_y + 2, size_z + 2))
+    slots = offset.shape[0]
+    tables = []
+    for d, (place, extent) in enumerate(((p, size_x + 2), (q, size_y + 2), (s, size_z + 2))):
+        displace = offset[:, d, :].reshape(-1)
+        nearer = place.reshape(-1)
+        farther = nearer + jnp.where(displace >= 0.0, 1, -1).astype(jnp.int32)
+        grid = jnp.arange(extent, dtype=jnp.int32)[None, :]
+        tables.append(
+            jnp.where(grid == nearer[:, None], (1.0 - jnp.abs(displace))[:, None], 0.0)
+            + jnp.where(grid == farther[:, None], jnp.abs(displace)[:, None], 0.0)
+        )
+    across = (tables[0][:, :, None] * tables[1][:, None, :]).reshape(slots * rows_block, -1)
     gray_fraction = solid_class.astype(jnp.float32) * 0.25
     fields = populations
     for repeat in range(STEPS):
         density, flow = moments(fields)
         rim_field = with_halo(flow, (("gx", 1), ("gy", 2), ("gz", 3)), 1)
-        flattened = rim_field.reshape(3, -1)
-        sampled = jnp.zeros_like(velocity)
-        for flat_index, weight in corners:
-            sampled = sampled + weight[:, None, :] * jnp.moveaxis(flattened[:, flat_index], 0, 1)
+        lines = rim_field.reshape(3, -1, size_z + 2)
+        along = jnp.einsum("nz,dkz->dnk", tables[2], lines, precision=lax.Precision.HIGHEST)
+        sampled = jnp.sum(along * across[None], axis=2).reshape(3, slots, rows_block)
+        sampled = jnp.moveaxis(sampled, 0, 1)
         drag_force = jnp.where(
             live_rows[:, None, :], drag_rate[:, None, :] * (sampled - velocity), 0.0
         )
         velocity = velocity + drag_force
-        ghosts = jnp.zeros_like(flattened)
-        for flat_index, weight in corners:
-            ghosts = ghosts.at[:, flat_index].add(
-                jnp.moveaxis(-weight[:, None, :] * drag_force, 1, 0)
-            )
+        pushed = -jnp.moveaxis(drag_force, 1, 0).reshape(3, -1)
+        ghosts = jnp.einsum(
+            "dnk,nz->dkz", pushed[:, :, None] * across[None], tables[2],
+            precision=lax.Precision.HIGHEST,
+        )
         ghosts = ghosts.reshape(3, size_x + 2, size_y + 2, size_z + 2)
         widened = with_halo(ghosts, (("gx", 1), ("gy", 2), ("gz", 3)), 1)
         cell_force = fold_ghost(fold_ghost(fold_ghost(widened, 1), 2), 3)

time: 922 us -> 154 us (0.17)
  other arithmetic: 496 us -> 14.3 us
  local copies, waits for them, and re-layouts: 295 us -> 7.11 us
  matrix products: 0 us -> 12.9 us
  starting transfers between devices: 72.3 us -> 61.5 us
    scatter-add x16 -> x0, other arithmetic: 481 us -> none  [per_device(): ghosts.at[:, flat_index]]
    gather x32 -> x0, local copies, waits for them, and re-layouts: 247 us -> none  [per_device(): flattened[:, flat_index]]
    transpose x16 -> x0, local copies, waits for them, and re-layouts: 27.9 us -> none  [per_device(): jnp.moveaxis(-weight[:, None, :] * drag_force, 1, 0)]
    ppermute x18, starting transfers between devices: 46.5 us -> 32.6 us  [with_halo(): lax.ppermute(head, axis, [((i + 1) % count, i) for i in range(count)])]
    dot_general x0 -> x4, matrix products: none -> 12.9 us  [the longest x2 6.6 us: per_device(): jnp.einsum('nz,dkz->dnk', tables[2], lines, precision=lax.Precision.HIGHEST)]
  transfers between devices with their start and end apart: 39 -> 39, of which waited for: 25 -> 30; matrix products, arithmetic and copies ran while one was open for 2% -> 8% of each run, Pallas kernels for 0% -> 0%
where the time goes in v1:
time: 154 us; the launch traced here: 153 us
  starting transfers between devices  61.5 us (40%)
  waiting for transfers between devices  55.2 us (36%)
  other arithmetic  14.3 us (9%)
  matrix products  12.9 us (8%)
  local copies, waits for them, and re-layouts  7.11 us (5%)
    ppermute x18, waiting for transfers between devices, with_halo(): lax.ppermute(tail, axis, [(i, (i + 1) % count) for i in range(count)])  36.8 us
    ppermute x18, starting transfers between devices, with_halo(): lax.ppermute(head, axis, [((i + 1) % count, i) for i in range(count)])  32.6 us
    ppermute x18, starting transfers between devices, with_halo(): lax.ppermute(tail, axis, [(i, (i + 1) % count) for i in range(count)])  15.5 us
    ppermute x18, waiting for transfers between devices, with_halo(): lax.ppermute(head, axis, [((i + 1) % count, i) for i in range(count)])  13 us
    dot_general x2, matrix products, per_device(): jnp.einsum('nz,dkz->dnk', tables[2], lines, precision=lax.Precision.HIGHEST)  6.6 us
    dot_general x2, matrix products, per_device(): jnp.einsum('dnk,nz->dkz', pushed[:, :, None] * across[None], tables[2], p...  6.32 us
    all_to_all x1, waiting for transfers between devices, per_device(): lax.all_to_all(send_cells, 'gx', split_axis=0, concat_axis=0, tiled=True)  5.46 us
    all_to_all x1, starting transfers between devices, per_device(): lax.all_to_all(send_cells, 'gx', split_axis=0, concat_axis=0, tiled=True)  5.1 us
  transfers between devices with their start and end apart: 39, of which 30 were waited for; matrix products, arithmetic and copies ran while one was open for 8% of the time, Pallas kernels for 0%

profile of v1, /device:TPU:0, one launch (start us, length us, event | category | flops | bytes accessed | tf_op | source)
XLA Modules:
  0.0 152.6 jit_solution(2688732863487197117)
XLA Ops:
  0.6 0.9 add_add_fusion.1
  1.5 0.9 negate_add_fusion.2
  2.4 0.9 negate_add_fusion.3
  3.3 3.1 %collective-permute-start = (f32[3,1,8,128]{3,2,1,0:T(8,128)S(1)}, f32[3,1,8,128]{3,2,1,0:T(8,128)S(1)}, u32[]{:S(2)}, u32[]{:S(2)}) collective-permute-start(f32[3,1,8,128]{3,2,1,0:T(8,128)S(1)} %get-tuple-element.115), channel_id=1, source_target_pairs={{0,8},{8,16},{16,24},{24,0},{1,9},{9,17},{17,25},{25,1},{2,10},{10... | collective-permute-start | bytes 36872 | tf_op jit(solution)/shard_map/ppermute | solution.py:43
  6.4 2.1 %collective-permute-start.1 = (f32[3,1,8,128]{3,2,1,0:T(8,128)S(1)}, f32[3,1,8,128]{3,2,1,0:T(8,128)S(1)}, u32[]{:S(2)}, u32[]{:S(2)}) collective-permute-start(f32[3,1,8,128]{3,2,1,0:T(8,128)S(1)} %get-tuple-element.116), channel_id=1, source_target_pairs={{8,0},{16,8},{24,16},{0,24},{9,1},{17,9},{25,17},{1,25},{10,2},{18... | collective-permute-start | bytes 36872 | tf_op jit(solution)/shard_map/ppermute | solution.py:45
  9.2 0.8 select_reduce_fusion.1
  11.0 1.4 gather_fusion
  13.1 3.2 %all-to-all-start = ((s32[4,8,1]{1,2,0:T(1,128)}), s32[4,8,1]{1,2,0:T(1,128)S(1)}, u32[]{:S(2)}, u32[]{:S(2)}) async-start(s32[4,8,1]{1,2,0:T(1,128)} %bitcast.22), calls=%async_computation | async-start | bytes 4096 | tf_op jit(solution)/shard_map/all_to_all | solution.py:158
  17.2 0.8 copy.19
  19.3 0.8 select_select_fusion
  20.8 1.7 %collective-permute-start.2 = (f32[3,6,1,128]{3,2,1,0:T(1,128)S(1)}, f32[3,6,1,128]{3,2,1,0:T(1,128)S(1)}, u32[]{:S(2)}, u32[]{:S(2)}) collective-permute-start(f32[3,6,1,128]{3,2,1,0:T(1,128)S(1)} %get-tuple-element.111), channel_id=1, source_target_pairs={{0,4},{4,0},{1,5},{5,1},{2,6},{6,2},{3,7},{7,3},{8,12},{12,8},{9,1... | collective-permute-start | bytes 27656 | tf_op jit(solution)/shard_map/ppermute | solution.py:43
  23.6 5.1 %all-to-all-start.1 = ((f32[32,7,128]{2,1,0:T(8,128)}), f32[32,7,128]{2,1,0:T(8,128)S(1)}, u32[]{:S(2)}, u32[]{:S(2)}) async-start(f32[32,7,128]{2,1,0:T(8,128)} %select_select_fusion), calls=%async_computation.1 | async-start | bytes 262144 | tf_op jit(solution)/shard_map/all_to_all | solution.py:156
  30.1 1.7 %collective-permute-start.5 = (f32[3,6,10,1]{3,2,1,0:T(8,128)S(1)}, f32[3,6,10,1]{3,2,1,0:T(8,128)S(1)}, u32[]{:S(2)}, u32[]{:S(2)}) collective-permute-start(f32[3,6,10,1]{3,2,1,0:T(8,128)S(1)} %get-tuple-element.97), channel_id=1, source_target_pairs={{1,0},{2,1},{3,2},{0,3},{5,4},{6,5},{7,6},{4,7},{9,8},{10,9},{11,1... | collective-permute-start | bytes 2168 | tf_op jit(solution)/shard_map/ppermute | solution.py:45
  31.9 2.7 %collective-permute-done.4 = f32[3,6,10,1]{3,2,1,0:T(8,128)S(1)} collective-permute-done((f32[3,6,10,1]{3,2,1,0:T(8,128)S(1)}, f32[3,6,10,1]{3,2,1,0:T(8,128)S(1)}, u32[]{:S(2)}, u32[]{:S(2)}) %collective-permute-start.4) | collective-permute-done | bytes 752 | tf_op jit(solution)/shard_map/ppermute | solution.py:43
  35.7 5.1 %all-to-all-start.2 = ((s32[4,8,128]{2,1,0:T(8,128)}), s32[4,8,128]{2,1,0:T(8,128)S(1)}, u32[]{:S(2)}, u32[]{:S(2)}) async-start(s32[4,8,128]{2,1,0:T(8,128)} %fusion.422), calls=%async_computation.2 | async-start | bytes 32768 | tf_op jit(solution)/shard_map/all_to_all | solution.py:157
  41.0 5.5 %all-to-all-done.2 = s32[4,8,128]{2,1,0:T(8,128)S(1)} async-done(((s32[4,8,128]{2,1,0:T(8,128)}), s32[4,8,128]{2,1,0:T(8,128)S(1)}, u32[]{:S(2)}, u32[]{:S(2)}) %all-to-all-start.2) | async-done | bytes 16416 | tf_op jit(solution)/shard_map/all_to_all | solution.py:157
  46.9 3.3 %fusion.14 = f32[3,4096]{1,0:T(4,128)S(1)} fusion(f32[4096,60]{0,1:T(8,128)S(1)} %mul.1044, f32[3,60,130]{2,1,0:T(8,128)S(1)} %reshape.518, f32[4096]{0:T(1024)S(1)} %bitcast.915, s32[4096]{0:T(1024)S(1)} %get-tuple-element.118, f32[4096]{0:T(1024)S(1)} %broadcast_subtract_fusion.2, s32[4096]{0:T(1024)S(1)} %get-tuple-element.117), kind=kOutput, calls=%fused_computation.22 | convolution fusion | flops 1154281472 | bytes 1191328 | tf_op jit(solution)/shard_map/nz,dkz->dnk/dot_general | solution.py:185
  50.3 3.2 %fusion.4 = f32[3,60,130]{2,1,0:T(8,128)S(1)} fusion(f32[3,4096]{1,0:T(4,128)S(1)} %negate_bitcast_fusion.1, f32[4096,60]{0,1:T(8,128)S(1)} %mul.1044, f32[4096]{0:T(1024)S(1)} %bitcast.916, s32[4096]{0:T(1024)S(1)} %get-tuple-element.118, f32[4096]{0:T(1024)S(1)} %broadcast_subtract_fusion.2, s32[4096]{0:T(1024)S(1)} %get-tuple-element.117), kind=kOutput, calls=%fused_computation.9 | convolution fusion | flops 1153556480 | bytes 1191328 | tf_op jit(solution)/shard_map/dnk,nz->dkz/dot_general | solution.py:193
  54.2 3.2 %collective-permute-start.7 = (f32[3,1,10,130]{3,2,1,0:T(8,128)S(1)}, f32[3,1,10,130]{3,2,1,0:T(8,128)S(1)}, u32[]{:S(2)}, u32[]{:S(2)}) collective-permute-start(f32[3,1,10,130]{3,2,1,0:T(8,128)S(1)} %get-tuple-element.74), channel_id=1, source_target_pairs={{8,0},{16,8},{24,16},{0,24},{9,1},{17,9},{25,17},{1,25},{10,2},{18... | collective-permute-start | bytes 46808 | tf_op jit(solution)/shard_map/ppermute | solution.py:45
  57.3 2.1 %collective-permute-done.6 = f32[3,1,10,130]{3,2,1,0:T(8,128)S(1)} collective-permute-done((f32[3,1,10,130]{3,2,1,0:T(8,128)S(1)}, f32[3,1,10,130]{3,2,1,0:T(8,128)S(1)}, u32[]{:S(2)}, u32[]{:S(2)}) %collective-permute-start.6) | collective-permute-done | bytes 15632 | tf_op jit(solution)/shard_map/ppermute | solution.py:43
  59.5 1.6 %collective-permute-start.8 = (f32[3,8,1,130]{3,2,1,0:T(1,128)S(1)}, f32[3,8,1,130]{3,2,1,0:T(1,128)S(1)}, u32[]{:S(2)}, u32[]{:S(2)}) collective-permute-start(f32[3,8,1,130]{3,2,1,0:T(1,128)S(1)} %get-tuple-element.30), channel_id=1, source_target_pairs={{0,4},{4,0},{1,5},{5,1},{2,6},{6,2},{3,7},{7,3},{8,12},{12,8},{9,1... | collective-permute-start | bytes 37448 | tf_op jit(solution)/shard_map/ppermute | solution.py:43
  61.6 1.8 %collective-permute-done.8 = f32[3,8,1,130]{3,2,1,0:T(1,128)S(1)} collective-permute-done((f32[3,8,1,130]{3,2,1,0:T(1,128)S(1)}, f32[3,8,1,130]{3,2,1,0:T(1,128)S(1)}, u32[]{:S(2)}, u32[]{:S(2)}) %collective-permute-start.8) | collective-permute-done | bytes 12512 | tf_op jit(solution)/shard_map/ppermute | solution.py:43
  63.4 1.5 collective-permute-done.9
  65.2 1.7 %collective-permute-start.11 = (f32[3,8,12,1]{3,2,1,0:T(8,128)S(1)}, f32[3,8,12,1]{3,2,1,0:T(8,128)S(1)}, u32[]{:S(2)}, u32[]{:S(2)}) collective-permute-start(f32[3,8,12,1]{3,2,1,0:T(8,128)S(1)} %get-tuple-element.29), channel_id=1, source_target_pairs={{1,0},{2,1},{3,2},{0,3},{5,4},{6,5},{7,6},{4,7},{9,8},{10,9},{11,1... | collective-permute-start | bytes 3464 | tf_op jit(solution)/shard_map/ppermute | solution.py:45
  67.0 3.4 %collective-permute-done.10 = f32[3,8,12,1]{3,2,1,0:T(8,128)S(1)} collective-permute-done((f32[3,8,12,1]{3,2,1,0:T(8,128)S(1)}, f32[3,8,12,1]{3,2,1,0:T(8,128)S(1)}, u32[]{:S(2)}, u32[]{:S(2)}) %collective-permute-start.10) | collective-permute-done | bytes 1184 | tf_op jit(solution)/shard_map/ppermute | solution.py:43
  70.3 1.3 collective-permute-done.11
  72.8 3.8 %collective-permute-start.13 = (f32[10,1,8,128]{3,2,1,0:T(8,128)S(1)}, f32[10,1,8,128]{3,2,1,0:T(8,128)S(1)}, u32[]{:S(2)}, u32[]{:S(2)}) collective-permute-start(f32[10,1,8,128]{3,2,1,0:T(8,128)S(1)} %get-tuple-element.92), channel_id=1, source_target_pairs={{8,0},{16,8},{24,16},{0,24},{9,1},{17,9},{25,17},{1,25},{10,2},{18... | collective-permute-start | bytes 122888 | tf_op jit(solution)/shard_map/ppermute | solution.py:45
  76.6 2.3 %collective-permute-done.12 = f32[10,1,8,128]{3,2,1,0:T(8,128)S(1)} collective-permute-done((f32[10,1,8,128]{3,2,1,0:T(8,128)S(1)}, f32[10,1,8,128]{3,2,1,0:T(8,128)S(1)}, u32[]{:S(2)}, u32[]{:S(2)}) %collective-permute-start.12) | collective-permute-done | bytes 40992 | tf_op jit(solution)/shard_map/ppermute | solution.py:43
  79.8 1.4 collective-permute-start.15
  81.3 1.7 %collective-permute-done.14 = f32[10,4,1,128]{3,2,1,0:T(1,128)S(1)} collective-permute-done((f32[10,4,1,128]{3,2,1,0:T(1,128)S(1)}, f32[10,4,1,128]{3,2,1,0:T(1,128)S(1)}, u32[]{:S(2)}, u32[]{:S(2)}) %collective-permute-start.14) | collective-permute-done | bytes 20512 | tf_op jit(solution)/shard_map/ppermute | solution.py:43
  84.1 1.7 %collective-permute-start.17 = (f32[10,4,8,1]{3,2,1,0:T(8,128)S(1)}, f32[10,4,8,1]{3,2,1,0:T(8,128)S(1)}, u32[]{:S(2)}, u32[]{:S(2)}) collective-permute-start(f32[10,4,8,1]{3,2,1,0:T(8,128)S(1)} %get-tuple-element.89), channel_id=1, source_target_pairs={{1,0},{2,1},{3,2},{0,3},{5,4},{6,5},{7,6},{4,7},{9,8},{10,9},{11,1... | collective-permute-start | bytes 3848 | tf_op jit(solution)/shard_map/ppermute | solution.py:45
  85.8 3.0 %collective-permute-done.16 = f32[10,4,8,1]{3,2,1,0:T(8,128)S(1)} collective-permute-done((f32[10,4,8,1]{3,2,1,0:T(8,128)S(1)}, f32[10,4,8,1]{3,2,1,0:T(8,128)S(1)}, u32[]{:S(2)}, u32[]{:S(2)}) %collective-permute-start.16) | collective-permute-done | bytes 1312 | tf_op jit(solution)/shard_map/ppermute | solution.py:43
  88.8 1.2 collective-permute-done.17
  90.5 1.3 collective-permute-start.18
  91.8 2.6 %collective-permute-start.19 = (f32[3,1,8,128]{3,2,1,0:T(8,128)S(1)}, f32[3,1,8,128]{3,2,1,0:T(8,128)S(1)}, u32[]{:S(2)}, u32[]{:S(2)}) collective-permute-start(f32[3,1,8,128]{3,2,1,0:T(8,128)S(1)} %get-tuple-element.114), channel_id=1, source_target_pairs={{8,0},{16,8},{24,16},{0,24},{9,1},{17,9},{25,17},{1,25},{10,2},{18... | collective-permute-start | bytes 36872 | tf_op jit(solution)/shard_map/ppermute | solution.py:45
  94.4 1.7 %collective-permute-done.18 = f32[3,1,8,128]{3,2,1,0:T(8,128)S(1)} collective-permute-done((f32[3,1,8,128]{3,2,1,0:T(8,128)S(1)}, f32[3,1,8,128]{3,2,1,0:T(8,128)S(1)}, u32[]{:S(2)}, u32[]{:S(2)}) %collective-permute-start.18) | collective-permute-done | bytes 12320 | tf_op jit(solution)/shard_map/ppermute | solution.py:43
  96.1 1.4 collective-permute-start.20
  98.2 1.6 %collective-permute-done.20 = f32[3,6,1,128]{3,2,1,0:T(1,128)S(1)} collective-permute-done((f32[3,6,1,128]{3,2,1,0:T(1,128)S(1)}, f32[3,6,1,128]{3,2,1,0:T(1,128)S(1)}, u32[]{:S(2)}, u32[]{:S(2)}) %collective-permute-start.20) | collective-permute-done | bytes 9248 | tf_op jit(solution)/shard_map/ppermute | solution.py:43
  99.8 1.3 collective-permute-done.21
  101.4 1.7 %collective-permute-start.23 = (f32[3,6,10,1]{3,2,1,0:T(8,128)S(1)}, f32[3,6,10,1]{3,2,1,0:T(8,128)S(1)}, u32[]{:S(2)}, u32[]{:S(2)}) collective-permute-start(f32[3,6,10,1]{3,2,1,0:T(8,128)S(1)} %get-tuple-element.95), channel_id=1, source_target_pairs={{1,0},{2,1},{3,2},{0,3},{5,4},{6,5},{7,6},{4,7},{9,8},{10,9},{11,1... | collective-permute-start | bytes 2168 | tf_op jit(solution)/shard_map/ppermute | solution.py:45
  103.1 2.8 %collective-permute-done.22 = f32[3,6,10,1]{3,2,1,0:T(8,128)S(1)} collective-permute-done((f32[3,6,10,1]{3,2,1,0:T(8,128)S(1)}, f32[3,6,10,1]{3,2,1,0:T(8,128)S(1)}, u32[]{:S(2)}, u32[]{:S(2)}) %collective-permute-start.22) | collective-permute-done | bytes 752 | tf_op jit(solution)/shard_map/ppermute | solution.py:43
  105.9 1.0 collective-permute-done.23
  107.2 3.3 %fusion.17 = f32[3,4096]{1,0:T(4,128)S(1)} fusion(f32[4096,60]{0,1:T(8,128)S(1)} %mul.1044, f32[3,60,130]{2,1,0:T(8,128)S(1)} %reshape.521, f32[4096]{0:T(1024)S(1)} %bitcast.917, s32[4096]{0:T(1024)S(1)} %get-tuple-element.118, f32[4096]{0:T(1024)S(1)} %broadcast_subtract_fusion.2, s32[4096]{0:T(1024)S(1)} %get-tuple-element.117), kind=kOutput, calls=%fused_computation.23 | convolution fusion | flops 1154281472 | bytes 1191328 | tf_op jit(solution)/shard_map/nz,dkz->dnk/dot_general | solution.py:185
  110.6 3.2 %fusion.2 = f32[3,60,130]{2,1,0:T(8,128)S(1)} fusion(f32[3,4096]{1,0:T(4,128)S(1)} %get-tuple-element.77, f32[4096,60]{0,1:T(8,128)S(1)} %mul.1044, f32[4096]{0:T(1024)S(1)} %bitcast.918, s32[4096]{0:T(1024)S(1)} %get-tuple-element.118, f32[4096]{0:T(1024)S(1)} %broadcast_subtract_fusion.2, s32[4096]{0:T(1024)S(1)} %get-tuple-element.117), kind=kOutput, calls=%fused_computation.7 | convolution fusion | flops 1153556480 | bytes 1191328 | tf_op jit(solution)/shard_map/dnk,nz->dkz/dot_general | solution.py:193
  113.9 1.4 collective-permute-start.24
  115.2 2.6 %collective-permute-start.25 = (f32[3,1,10,130]{3,2,1,0:T(8,128)S(1)}, f32[3,1,10,130]{3,2,1,0:T(8,128)S(1)}, u32[]{:S(2)}, u32[]{:S(2)}) collective-permute-start(f32[3,1,10,130]{3,2,1,0:T(8,128)S(1)} %get-tuple-element.72), channel_id=1, source_target_pairs={{8,0},{16,8},{24,16},{0,24},{9,1},{17,9},{25,17},{1,25},{10,2},{18... | collective-permute-start | bytes 46808 | tf_op jit(solution)/shard_map/ppermute | solution.py:45
  117.9 2.3 %collective-permute-done.24 = f32[3,1,10,130]{3,2,1,0:T(8,128)S(1)} collective-permute-done((f32[3,1,10,130]{3,2,1,0:T(8,128)S(1)}, f32[3,1,10,130]{3,2,1,0:T(8,128)S(1)}, u32[]{:S(2)}, u32[]{:S(2)}) %collective-permute-start.24) | collective-permute-done | bytes 15632 | tf_op jit(solution)/shard_map/ppermute | solution.py:43
  120.8 1.0 collective-permute-start.26
  121.8 1.1 collective-permute-start.27
  122.9 1.8 %collective-permute-done.26 = f32[3,8,1,130]{3,2,1,0:T(1,128)S(1)} collective-permute-done((f32[3,8,1,130]{3,2,1,0:T(1,128)S(1)}, f32[3,8,1,130]{3,2,1,0:T(1,128)S(1)}, u32[]{:S(2)}, u32[]{:S(2)}) %collective-permute-start.26) | collective-permute-done | bytes 12512 | tf_op jit(solution)/shard_map/ppermute | solution.py:43
  124.7 0.9 collective-permute-done.27
  125.9 1.7 %collective-permute-start.29 = (f32[3,8,12,1]{3,2,1,0:T(8,128)S(1)}, f32[3,8,12,1]{3,2,1,0:T(8,128)S(1)}, u32[]{:S(2)}, u32[]{:S(2)}) collective-permute-start(f32[3,8,12,1]{3,2,1,0:T(8,128)S(1)} %get-tuple-element.25), channel_id=1, source_target_pairs={{1,0},{2,1},{3,2},{0,3},{5,4},{6,5},{7,6},{4,7},{9,8},{10,9},{11,1... | collective-permute-start | bytes 3464 | tf_op jit(solution)/shard_map/ppermute | solution.py:45
  127.6 3.3 %collective-permute-done.28 = f32[3,8,12,1]{3,2,1,0:T(8,128)S(1)} collective-permute-done((f32[3,8,12,1]{3,2,1,0:T(8,128)S(1)}, f32[3,8,12,1]{3,2,1,0:T(8,128)S(1)}, u32[]{:S(2)}, u32[]{:S(2)}) %collective-permute-start.28) | collective-permute-done | bytes 1184 | tf_op jit(solution)/shard_map/ppermute | solution.py:43
  131.0 1.6 %collective-permute-done.29 = f32[3,8,12,1]{3,2,1,0:T(8,128)S(1)} collective-permute-done((f32[3,8,12,1]{3,2,1,0:T(8,128)S(1)}, f32[3,8,12,1]{3,2,1,0:T(8,128)S(1)}, u32[]{:S(2)}, u32[]{:S(2)}) %collective-permute-start.29) | collective-permute-done | bytes 1184 | tf_op jit(solution)/shard_map/ppermute | solution.py:45
  133.9 1.1 collective-permute-start.30
  135.2 2.7 %collective-permute-start.31 = (f32[10,1,8,128]{3,2,1,0:T(8,128)S(1)}, f32[10,1,8,128]{3,2,1,0:T(8,128)S(1)}, u32[]{:S(2)}, u32[]{:S(2)}) collective-permute-start(f32[10,1,8,128]{3,2,1,0:T(8,128)S(1)} %get-tuple-element.86), channel_id=1, source_target_pairs={{8,0},{16,8},{24,16},{0,24},{9,1},{17,9},{25,17},{1,25},{10,2},{18... | collective-permute-start | bytes 122888 | tf_op jit(solution)/shard_map/ppermute | solution.py:45
  137.9 2.0 %collective-permute-done.30 = f32[10,1,8,128]{3,2,1,0:T(8,128)S(1)} collective-permute-done((f32[10,1,8,128]{3,2,1,0:T(8,128)S(1)}, f32[10,1,8,128]{3,2,1,0:T(8,128)S(1)}, u32[]{:S(2)}, u32[]{:S(2)}) %collective-permute-start.30) | collective-permute-done | bytes 40992 | tf_op jit(solution)/shard_map/ppermute | solution.py:43
  140.4 1.0 collective-permute-start.32
  141.4 1.1 collective-permute-start.33
  142.5 1.8 %collective-permute-done.32 = f32[10,4,1,128]{3,2,1,0:T(1,128)S(1)} collective-permute-done((f32[10,4,1,128]{3,2,1,0:T(1,128)S(1)}, f32[10,4,1,128]{3,2,1,0:T(1,128)S(1)}, u32[]{:S(2)}, u32[]{:S(2)}) %collective-permute-start.32) | collective-permute-done | bytes 20512 | tf_op jit(solution)/shard_map/ppermute | solution.py:43
  144.3 0.9 collective-permute-done.33
  145.5 1.7 %collective-permute-start.35 = (f32[10,4,8,1]{3,2,1,0:T(8,128)S(1)}, f32[10,4,8,1]{3,2,1,0:T(8,128)S(1)}, u32[]{:S(2)}, u32[]{:S(2)}) collective-permute-start(f32[10,4,8,1]{3,2,1,0:T(8,128)S(1)} %get-tuple-element.83), channel_id=1, source_target_pairs={{1,0},{2,1},{3,2},{0,3},{5,4},{6,5},{7,6},{4,7},{9,8},{10,9},{11,1... | collective-permute-start | bytes 3848 | tf_op jit(solution)/shard_map/ppermute | solution.py:45
  147.9 2.4 %collective-permute-done.34 = f32[10,4,8,1]{3,2,1,0:T(8,128)S(1)} collective-permute-done((f32[10,4,8,1]{3,2,1,0:T(8,128)S(1)}, f32[10,4,8,1]{3,2,1,0:T(8,128)S(1)}, u32[]{:S(2)}, u32[]{:S(2)}) %collective-permute-start.34) | collective-permute-done | bytes 1312 | tf_op jit(solution)/shard_map/ppermute | solution.py:43
  150.3 1.2 collective-permute-done.35
  (189 shorter events, 20.6 us)
Async XLA Ops:
  0.6 19.5 %copy-start = (s32[16,128]{1,0:T(8,128)S(1)}, s32[16,128]{1,0:T(8,128)}, u32[]{:S(2)}) copy-start(s32[16,128]{1,0:T(8,128)} %param.13) | copy-start | bytes 24580
  3.3 17.4 %collective-permute-start = (f32[3,1,8,128]{3,2,1,0:T(8,128)S(1)}, f32[3,1,8,128]{3,2,1,0:T(8,128)S(1)}, u32[]{:S(2)}, u32[]{:S(2)}) collective-permute-start(f32[3,1,8,128]{3,2,1,0:T(8,128)S(1)} %get-tuple-element.115), channel_id=1, source_target_pairs={{0,8},{8,16},{16,24},{24,0},{1,9},{9,17},{17,25},{25,1},{2,10},{10... | collective-permute-start | bytes 36872 | tf_op jit(solution)/shard_map/ppermute | solution.py:43
  6.4 14.4 %collective-permute-start.1 = (f32[3,1,8,128]{3,2,1,0:T(8,128)S(1)}, f32[3,1,8,128]{3,2,1,0:T(8,128)S(1)}, u32[]{:S(2)}, u32[]{:S(2)}) collective-permute-start(f32[3,1,8,128]{3,2,1,0:T(8,128)S(1)} %get-tuple-element.116), channel_id=1, source_target_pairs={{8,0},{16,8},{24,16},{0,24},{9,1},{17,9},{25,17},{1,25},{10,2},{18... | collective-permute-start | bytes 36872 | tf_op jit(solution)/shard_map/ppermute | solution.py:45
  13.1 10.4 %all-to-all-start = ((s32[4,8,1]{1,2,0:T(1,128)}), s32[4,8,1]{1,2,0:T(1,128)S(1)}, u32[]{:S(2)}, u32[]{:S(2)}) async-start(s32[4,8,1]{1,2,0:T(1,128)} %bitcast.22), calls=%async_computation | async-start | bytes 4096 | tf_op jit(solution)/shard_map/all_to_all | solution.py:158
  20.8 9.1 %collective-permute-start.2 = (f32[3,6,1,128]{3,2,1,0:T(1,128)S(1)}, f32[3,6,1,128]{3,2,1,0:T(1,128)S(1)}, u32[]{:S(2)}, u32[]{:S(2)}) collective-permute-start(f32[3,6,1,128]{3,2,1,0:T(1,128)S(1)} %get-tuple-element.111), channel_id=1, source_target_pairs={{0,4},{4,0},{1,5},{5,1},{2,6},{6,2},{3,7},{7,3},{8,12},{12,8},{9,1... | collective-permute-start | bytes 27656 | tf_op jit(solution)/shard_map/ppermute | solution.py:43
  22.5 7.4 %collective-permute-start.3 = (f32[3,6,1,128]{3,2,1,0:T(1,128)S(1)}, f32[3,6,1,128]{3,2,1,0:T(1,128)S(1)}, u32[]{:S(2)}, u32[]{:S(2)}) collective-permute-start(f32[3,6,1,128]{3,2,1,0:T(1,128)S(1)} %get-tuple-element.112), channel_id=1, source_target_pairs={{4,0},{0,4},{5,1},{1,5},{6,2},{2,6},{7,3},{3,7},{12,8},{8,12},{13,... | collective-permute-start | bytes 27656 | tf_op jit(solution)/shard_map/ppermute | solution.py:45
  23.6 12.2 %all-to-all-start.1 = ((f32[32,7,128]{2,1,0:T(8,128)}), f32[32,7,128]{2,1,0:T(8,128)S(1)}, u32[]{:S(2)}, u32[]{:S(2)}) async-start(f32[32,7,128]{2,1,0:T(8,128)} %select_select_fusion), calls=%async_computation.1 | async-start | bytes 262144 | tf_op jit(solution)/shard_map/all_to_all | solution.py:156
  30.1 4.6 %collective-permute-start.4 = (f32[3,6,10,1]{3,2,1,0:T(8,128)S(1)}, f32[3,6,10,1]{3,2,1,0:T(8,128)S(1)}, u32[]{:S(2)}, u32[]{:S(2)}) collective-permute-start(f32[3,6,10,1]{3,2,1,0:T(8,128)S(1)} %get-tuple-element.96), channel_id=1, source_target_pairs={{0,1},{1,2},{2,3},{3,0},{4,5},{5,6},{6,7},{7,4},{8,9},{9,10},{10,1... | collective-permute-start | bytes 2168 | tf_op jit(solution)/shard_map/ppermute | solution.py:43
  30.1 5.3 %collective-permute-start.5 = (f32[3,6,10,1]{3,2,1,0:T(8,128)S(1)}, f32[3,6,10,1]{3,2,1,0:T(8,128)S(1)}, u32[]{:S(2)}, u32[]{:S(2)}) collective-permute-start(f32[3,6,10,1]{3,2,1,0:T(8,128)S(1)} %get-tuple-element.97), channel_id=1, source_target_pairs={{1,0},{2,1},{3,2},{0,3},{5,4},{6,5},{7,6},{4,7},{9,8},{10,9},{11,1... | collective-permute-start | bytes 2168 | tf_op jit(solution)/shard_map/ppermute | solution.py:45
  35.7 10.7 %all-to-all-start.2 = ((s32[4,8,128]{2,1,0:T(8,128)}), s32[4,8,128]{2,1,0:T(8,128)S(1)}, u32[]{:S(2)}, u32[]{:S(2)}) async-start(s32[4,8,128]{2,1,0:T(8,128)} %fusion.422), calls=%async_computation.2 | async-start | bytes 32768 | tf_op jit(solution)/shard_map/all_to_all | solution.py:157
  53.5 5.9 %collective-permute-start.6 = (f32[3,1,10,130]{3,2,1,0:T(8,128)S(1)}, f32[3,1,10,130]{3,2,1,0:T(8,128)S(1)}, u32[]{:S(2)}, u32[]{:S(2)}) collective-permute-start(f32[3,1,10,130]{3,2,1,0:T(8,128)S(1)} %get-tuple-element.75), channel_id=1, source_target_pairs={{0,8},{8,16},{16,24},{24,0},{1,9},{9,17},{17,25},{25,1},{2,10},{10... | collective-permute-start | bytes 46808 | tf_op jit(solution)/shard_map/ppermute | solution.py:43
  54.2 5.3 %collective-permute-start.7 = (f32[3,1,10,130]{3,2,1,0:T(8,128)S(1)}, f32[3,1,10,130]{3,2,1,0:T(8,128)S(1)}, u32[]{:S(2)}, u32[]{:S(2)}) collective-permute-start(f32[3,1,10,130]{3,2,1,0:T(8,128)S(1)} %get-tuple-element.74), channel_id=1, source_target_pairs={{8,0},{16,8},{24,16},{0,24},{9,1},{17,9},{25,17},{1,25},{10,2},{18... | collective-permute-start | bytes 46808 | tf_op jit(solution)/shard_map/ppermute | solution.py:45
  59.4 12.5 %copy-start.5 = (pred[4]{0:T(512)(128)(4,1)S(1)}, pred[4]{0:T(512)(128)(4,1)}, u32[]{:S(2)}) copy-start(pred[4]{0:T(512)(128)(4,1)} %constant.133.clone.1) | copy-start | bytes 16
  59.5 3.9 %collective-permute-start.8 = (f32[3,8,1,130]{3,2,1,0:T(1,128)S(1)}, f32[3,8,1,130]{3,2,1,0:T(1,128)S(1)}, u32[]{:S(2)}, u32[]{:S(2)}) collective-permute-start(f32[3,8,1,130]{3,2,1,0:T(1,128)S(1)} %get-tuple-element.30), channel_id=1, source_target_pairs={{0,4},{4,0},{1,5},{5,1},{2,6},{6,2},{3,7},{7,3},{8,12},{12,8},{9,1... | collective-permute-start | bytes 37448 | tf_op jit(solution)/shard_map/ppermute | solution.py:43
  61.1 3.8 %collective-permute-start.9 = (f32[3,8,1,130]{3,2,1,0:T(1,128)S(1)}, f32[3,8,1,130]{3,2,1,0:T(1,128)S(1)}, u32[]{:S(2)}, u32[]{:S(2)}) collective-permute-start(f32[3,8,1,130]{3,2,1,0:T(1,128)S(1)} %get-tuple-element.31), channel_id=1, source_target_pairs={{4,0},{0,4},{5,1},{1,5},{6,2},{2,6},{7,3},{3,7},{12,8},{8,12},{13,... | collective-permute-start | bytes 37448 | tf_op jit(solution)/shard_map/ppermute | solution.py:45
  65.0 7.1 %copy-start.4 = (pred[8]{0:T(512)(128)(4,1)S(1)}, pred[8]{0:T(512)(128)(4,1)}, u32[]{:S(2)}) copy-start(pred[8]{0:T(512)(128)(4,1)} %constant.134.clone.1) | copy-start | bytes 28
  65.1 7.2 %copy-start.3 = (pred[128]{0:T(512)(128)(4,1)S(1)}, pred[128]{0:T(512)(128)(4,1)}, u32[]{:S(2)}) copy-start(pred[128]{0:T(512)(128)(4,1)} %constant.135.clone.1) | copy-start | bytes 388
  65.1 5.2 %collective-permute-start.10 = (f32[3,8,12,1]{3,2,1,0:T(8,128)S(1)}, f32[3,8,12,1]{3,2,1,0:T(8,128)S(1)}, u32[]{:S(2)}, u32[]{:S(2)}) collective-permute-start(f32[3,8,12,1]{3,2,1,0:T(8,128)S(1)} %get-tuple-element.28), channel_id=1, source_target_pairs={{0,1},{1,2},{2,3},{3,0},{4,5},{5,6},{6,7},{7,4},{8,9},{9,10},{10,1... | collective-permute-start | bytes 3464 | tf_op jit(solution)/shard_map/ppermute | solution.py:43
  65.2 7.2 %copy-start.1 = (s32[4,8,128]{2,1,0:T(8,128)S(1)}, s32[4,8,128]{2,1,0:T(8,128)}, u32[]{:S(2)}) copy-start(s32[4,8,128]{2,1,0:T(8,128)} %param.9) | copy-start | bytes 49156
  65.2 7.2 %copy-start.2 = (f32[19,4,8,128]{3,2,1,0:T(8,128)S(1)}, f32[19,4,8,128]{3,2,1,0:T(8,128)}, u32[]{:S(2)}) copy-start(f32[19,4,8,128]{3,2,1,0:T(8,128)} %param.8) | copy-start | bytes 933892
  65.2 6.4 %collective-permute-start.11 = (f32[3,8,12,1]{3,2,1,0:T(8,128)S(1)}, f32[3,8,12,1]{3,2,1,0:T(8,128)S(1)}, u32[]{:S(2)}, u32[]{:S(2)}) collective-permute-start(f32[3,8,12,1]{3,2,1,0:T(8,128)S(1)} %get-tuple-element.29), channel_id=1, source_target_pairs={{1,0},{2,1},{3,2},{0,3},{5,4},{6,5},{7,6},{4,7},{9,8},{10,9},{11,1... | collective-permute-start | bytes 3464 | tf_op jit(solution)/shard_map/ppermute | solution.py:45
  72.8 6.2 %collective-permute-start.12 = (f32[10,1,8,128]{3,2,1,0:T(8,128)S(1)}, f32[10,1,8,128]{3,2,1,0:T(8,128)S(1)}, u32[]{:S(2)}, u32[]{:S(2)}) collective-permute-start(f32[10,1,8,128]{3,2,1,0:T(8,128)S(1)} %get-tuple-element.93), channel_id=1, source_target_pairs={{0,8},{8,16},{16,24},{24,0},{1,9},{9,17},{17,25},{25,1},{2,10},{10... | collective-permute-start | bytes 122888 | tf_op jit(solution)/shard_map/ppermute | solution.py:43
  72.8 6.1 %collective-permute-start.13 = (f32[10,1,8,128]{3,2,1,0:T(8,128)S(1)}, f32[10,1,8,128]{3,2,1,0:T(8,128)S(1)}, u32[]{:S(2)}, u32[]{:S(2)}) collective-permute-start(f32[10,1,8,128]{3,2,1,0:T(8,128)S(1)} %get-tuple-element.92), channel_id=1, source_target_pairs={{8,0},{16,8},{24,16},{0,24},{9,1},{17,9},{25,17},{1,25},{10,2},{18... | collective-permute-start | bytes 122888 | tf_op jit(solution)/shard_map/ppermute | solution.py:45
  79.2 3.8 %collective-permute-start.14 = (f32[10,4,1,128]{3,2,1,0:T(1,128)S(1)}, f32[10,4,1,128]{3,2,1,0:T(1,128)S(1)}, u32[]{:S(2)}, u32[]{:S(2)}) collective-permute-start(f32[10,4,1,128]{3,2,1,0:T(1,128)S(1)} %get-tuple-element.90), channel_id=1, source_target_pairs={{0,4},{4,0},{1,5},{5,1},{2,6},{6,2},{3,7},{7,3},{8,12},{12,8},{9,1... | collective-permute-start | bytes 61448 | tf_op jit(solution)/shard_map/ppermute | solution.py:43
  79.8 3.8 %collective-permute-start.15 = (f32[10,4,1,128]{3,2,1,0:T(1,128)S(1)}, f32[10,4,1,128]{3,2,1,0:T(1,128)S(1)}, u32[]{:S(2)}, u32[]{:S(2)}) collective-permute-start(f32[10,4,1,128]{3,2,1,0:T(1,128)S(1)} %get-tuple-element.91), channel_id=1, source_target_pairs={{4,0},{0,4},{5,1},{1,5},{6,2},{2,6},{7,3},{3,7},{12,8},{8,12},{13,... | collective-permute-start | bytes 61448 | tf_op jit(solution)/shard_map/ppermute | solution.py:45
  83.9 5.0 %collective-permute-start.16 = (f32[10,4,8,1]{3,2,1,0:T(8,128)S(1)}, f32[10,4,8,1]{3,2,1,0:T(8,128)S(1)}, u32[]{:S(2)}, u32[]{:S(2)}) collective-permute-start(f32[10,4,8,1]{3,2,1,0:T(8,128)S(1)} %get-tuple-element.88), channel_id=1, source_target_pairs={{0,1},{1,2},{2,3},{3,0},{4,5},{5,6},{6,7},{7,4},{8,9},{9,10},{10,1... | collective-permute-start | bytes 3848 | tf_op jit(solution)/shard_map/ppermute | solution.py:43
  84.1 5.9 %collective-permute-start.17 = (f32[10,4,8,1]{3,2,1,0:T(8,128)S(1)}, f32[10,4,8,1]{3,2,1,0:T(8,128)S(1)}, u32[]{:S(2)}, u32[]{:S(2)}) collective-permute-start(f32[10,4,8,1]{3,2,1,0:T(8,128)S(1)} %get-tuple-element.89), channel_id=1, source_target_pairs={{1,0},{2,1},{3,2},{0,3},{5,4},{6,5},{7,6},{4,7},{9,8},{10,9},{11,1... | collective-permute-start | bytes 3848 | tf_op jit(solution)/shard_map/ppermute | solution.py:45
  90.5 5.6 %collective-permute-start.18 = (f32[3,1,8,128]{3,2,1,0:T(8,128)S(1)}, f32[3,1,8,128]{3,2,1,0:T(8,128)S(1)}, u32[]{:S(2)}, u32[]{:S(2)}) collective-permute-start(f32[3,1,8,128]{3,2,1,0:T(8,128)S(1)} %get-tuple-element.113), channel_id=1, source_target_pairs={{0,8},{8,16},{16,24},{24,0},{1,9},{9,17},{17,25},{25,1},{2,10},{10... | collective-permute-start | bytes 36872 | tf_op jit(solution)/shard_map/ppermute | solution.py:43
  91.8 4.3 %collective-permute-start.19 = (f32[3,1,8,128]{3,2,1,0:T(8,128)S(1)}, f32[3,1,8,128]{3,2,1,0:T(8,128)S(1)}, u32[]{:S(2)}, u32[]{:S(2)}) collective-permute-start(f32[3,1,8,128]{3,2,1,0:T(8,128)S(1)} %get-tuple-element.114), channel_id=1, source_target_pairs={{8,0},{16,8},{24,16},{0,24},{9,1},{17,9},{25,17},{1,25},{10,2},{18... | collective-permute-start | bytes 36872 | tf_op jit(solution)/shard_map/ppermute | solution.py:45
  96.1 3.7 %collective-permute-start.20 = (f32[3,6,1,128]{3,2,1,0:T(1,128)S(1)}, f32[3,6,1,128]{3,2,1,0:T(1,128)S(1)}, u32[]{:S(2)}, u32[]{:S(2)}) collective-permute-start(f32[3,6,1,128]{3,2,1,0:T(1,128)S(1)} %get-tuple-element.109), channel_id=1, source_target_pairs={{0,4},{4,0},{1,5},{5,1},{2,6},{6,2},{3,7},{7,3},{8,12},{12,8},{9,1... | collective-permute-start | bytes 27656 | tf_op jit(solution)/shard_map/ppermute | solution.py:43
  97.5 3.7 %collective-permute-start.21 = (f32[3,6,1,128]{3,2,1,0:T(1,128)S(1)}, f32[3,6,1,128]{3,2,1,0:T(1,128)S(1)}, u32[]{:S(2)}, u32[]{:S(2)}) collective-permute-start(f32[3,6,1,128]{3,2,1,0:T(1,128)S(1)} %get-tuple-element.110), channel_id=1, source_target_pairs={{4,0},{0,4},{5,1},{1,5},{6,2},{2,6},{7,3},{3,7},{12,8},{8,12},{13,... | collective-permute-start | bytes 27656 | tf_op jit(solution)/shard_map/ppermute | solution.py:45
  101.3 4.6 %collective-permute-start.22 = (f32[3,6,10,1]{3,2,1,0:T(8,128)S(1)}, f32[3,6,10,1]{3,2,1,0:T(8,128)S(1)}, u32[]{:S(2)}, u32[]{:S(2)}) collective-permute-start(f32[3,6,10,1]{3,2,1,0:T(8,128)S(1)} %get-tuple-element.94), channel_id=1, source_target_pairs={{0,1},{1,2},{2,3},{3,0},{4,5},{5,6},{6,7},{7,4},{8,9},{9,10},{10,1... | collective-permute-start | bytes 2168 | tf_op jit(solution)/shard_map/ppermute | solution.py:43
  101.4 5.6 %collective-permute-start.23 = (f32[3,6,10,1]{3,2,1,0:T(8,128)S(1)}, f32[3,6,10,1]{3,2,1,0:T(8,128)S(1)}, u32[]{:S(2)}, u32[]{:S(2)}) collective-permute-start(f32[3,6,10,1]{3,2,1,0:T(8,128)S(1)} %get-tuple-element.95), channel_id=1, source_target_pairs={{1,0},{2,1},{3,2},{0,3},{5,4},{6,5},{7,6},{4,7},{9,8},{10,9},{11,1... | collective-permute-start | bytes 2168 | tf_op jit(solution)/shard_map/ppermute | solution.py:45
  113.9 6.3 %collective-permute-start.24 = (f32[3,1,10,130]{3,2,1,0:T(8,128)S(1)}, f32[3,1,10,130]{3,2,1,0:T(8,128)S(1)}, u32[]{:S(2)}, u32[]{:S(2)}) collective-permute-start(f32[3,1,10,130]{3,2,1,0:T(8,128)S(1)} %get-tuple-element.73), channel_id=1, source_target_pairs={{0,8},{8,16},{16,24},{24,0},{1,9},{9,17},{17,25},{25,1},{2,10},{10... | collective-permute-start | bytes 46808 | tf_op jit(solution)/shard_map/ppermute | solution.py:43
  115.2 5.5 %collective-permute-start.25 = (f32[3,1,10,130]{3,2,1,0:T(8,128)S(1)}, f32[3,1,10,130]{3,2,1,0:T(8,128)S(1)}, u32[]{:S(2)}, u32[]{:S(2)}) collective-permute-start(f32[3,1,10,130]{3,2,1,0:T(8,128)S(1)} %get-tuple-element.72), channel_id=1, source_target_pairs={{8,0},{16,8},{24,16},{0,24},{9,1},{17,9},{25,17},{1,25},{10,2},{18... | collective-permute-start | bytes 46808 | tf_op jit(solution)/shard_map/ppermute | solution.py:45
  120.8 3.9 %collective-permute-start.26 = (f32[3,8,1,130]{3,2,1,0:T(1,128)S(1)}, f32[3,8,1,130]{3,2,1,0:T(1,128)S(1)}, u32[]{:S(2)}, u32[]{:S(2)}) collective-permute-start(f32[3,8,1,130]{3,2,1,0:T(1,128)S(1)} %get-tuple-element.26), channel_id=1, source_target_pairs={{0,4},{4,0},{1,5},{5,1},{2,6},{6,2},{3,7},{7,3},{8,12},{12,8},{9,1... | collective-permute-start | bytes 37448 | tf_op jit(solution)/shard_map/ppermute | solution.py:43
  121.8 3.8 %collective-permute-start.27 = (f32[3,8,1,130]{3,2,1,0:T(1,128)S(1)}, f32[3,8,1,130]{3,2,1,0:T(1,128)S(1)}, u32[]{:S(2)}, u32[]{:S(2)}) collective-permute-start(f32[3,8,1,130]{3,2,1,0:T(1,128)S(1)} %get-tuple-element.27), channel_id=1, source_target_pairs={{4,0},{0,4},{5,1},{1,5},{6,2},{2,6},{7,3},{3,7},{12,8},{8,12},{13,... | collective-permute-start | bytes 37448 | tf_op jit(solution)/shard_map/ppermute | solution.py:45
  125.8 5.1 %collective-permute-start.28 = (f32[3,8,12,1]{3,2,1,0:T(8,128)S(1)}, f32[3,8,12,1]{3,2,1,0:T(8,128)S(1)}, u32[]{:S(2)}, u32[]{:S(2)}) collective-permute-start(f32[3,8,12,1]{3,2,1,0:T(8,128)S(1)} %get-tuple-element.24), channel_id=1, source_target_pairs={{0,1},{1,2},{2,3},{3,0},{4,5},{5,6},{6,7},{7,4},{8,9},{9,10},{10,1... | collective-permute-start | bytes 3464 | tf_op jit(solution)/shard_map/ppermute | solution.py:43
  125.9 6.7 %collective-permute-start.29 = (f32[3,8,12,1]{3,2,1,0:T(8,128)S(1)}, f32[3,8,12,1]{3,2,1,0:T(8,128)S(1)}, u32[]{:S(2)}, u32[]{:S(2)}) collective-permute-start(f32[3,8,12,1]{3,2,1,0:T(8,128)S(1)} %get-tuple-element.25), channel_id=1, source_target_pairs={{1,0},{2,1},{3,2},{0,3},{5,4},{6,5},{7,6},{4,7},{9,8},{10,9},{11,1... | collective-permute-start | bytes 3464 | tf_op jit(solution)/shard_map/ppermute | solution.py:45
  133.9 6.0 %collective-permute-start.30 = (f32[10,1,8,128]{3,2,1,0:T(8,128)S(1)}, f32[10,1,8,128]{3,2,1,0:T(8,128)S(1)}, u32[]{:S(2)}, u32[]{:S(2)}) collective-permute-start(f32[10,1,8,128]{3,2,1,0:T(8,128)S(1)} %get-tuple-element.87), channel_id=1, source_target_pairs={{0,8},{8,16},{16,24},{24,0},{1,9},{9,17},{17,25},{25,1},{2,10},{10... | collective-permute-start | bytes 122888 | tf_op jit(solution)/shard_map/ppermute | solution.py:43
  135.2 4.9 %collective-permute-start.31 = (f32[10,1,8,128]{3,2,1,0:T(8,128)S(1)}, f32[10,1,8,128]{3,2,1,0:T(8,128)S(1)}, u32[]{:S(2)}, u32[]{:S(2)}) collective-permute-start(f32[10,1,8,128]{3,2,1,0:T(8,128)S(1)} %get-tuple-element.86), channel_id=1, source_target_pairs={{8,0},{16,8},{24,16},{0,24},{9,1},{17,9},{25,17},{1,25},{10,2},{18... | collective-permute-start | bytes 122888 | tf_op jit(solution)/shard_map/ppermute | solution.py:45
  140.4 3.8 %collective-permute-start.32 = (f32[10,4,1,128]{3,2,1,0:T(1,128)S(1)}, f32[10,4,1,128]{3,2,1,0:T(1,128)S(1)}, u32[]{:S(2)}, u32[]{:S(2)}) collective-permute-start(f32[10,4,1,128]{3,2,1,0:T(1,128)S(1)} %get-tuple-element.84), channel_id=1, source_target_pairs={{0,4},{4,0},{1,5},{5,1},{2,6},{6,2},{3,7},{7,3},{8,12},{12,8},{9,1... | collective-permute-start | bytes 61448 | tf_op jit(solution)/shard_map/ppermute | solution.py:43
  141.4 3.8 %collective-permute-start.33 = (f32[10,4,1,128]{3,2,1,0:T(1,128)S(1)}, f32[10,4,1,128]{3,2,1,0:T(1,128)S(1)}, u32[]{:S(2)}, u32[]{:S(2)}) collective-permute-start(f32[10,4,1,128]{3,2,1,0:T(1,128)S(1)} %get-tuple-element.85), channel_id=1, source_target_pairs={{4,0},{0,4},{5,1},{1,5},{6,2},{2,6},{7,3},{3,7},{12,8},{8,12},{13,... | collective-permute-start | bytes 61448 | tf_op jit(solution)/shard_map/ppermute | solution.py:45
  145.5 4.8 %collective-permute-start.34 = (f32[10,4,8,1]{3,2,1,0:T(8,128)S(1)}, f32[10,4,8,1]{3,2,1,0:T(8,128)S(1)}, u32[]{:S(2)}, u32[]{:S(2)}) collective-permute-start(f32[10,4,8,1]{3,2,1,0:T(8,128)S(1)} %get-tuple-element.82), channel_id=1, source_target_pairs={{0,1},{1,2},{2,3},{3,0},{4,5},{5,6},{6,7},{7,4},{8,9},{9,10},{10,1... | collective-permute-start | bytes 3848 | tf_op jit(solution)/shard_map/ppermute | solution.py:43
  145.5 5.9 %collective-permute-start.35 = (f32[10,4,8,1]{3,2,1,0:T(8,128)S(1)}, f32[10,4,8,1]{3,2,1,0:T(8,128)S(1)}, u32[]{:S(2)}, u32[]{:S(2)}) collective-permute-start(f32[10,4,8,1]{3,2,1,0:T(8,128)S(1)} %get-tuple-element.83), channel_id=1, source_target_pairs={{1,0},{2,1},{3,2},{0,3},{5,4},{6,5},{7,6},{4,7},{9,8},{10,9},{11,1... | collective-permute-start | bytes 3848 | tf_op jit(solution)/shard_map/ppermute | solution.py:45

commit v2 on v1

--- a/solution.py
+++ b/solution.py
@@ -33,20 +33,41 @@
 speed_unit = 0.05
 
 
+def swap(axis, onward, backward):
+    count = lax.axis_size(axis)
+    if count == 2:
+        both = lax.ppermute(jnp.stack([onward, backward]), axis, [(0, 1), (1, 0)])
+        return (both[0], both[1])
+    return (
+        lax.ppermute(onward, axis, [(i, (i + 1) % count) for i in range(count)]),
+        lax.ppermute(backward, axis, [((i + 1) % count, i) for i in range(count)]),
+    )
+
+
 def with_halo(cells, sides, width):
     for axis, dim in sides:
-        count = lax.axis_size(axis)
+        length = cells.shape[dim]
         head = lax.slice_in_dim(cells, 0, width, axis=dim)
-        tail = lax.slice_in_dim(cells, cells.shape[dim] - width, cells.shape[dim], axis=dim)
-        cells = jnp.concatenate(
-            [
-                lax.ppermute(tail, axis, [(i, (i + 1) % count) for i in range(count)]),
-                cells,
-                lax.ppermute(head, axis, [((i + 1) % count, i) for i in range(count)]),
-            ],
-            axis=dim,
-        )
+        tail = lax.slice_in_dim(cells, length - width, length, axis=dim)
+        before, after = swap(axis, tail, head)
+        cells = jnp.concatenate([before, cells, after], axis=dim)
     return cells
+
+
+def spread_sums(ghosts, sides, width):
+    for axis, dim in sides:
+        length = ghosts.shape[dim]
+        head = lax.slice_in_dim(ghosts, 0, width + 1, axis=dim)
+        tail = lax.slice_in_dim(ghosts, length - width - 1, length, axis=dim)
+        before, after = swap(axis, tail, head)
+        around = [(0, 0)] * 4
+        around[dim] = (width - 1, width - 1)
+        low, high = list(around), list(around)
+        rest = length + 2 * (width - 1) - (width + 1)
+        low[dim] = (0, rest)
+        high[dim] = (rest, 0)
+        ghosts = jnp.pad(ghosts, around) + jnp.pad(before, low) + jnp.pad(after, high)
+    return ghosts
 
 
 def project(vector, direction):
@@ -90,38 +111,15 @@
     return post_list
 
 
-def fold_ghost(widened, dim):
-    length = widened.shape[dim] - 4
-    folded = lax.slice_in_dim(widened, 2, length + 2, axis=dim)
-    lower = lax.slice_in_dim(widened, 0, 1, axis=dim)
-    upper = lax.slice_in_dim(widened, length + 3, length + 4, axis=dim)
-    lower_pad = [(0, 0)] * 4
-    upper_pad = [(0, 0)] * 4
-    lower_pad[dim] = (0, length - 1)
-    upper_pad[dim] = (length - 1, 0)
-    return folded + jnp.pad(lower, lower_pad) + jnp.pad(upper, upper_pad)
-
-
-def move_layers(layers, moving, widened, dim):
-    for k, i in enumerate(moving):
-        extent = layers[i].shape[dim]
-        start = 1 - directions[i][dim]
-        layers[i] = lax.slice_in_dim(widened[k], start, start + extent, axis=dim)
-    return layers
-
-
-def propagate_by_axis(post_list):
-    layers = list(post_list)
-    moving = [i for i in range(19) if directions[i][0] != 0]
-    widened = with_halo(jnp.stack([layers[i] for i in moving]), (("gx", 1),), 1)
-    layers = move_layers(layers, moving, widened, 0)
-    moving = [i for i in range(19) if directions[i][1] != 0]
-    widened = with_halo(jnp.stack([layers[i] for i in moving]), (("gy", 2),), 1)
-    layers = move_layers(layers, moving, widened, 1)
-    moving = [i for i in range(19) if directions[i][2] != 0]
-    widened = with_halo(jnp.stack([layers[i] for i in moving]), (("gz", 3),), 1)
-    layers = move_layers(layers, moving, widened, 2)
-    return layers
+def propagate(post_list):
+    moved = []
+    for i in range(19):
+        layer = post_list[i]
+        for dim in range(3):
+            start = 1 - directions[i][dim]
+            layer = lax.slice_in_dim(layer, start, start + layer.shape[dim] - 2, axis=dim)
+        moved.append(layer)
+    return moved
 
 
 def per_device(
@@ -148,19 +146,19 @@
     match = slot_index[None, :] == jnp.arange(slot_count, dtype=jnp.int32)[:, None]
     filled = jnp.any(match, axis=1)
     source = jnp.sum(jnp.where(match, jnp.arange(block_count, dtype=jnp.int32)[None, :], 0), axis=1)
-    floats = jnp.concatenate([part_offset, part_velocity, part_drag[:, None, :]], axis=1)
-    send_floats = jnp.where(filled[:, None, None], jnp.take(floats, source, axis=0), 0.0)
-    send_cells = jnp.where(filled[:, None], jnp.take(part_cell, source, axis=0), 0)
-    send_rows = jnp.where(filled, jnp.take(block_rows, source, axis=0), 0)
-    got_floats, got_cells, got_rows = (
-        lax.all_to_all(send_floats, "gx", split_axis=0, concat_axis=0, tiled=True),
-        lax.all_to_all(send_cells, "gx", split_axis=0, concat_axis=0, tiled=True),
-        lax.all_to_all(send_rows, "gx", split_axis=0, concat_axis=0, tiled=True),
-    )
+    alive = jnp.arange(rows_block, dtype=jnp.int32)[None, :] < block_rows[:, None]
+    named = jnp.where(alive, part_cell, -1).astype(jnp.float32)
+    floats = jnp.concatenate(
+        [part_offset, part_velocity, part_drag[:, None, :], named[:, None, :]], axis=1
+    )
+    empty = jnp.where(jnp.arange(8) == 7, -1.0, 0.0).astype(jnp.float32)[None, :, None]
+    send_floats = jnp.where(filled[:, None, None], jnp.take(floats, source, axis=0), empty)
+    got_floats = lax.all_to_all(send_floats, "gx", split_axis=0, concat_axis=0, tiled=True)
     offset = got_floats[:, 0:3, :]
     velocity = got_floats[:, 3:6, :]
     drag_rate = got_floats[:, 6, :]
-    live_rows = jnp.arange(rows_block, dtype=jnp.int32)[None, :] < got_rows[:, None]
+    live_rows = got_floats[:, 7, :] >= 0.0
+    got_cells = jnp.maximum(got_floats[:, 7, :], 0.0).astype(jnp.int32)
     p = got_cells // (size_y * size_z) + 1
     q = got_cells // size_z % size_y + 1
     s = got_cells % size_z + 1
@@ -176,13 +174,19 @@
             + jnp.where(grid == farther[:, None], jnp.abs(displace)[:, None], 0.0)
         )
     across = (tables[0][:, :, None] * tables[1][:, None, :]).reshape(slots * rows_block, -1)
-    gray_fraction = solid_class.astype(jnp.float32) * 0.25
-    fields = populations
+    sides = (("gz", 3), ("gx", 1), ("gy", 2))
+    gray = solid_class.astype(jnp.float32) * 0.25
+    wide = with_halo(jnp.concatenate([populations, gray[None]]), sides, STEPS)
+    fields = [wide[i] for i in range(19)]
+    gray_fraction = wide[19]
     for repeat in range(STEPS):
+        reach = STEPS - repeat
         density, flow = moments(fields)
-        rim_field = with_halo(flow, (("gx", 1), ("gy", 2), ("gz", 3)), 1)
-        lines = rim_field.reshape(3, -1, size_z + 2)
-        along = jnp.einsum("nz,dkz->dnk", tables[2], lines, precision=lax.Precision.HIGHEST)
+        near = flow
+        for d, size in enumerate((size_x, size_y, size_z)):
+            near = lax.slice_in_dim(near, reach - 1, reach + 1 + size, axis=d + 1)
+        lines = near.reshape(3, -1, size_z + 2)
+        along = jnp.einsum("nz,dkz->dnk", tables[2], lines, precision=lax.Precision.HIGH)
         sampled = jnp.sum(along * across[None], axis=2).reshape(3, slots, rows_block)
         sampled = jnp.moveaxis(sampled, 0, 1)
         drag_force = jnp.where(
@@ -192,13 +196,13 @@
         pushed = -jnp.moveaxis(drag_force, 1, 0).reshape(3, -1)
         ghosts = jnp.einsum(
             "dnk,nz->dkz", pushed[:, :, None] * across[None], tables[2],
-            precision=lax.Precision.HIGHEST,
+            precision=lax.Precision.HIGH,
         )
         ghosts = ghosts.reshape(3, size_x + 2, size_y + 2, size_z + 2)
-        widened = with_halo(ghosts, (("gx", 1), ("gy", 2), ("gz", 3)), 1)
-        cell_force = fold_ghost(fold_ghost(fold_ghost(widened, 1), 2), 3)
+        cell_force = spread_sums(ghosts, sides, reach)
         post_list = collide(fields, density, flow, cell_force, gray_fraction)
-        fields = jnp.stack(propagate_by_axis(post_list))
+        fields = propagate(post_list)
+        gray_fraction = gray_fraction[1:-1, 1:-1, 1:-1]
     density, flow = moments(fields)
     fluid_velocity = flow / speed_unit
     particle_velocity = jnp.where(live_rows[:, None, :], velocity / speed_unit, 0.0)

time: 154 us -> 116 us (0.75)
  starting transfers between devices: 61.5 us -> 22.1 us
  other arithmetic: 14.3 us -> 23.9 us
  matrix products: 12.9 us -> 9.07 us
  waiting for transfers between devices: 55.2 us -> 53.4 us
  local copies, waits for them, and re-layouts: 7.11 us -> 5.44 us
    ppermute x36 -> x15, starting transfers between devices: 48.1 us -> 17 us  [the longest x6 10.9 us: swap(): lax.ppermute(backward, axis, [((i + 1) % count, i) for i in range(count)])]
    all_to_all x2 -> x0, starting transfers between devices: 8.33 us -> none  [the longest x1 5.1 us: per_device(): lax.all_to_all(send_cells, 'gx', split_axis=0, concat_axis=0, tiled=True)]
    all_to_all x2 -> x0, waiting for transfers between devices: 5.46 us -> none  [the longest x1 5.46 us: per_device(): lax.all_to_all(send_cells, 'gx', split_axis=0, concat_axis=0, tiled=True)]
    mul x0 -> x4, other arithmetic: none -> 4.55 us  [collide(): equilibrium = weights[i] * baseline]
    ppermute x36 -> x15, waiting for transfers between devices: 49.8 us -> 53.4 us  [the longest x6 19.2 us: swap(): lax.ppermute(backward, axis, [((i + 1) % count, i) for i in range(count)])]
    concatenate x13 -> x4, other arithmetic: 2.65 us -> 5.4 us  [the longest x2 3.43 us: with_halo(): cells = jnp.concatenate([before, cells, after], axis=dim)]
    dot_general x2, matrix products: 6.32 us -> 3.8 us  [per_device(): jnp.einsum('dnk,nz->dkz', pushed[:, :, None] * across[None], tables[2], p...]
    another operation x3 -> x4, other arithmetic: 0.26 us -> 2.71 us  [moments(): return (density, jnp.stack(components))]
  transfers between devices with their start and end apart: 39 -> 16, of which waited for: 30 -> 14; matrix products, arithmetic and copies ran while one was open for 8% -> 11% of each run, Pallas kernels for 0% -> 0%
where the time goes in v2:
time: 116 us
  waiting for transfers between devices  53.4 us (46%)
  other arithmetic  23.9 us (21%)
  starting transfers between devices  22.1 us (19%)
  matrix products  9.07 us (8%)
  local copies, waits for them, and re-layouts  5.44 us (5%)
  between operations  1.63 us (1%)
    ppermute x6, waiting for transfers between devices, swap(): lax.ppermute(backward, axis, [((i + 1) % count, i) for i in range(count)])  19.2 us
    ppermute x6, waiting for transfers between devices, swap(): lax.ppermute(onward, axis, [(i, (i + 1) % count) for i in range(count)])  18 us
    ppermute x3, waiting for transfers between devices, swap(): both = lax.ppermute(jnp.stack([onward, backward]), axis, [(0, 1), (1, 0)])  16.2 us
    ppermute x6, starting transfers between devices, swap(): lax.ppermute(backward, axis, [((i + 1) % count, i) for i in range(count)])  10.9 us
    dot_general x2, matrix products, per_device(): jnp.einsum('nz,dkz->dnk', tables[2], lines, precision=lax.Precision.HIGH)  5.27 us
    all_to_all x1, starting transfers between devices, per_device(): lax.all_to_all(send_floats, 'gx', split_axis=0, concat_axis=0, tiled=True)  5.09 us
    ppermute x3, starting transfers between devices, swap(): both = lax.ppermute(jnp.stack([onward, backward]), axis, [(0, 1), (1, 0)])  4.6 us
    mul x4, other arithmetic, collide(): equilibrium = weights[i] * baseline  4.55 us
  transfers between devices with their start and end apart: 16, of which 14 were waited for; matrix products, arithmetic and copies ran while one was open for 11% of the time, Pallas kernels for 0%

profile of v2, /device:TPU:0, one launch (start us, length us, event | category | flops | bytes accessed | tf_op | source)
XLA Modules:
  0.0 115.6 jit_solution(8959427455303428643)
XLA Ops:
  0.6 0.7 multiply_bitcast_fusion
  1.4 1.2 %slice_maximum_fusion = (f32[20,4,8,2]{3,2,1,0:T(8,128)S(1)}, f32[20,4,8,2]{3,2,1,0:T(8,128)S(1)}) fusion(f32[1,4,8,128]{3,2,1,0:T(8,128)S(1)} %multiply_bitcast_fusion, f32[19,4,8,128]{3,2,1,0:T(8,128)} %param.8), kind=kLoop, calls=%fused_computation.58 | loop fusion | flops 2560 | bytes 337920 | tf_op jit(solution)/shard_map/concatenate | solution.py:179
  2.6 2.5 %collective-permute-start.1 = (f32[20,4,8,2]{3,2,1,0:T(8,128)S(1)}, f32[20,4,8,2]{3,2,1,0:T(8,128)S(1)}, u32[]{:S(2)}, u32[]{:S(2)}) collective-permute-start(f32[20,4,8,2]{3,2,1,0:T(8,128)S(1)} %get-tuple-element.102), channel_id=1, source_target_pairs={{1,0},{2,1},{3,2},{0,3},{5,4},{6,5},{7,6},{4,7},{9,8},{10,9},{11,1... | collective-permute-start | bytes 15368 | tf_op jit(solution)/shard_map/ppermute | solution.py:43
  5.1 0.7 fusion.357
  5.8 0.8 select_reduce_fusion.1
  6.7 0.7 multiply_add_fusion
  7.5 0.8 copy.17
  8.3 0.8 copy.16
  9.1 0.8 select_convert_fusion
  9.8 0.7 pad_maximum_fusion.13
  10.6 0.6 gather_fusion
  11.2 1.9 %collective-permute-done.1 = f32[20,4,8,2]{3,2,1,0:T(8,128)S(1)} collective-permute-done((f32[20,4,8,2]{3,2,1,0:T(8,128)S(1)}, f32[20,4,8,2]{3,2,1,0:T(8,128)S(1)}, u32[]{:S(2)}, u32[]{:S(2)}) %collective-permute-start.1) | collective-permute-done | bytes 5152 | tf_op jit(solution)/shard_map/ppermute | solution.py:43
  13.1 1.1 collective-permute-done
  14.2 1.4 %pad_maximum_fusion.1 = f32[20,4,8,132]{3,2,1,0:T(8,128)S(1)} fusion(f32[20,4,8,2]{3,2,1,0:T(8,128)S(1)} %collective-permute-done.1, f32[1,4,8,128]{3,2,1,0:T(8,128)S(1)} %multiply_bitcast_fusion, f32[19,4,8,128]{3,2,1,0:T(8,128)} %param.8, f32[20,4,8,2]{3,2,1,0:T(8,128)S(1)} %collective-permute-done), kind=kLoop, calls=%fused_computation.44 | loop fusion | flops 253440 | bytes 675840 | tf_op jit(solution)/shard_map/concatenate | solution.py:53
  15.7 3.7 %collective-permute-start.3 = (f32[20,2,8,132]{3,2,1,0:T(8,128)S(1)}, f32[20,2,8,132]{3,2,1,0:T(8,128)S(1)}, u32[]{:S(2)}, u32[]{:S(2)}) collective-permute-start(f32[20,2,8,132]{3,2,1,0:T(8,128)S(1)} %get-tuple-element.80), channel_id=1, source_target_pairs={{8,0},{16,8},{24,16},{0,24},{9,1},{17,9},{25,17},{1,25},{10,2},{18... | collective-permute-start | bytes 506888 | tf_op jit(solution)/shard_map/ppermute | solution.py:43
  19.3 0.8 select_select_fusion
  20.1 5.1 %all-to-all-start = ((f32[32,8,128]{2,1,0:T(8,128)}), f32[32,8,128]{2,1,0:T(8,128)S(1)}, u32[]{:S(2)}, u32[]{:S(2)}) async-start(f32[32,8,128]{2,1,0:T(8,128)} %select_select_fusion), calls=%async_computation | async-start | bytes 262144 | tf_op jit(solution)/shard_map/all_to_all | solution.py:156
  25.2 2.3 %collective-permute-done.3 = f32[20,2,8,132]{3,2,1,0:T(8,128)S(1)} collective-permute-done((f32[20,2,8,132]{3,2,1,0:T(8,128)S(1)}, f32[20,2,8,132]{3,2,1,0:T(8,128)S(1)}, u32[]{:S(2)}, u32[]{:S(2)}) %collective-permute-start.3) | collective-permute-done | bytes 168992 | tf_op jit(solution)/shard_map/ppermute | solution.py:43
  27.5 7.3 %collective-permute-done.2 = f32[20,2,8,132]{3,2,1,0:T(8,128)S(1)} collective-permute-done((f32[20,2,8,132]{3,2,1,0:T(8,128)S(1)}, f32[20,2,8,132]{3,2,1,0:T(8,128)S(1)}, u32[]{:S(2)}, u32[]{:S(2)}) %collective-permute-start.2) | collective-permute-done | bytes 168992 | tf_op jit(solution)/shard_map/ppermute | solution.py:42
  34.8 0.6 maximum_bitcast_fusion
  35.5 1.2 %pad_maximum_fusion.2 = f32[2,20,8,2,132]{4,3,2,1,0:T(2,128)} fusion(f32[1,20,8,2,132]{4,3,2,1,0:T(2,128)S(1)} %get-tuple-element.76, f32[1,20,8,2,132]{4,3,2,1,0:T(2,128)S(1)} %get-tuple-element.75), kind=kLoop, calls=%fused_computation.45 | loop fusion | flops 84480 | bytes 675840 | tf_op jit(solution)/shard_map/stack | solution.py:39
  36.7 1.5 %collective-permute-start.4 = (f32[2,20,8,2,132]{4,3,2,1,0:T(2,128)}, f32[2,20,8,2,132]{4,3,2,1,0:T(2,128)S(1)}, u32[]{:S(2)}, u32[]{:S(2)}) collective-permute-start(f32[2,20,8,2,132]{4,3,2,1,0:T(2,128)} %pad_maximum_fusion.2), channel_id=1, source_target_pairs={{0,4},{4,0},{1,5},{5,1},{2,6},{6,2},{3,7},{7,3},{8,12},{12,8},{9,1... | collective-permute-start | bytes 1013768 | tf_op jit(solution)/shard_map/ppermute | solution.py:39
  38.5 0.1 broadcast_multiply_fusion
  38.7 1.2 %mul.1044 = f32[4096,60]{0,1:T(8,128)} reshape(f32[4096,6,10]{0,2,1:T(8,128)S(1)} %broadcast_multiply_fusion) | data formatting | bytes 1966080 | tf_op jit(solution)/shard_map/mul | solution.py:176
  39.9 10.8 %collective-permute-done.4 = f32[2,20,8,2,132]{4,3,2,1,0:T(2,128)S(1)} collective-permute-done((f32[2,20,8,2,132]{4,3,2,1,0:T(2,128)}, f32[2,20,8,2,132]{4,3,2,1,0:T(2,128)S(1)}, u32[]{:S(2)}, u32[]{:S(2)}) %collective-permute-start.4) | collective-permute-done | bytes 337952 | tf_op jit(solution)/shard_map/ppermute | solution.py:39
  50.7 0.2 slice_bitcast_fusion.1
  51.0 2.0 %pad_maximum_fusion = f32[20,8,12,132]{3,2,1,0:T(8,128)S(1)} fusion(f32[20,8,2,132]{3,2,1,0:T(2,128)S(1)} %get-tuple-element.78, f32[20,2,8,132]{3,2,1,0:T(8,128)} %copy-done.2, f32[20,4,8,2]{3,2,1,0:T(8,128)S(1)} %collective-permute-done.1, f32[1,4,8,128]{3,2,1,0:T(8,128)S(1)} %multiply_bitcast_fusion, f32[19,4,8,128]{3,2,1,0:T(8,128)S(1)} %copy-done, ...), kind=kLoop, calls=%fused_computation.9 | loop fusion | flops 1774080 | bytes 2027520 | tf_op jit(solution)/shard_map/concatenate | solution.py:53
  53.0 0.8 add_add_fusion
  53.8 1.0 slice_bitcast_fusion.10
  54.8 1.0 slice_bitcast_fusion.16
  55.8 0.1 pad_maximum_fusion.9
  56.0 0.7 reshape.363
  56.7 3.3 %fusion.14 = f32[3,4096]{1,0:T(4,128)S(1)} fusion(f32[4096,60]{0,1:T(8,128)} %mul.1044, f32[3,60,130]{2,1,0:T(8,128)} %reshape.363, f32[4096]{0:T(1024)S(1)} %bitcast.334, s32[4096]{0:T(1024)S(1)} %get-tuple-element.178, f32[4096]{0:T(1024)S(1)} %broadcast_subtract_fusion.4, s32[4096]{0:T(1024)S(1)} %get-tuple-element.177), kind=kOutput, calls=%fused_computation.21 | convolution fusion | flops 579203072 | bytes 1191328 | tf_op jit(solution)/shard_map/nz,dkz->dnk/dot_general | solution.py:189
  60.2 1.9 %fusion.4 = f32[3,60,130]{2,1,0:T(8,128)S(1)} fusion(f32[3,4096]{1,0:T(4,128)S(1)} %negate_bitcast_fusion.1, f32[4096,60]{0,1:T(8,128)S(1)} %copy-done.6, f32[4096]{0:T(1024)S(1)} %bitcast.335, s32[4096]{0:T(1024)S(1)} %get-tuple-element.178, f32[4096]{0:T(1024)S(1)} %broadcast_subtract_fusion.4, s32[4096]{0:T(1024)S(1)} %get-tuple-element.177), kind=kOutput, calls=%fused_computation.7 | convolution fusion | flops 578478080 | bytes 1191328 | tf_op jit(solution)/shard_map/dnk,nz->dkz/dot_general | solution.py:197
  62.1 0.1 fusion.409
  62.2 0.2 collective-permute-start.6
  62.5 0.3 collective-permute-start.5
  62.8 2.4 %collective-permute-done.6 = f32[3,6,10,3]{3,2,1,0:T(8,128)S(1)} collective-permute-done((f32[3,6,10,3]{3,2,1,0:T(8,128)S(1)}, f32[3,6,10,3]{3,2,1,0:T(8,128)S(1)}, u32[]{:S(2)}, u32[]{:S(2)}) %collective-permute-start.6) | collective-permute-done | bytes 2192 | tf_op jit(solution)/shard_map/ppermute | solution.py:43
  65.1 4.6 %collective-permute-done.5 = f32[3,6,10,3]{3,2,1,0:T(8,128)S(1)} collective-permute-done((f32[3,6,10,3]{3,2,1,0:T(8,128)S(1)}, f32[3,6,10,3]{3,2,1,0:T(8,128)S(1)}, u32[]{:S(2)}, u32[]{:S(2)}) %collective-permute-start.5) | collective-permute-done | bytes 2192 | tf_op jit(solution)/shard_map/ppermute | solution.py:42
  69.8 0.2 pad_add_fusion.5
  70.0 1.4 %collective-permute-start.8 = (f32[3,3,10,132]{3,2,1,0:T(8,128)S(1)}, f32[3,3,10,132]{3,2,1,0:T(8,128)S(1)}, u32[]{:S(2)}, u32[]{:S(2)}) collective-permute-start(f32[3,3,10,132]{3,2,1,0:T(8,128)S(1)} %get-tuple-element.128), channel_id=1, source_target_pairs={{8,0},{16,8},{24,16},{0,24},{9,1},{17,9},{25,17},{1,25},{10,2},{18... | collective-permute-start | bytes 142568 | tf_op jit(solution)/shard_map/ppermute | solution.py:43
  71.4 0.7 collective-permute-start.7
  72.1 0.3 fusion.49
  72.4 6.7 %collective-permute-done.8 = f32[3,3,10,132]{3,2,1,0:T(8,128)S(1)} collective-permute-done((f32[3,3,10,132]{3,2,1,0:T(8,128)S(1)}, f32[3,3,10,132]{3,2,1,0:T(8,128)S(1)}, u32[]{:S(2)}, u32[]{:S(2)}) %collective-permute-start.8) | collective-permute-done | bytes 47552 | tf_op jit(solution)/shard_map/ppermute | solution.py:43
  79.2 1.6 %collective-permute-start.9 = (f32[2,3,8,3,132]{4,3,2,1,0:T(4,128)S(1)}, f32[2,3,8,3,132]{4,3,2,1,0:T(4,128)S(1)}, u32[]{:S(2)}, u32[]{:S(2)}) collective-permute-start(f32[2,3,8,3,132]{4,3,2,1,0:T(4,128)S(1)} %pad_maximum_fusion.11), channel_id=1, source_target_pairs={{0,4},{4,0},{1,5},{5,1},{2,6},{6,2},{3,7},{7,3},{8,12},{12,8},{9,1... | collective-permute-start | bytes 228104 | tf_op jit(solution)/shard_map/ppermute | solution.py:39
  80.8 0.5 fusion.79
  81.5 3.5 %collective-permute-done.9 = f32[2,3,8,3,132]{4,3,2,1,0:T(4,128)S(1)} collective-permute-done((f32[2,3,8,3,132]{4,3,2,1,0:T(4,128)S(1)}, f32[2,3,8,3,132]{4,3,2,1,0:T(4,128)S(1)}, u32[]{:S(2)}, u32[]{:S(2)}) %collective-permute-start.9) | collective-permute-done | bytes 76064 | tf_op jit(solution)/shard_map/ppermute | solution.py:39
  85.4 3.4 %fusion.83 = (f32[6,10,130]{2,1,0:T(8,128)}, f32[6,10,130]{2,1,0:T(8,128)S(1)}, f32[6,10,130]{2,1,0:T(8,128)S(1)}, f32[6,10,130]{2,1,0:T(8,128)S(1)}, f32[6,10,1...) fusion(f32[8,12,132]{2,1,0:T(8,128)S(1)} %get-tuple-element.74,, ...), kind=kLoop, calls=%fused_computation.184 | loop fusion | flops 1817400 | bytes 4586400 | tf_op jit(solution)/shard_map/mul | solution.py:106
  88.9 1.9 %fusion.17 = f32[3,4096]{1,0:T(4,128)S(1)} fusion(f32[4096,60]{0,1:T(8,128)S(1)} %copy-done.7, f32[4096]{0:T(1024)S(1)} %bitcast.336, s32[4096]{0:T(1024)S(1)} %copy-done.36, f32[4096]{0:T(1024)S(1)} %copy-done.39, s32[4096]{0:T(1024)S(1)} %copy-done.34, f32[1,60,130]{2,1,0:T(8,128)S(1)} %stack.66, f32[1,60,130]{2,1,0:T(8,128)S(1)} %stack.65, ...), kind=kOutput, calls=%fused_computation.22 | convolution fusion | flops 579249856 | bytes 1191328 | tf_op jit(solution)/shard_map/nz,dkz->dnk/dot_general | solution.py:189
  91.0 1.9 %fusion.2 = f32[3,60,130]{2,1,0:T(8,128)S(1)} fusion(f32[3,4096]{1,0:T(4,128)S(1)} %get-tuple-element.132, f32[4096,60]{0,1:T(8,128)S(1)} %copy-done.7, f32[4096]{0:T(1024)S(1)} %bitcast.337, s32[4096]{0:T(1024)S(1)} %copy-done.37, f32[4096]{0:T(1024)S(1)} %copy-done.40, s32[4096]{0:T(1024)S(1)} %copy-done.34), kind=kOutput, calls=%fused_computation.5 | convolution fusion | flops 578478080 | bytes 1191328 | tf_op jit(solution)/shard_map/dnk,nz->dkz/dot_general | solution.py:197
  93.0 0.5 collective-permute-start.10
  93.5 3.6 %collective-permute-done.11 = f32[3,6,10,2]{3,2,1,0:T(8,128)S(1)} collective-permute-done((f32[3,6,10,2]{3,2,1,0:T(8,128)S(1)}, f32[3,6,10,2]{3,2,1,0:T(8,128)S(1)}, u32[]{:S(2)}, u32[]{:S(2)}) %collective-permute-start.11) | collective-permute-done | bytes 1472 | tf_op jit(solution)/shard_map/ppermute | solution.py:43
  97.1 0.6 collective-permute-done.10
  97.7 3.0 %collective-permute-start.13 = (f32[3,2,10,130]{3,2,1,0:T(8,128)S(1)}, f32[3,2,10,130]{3,2,1,0:T(8,128)S(1)}, u32[]{:S(2)}, u32[]{:S(2)}) collective-permute-start(f32[3,2,10,130]{3,2,1,0:T(8,128)S(1)} %get-tuple-element.124), channel_id=1, source_target_pairs={{8,0},{16,8},{24,16},{0,24},{9,1},{17,9},{25,17},{1,25},{10,2},{18... | collective-permute-start | bytes 93608 | tf_op jit(solution)/shard_map/ppermute | solution.py:43
  100.9 2.4 %collective-permute-done.13 = f32[3,2,10,130]{3,2,1,0:T(8,128)S(1)} collective-permute-done((f32[3,2,10,130]{3,2,1,0:T(8,128)S(1)}, f32[3,2,10,130]{3,2,1,0:T(8,128)S(1)}, u32[]{:S(2)}, u32[]{:S(2)}) %collective-permute-start.13) | collective-permute-done | bytes 31232 | tf_op jit(solution)/shard_map/ppermute | solution.py:43
  103.3 4.4 %collective-permute-done.12 = f32[3,2,10,130]{3,2,1,0:T(8,128)S(1)} collective-permute-done((f32[3,2,10,130]{3,2,1,0:T(8,128)S(1)}, f32[3,2,10,130]{3,2,1,0:T(8,128)S(1)}, u32[]{:S(2)}, u32[]{:S(2)}) %collective-permute-start.12) | collective-permute-done | bytes 31232 | tf_op jit(solution)/shard_map/ppermute | solution.py:42
  107.8 1.6 %collective-permute-start.14 = (f32[2,3,6,2,130]{4,3,2,1,0:T(2,128)S(1)}, f32[2,3,6,2,130]{4,3,2,1,0:T(2,128)S(1)}, u32[]{:S(2)}, u32[]{:S(2)}) collective-permute-start(f32[2,3,6,2,130]{4,3,2,1,0:T(2,128)S(1)} %pad_maximum_fusion.12), channel_id=1, source_target_pairs={{0,4},{4,0},{1,5},{5,1},{2,6},{6,2},{3,7},{7,3},{8,12},{12,8},{9,1... | collective-permute-start | bytes 112328 | tf_op jit(solution)/shard_map/ppermute | solution.py:39
  109.4 0.4 fusion.115
  109.8 0.6 copy.18
  110.4 1.9 %collective-permute-done.14 = f32[2,3,6,2,130]{4,3,2,1,0:T(2,128)S(1)} collective-permute-done((f32[2,3,6,2,130]{4,3,2,1,0:T(2,128)S(1)}, f32[2,3,6,2,130]{4,3,2,1,0:T(2,128)S(1)}, u32[]{:S(2)}, u32[]{:S(2)}) %collective-permute-start.14) | collective-permute-done | bytes 37472 | tf_op jit(solution)/shard_map/ppermute | solution.py:39
  112.4 1.3 %fusion.346 = (f32[1,4,8,128]{3,2,1,0:T(8,128)S(1)}, f32[4,8,128]{2,1,0:T(8,128)S(1)}, f32[4,8,128]{2,1,0:T(8,128)S(1)}, f32[4,8,128]{2,1,0:T(8,128)S(1)}, f32[4...) fusion(f32[6,10,130]{2,1,0:T(8,128)S(1)} %get-tuple-element.21,, ...), kind=kLoop, calls=%fused_computation.625 | loop fusion | flops 417792 | bytes 1261568 | tf_op jit(solution)/shard_map/stack | solution.py:94
  113.7 0.2 fusion.285
  113.9 1.0 fusion.245
  114.9 0.6 maximum_multiply_fusion
  (132 shorter events, 1.7 us)
Async XLA Ops:
  2.6 32.2 %copy-start = (f32[19,4,8,128]{3,2,1,0:T(8,128)S(1)}, f32[19,4,8,128]{3,2,1,0:T(8,128)}, u32[]{:S(2)}) copy-start(f32[19,4,8,128]{3,2,1,0:T(8,128)} %param.8) | copy-start | bytes 933892
  2.6 10.5 %collective-permute-start.1 = (f32[20,4,8,2]{3,2,1,0:T(8,128)S(1)}, f32[20,4,8,2]{3,2,1,0:T(8,128)S(1)}, u32[]{:S(2)}, u32[]{:S(2)}) collective-permute-start(f32[20,4,8,2]{3,2,1,0:T(8,128)S(1)} %get-tuple-element.102), channel_id=1, source_target_pairs={{1,0},{2,1},{3,2},{0,3},{5,4},{6,5},{7,6},{4,7},{9,8},{10,9},{11,1... | collective-permute-start | bytes 15368 | tf_op jit(solution)/shard_map/ppermute | solution.py:43
  5.1 9.1 %collective-permute-start = (f32[20,4,8,2]{3,2,1,0:T(8,128)S(1)}, f32[20,4,8,2]{3,2,1,0:T(8,128)S(1)}, u32[]{:S(2)}, u32[]{:S(2)}) collective-permute-start(f32[20,4,8,2]{3,2,1,0:T(8,128)S(1)} %get-tuple-element.101), channel_id=1, source_target_pairs={{0,1},{1,2},{2,3},{3,0},{4,5},{5,6},{6,7},{7,4},{8,9},{9,10},{10,1... | collective-permute-start | bytes 15368 | tf_op jit(solution)/shard_map/ppermute | solution.py:42
  14.2 21.3 %copy-start.1 = (f32[20,4,8,2]{3,2,1,0:T(8,128)}, f32[20,4,8,2]{3,2,1,0:T(8,128)S(1)}, u32[]{:S(2)}) copy-start(f32[20,4,8,2]{3,2,1,0:T(8,128)S(1)} %collective-permute-done) | copy-start | bytes 15364
  15.7 11.8 %collective-permute-start.3 = (f32[20,2,8,132]{3,2,1,0:T(8,128)S(1)}, f32[20,2,8,132]{3,2,1,0:T(8,128)S(1)}, u32[]{:S(2)}, u32[]{:S(2)}) collective-permute-start(f32[20,2,8,132]{3,2,1,0:T(8,128)S(1)} %get-tuple-element.80), channel_id=1, source_target_pairs={{8,0},{16,8},{24,16},{0,24},{9,1},{17,9},{25,17},{1,25},{10,2},{18... | collective-permute-start | bytes 506888 | tf_op jit(solution)/shard_map/ppermute | solution.py:43
  19.3 15.5 %collective-permute-start.2 = (f32[20,2,8,132]{3,2,1,0:T(8,128)S(1)}, f32[20,2,8,132]{3,2,1,0:T(8,128)S(1)}, u32[]{:S(2)}, u32[]{:S(2)}) collective-permute-start(f32[20,2,8,132]{3,2,1,0:T(8,128)S(1)} %get-tuple-element.79), channel_id=1, source_target_pairs={{0,8},{8,16},{16,24},{24,0},{1,9},{9,17},{17,25},{25,1},{2,10},{10... | collective-permute-start | bytes 506888 | tf_op jit(solution)/shard_map/ppermute | solution.py:42
  20.1 18.0 %all-to-all-start = ((f32[32,8,128]{2,1,0:T(8,128)}), f32[32,8,128]{2,1,0:T(8,128)S(1)}, u32[]{:S(2)}, u32[]{:S(2)}) async-start(f32[32,8,128]{2,1,0:T(8,128)} %select_select_fusion), calls=%async_computation | async-start | bytes 262144 | tf_op jit(solution)/shard_map/all_to_all | solution.py:156
  27.5 11.0 %copy-start.2 = (f32[20,2,8,132]{3,2,1,0:T(8,128)}, f32[20,2,8,132]{3,2,1,0:T(8,128)S(1)}, u32[]{:S(2)}) copy-start(f32[20,2,8,132]{3,2,1,0:T(8,128)S(1)} %collective-permute-done.3) | copy-start | bytes 506884
  34.8 3.7 %copy-start.3 = (f32[20,2,8,132]{3,2,1,0:T(8,128)}, f32[20,2,8,132]{3,2,1,0:T(8,128)S(1)}, u32[]{:S(2)}) copy-start(f32[20,2,8,132]{3,2,1,0:T(8,128)S(1)} %collective-permute-done.2) | copy-start | bytes 506884
  36.7 14.1 %collective-permute-start.4 = (f32[2,20,8,2,132]{4,3,2,1,0:T(2,128)}, f32[2,20,8,2,132]{4,3,2,1,0:T(2,128)S(1)}, u32[]{:S(2)}, u32[]{:S(2)}) collective-permute-start(f32[2,20,8,2,132]{4,3,2,1,0:T(2,128)} %pad_maximum_fusion.2), channel_id=1, source_target_pairs={{0,4},{4,0},{1,5},{5,1},{2,6},{6,2},{3,7},{7,3},{8,12},{12,8},{9,1... | collective-permute-start | bytes 1013768 | tf_op jit(solution)/shard_map/ppermute | solution.py:39
  38.2 21.9 %copy-start.4 = (f32[32,8,128]{2,1,0:T(8,128)}, f32[32,8,128]{2,1,0:T(8,128)S(1)}, u32[]{:S(2)}) copy-start(f32[32,8,128]{2,1,0:T(8,128)S(1)} %all-to-all-done) | copy-start | bytes 393220
  38.2 21.8 %copy-start.27 = (f32[32,1,128]{2,1,0:T(1,128)}, f32[32,1,128]{2,1,0:T(1,128)S(1)}, u32[]{:S(2)}) copy-start(f32[32,1,128]{2,1,0:T(1,128)S(1)} %get-tuple-element.167) | copy-start | bytes 49156
  38.2 21.9 %copy-start.29 = (f32[32,1,128]{2,1,0:T(1,128)}, f32[32,1,128]{2,1,0:T(1,128)S(1)}, u32[]{:S(2)}) copy-start(f32[32,1,128]{2,1,0:T(1,128)S(1)} %get-tuple-element.171) | copy-start | bytes 49156
  38.4 21.7 %copy-start.33 = (s32[4096]{0:T(1024)}, s32[4096]{0:T(1024)S(1)}, u32[]{:S(2)}) copy-start(s32[4096]{0:T(1024)S(1)} %get-tuple-element.177) | copy-start | bytes 49156
  38.4 21.7 %copy-start.35 = (s32[4096]{0:T(1024)}, s32[4096]{0:T(1024)S(1)}, u32[]{:S(2)}) copy-start(s32[4096]{0:T(1024)S(1)} %get-tuple-element.178) | copy-start | bytes 49156
  39.9 20.2 %copy-start.31 = (pred[32,1,128]{2,0,1:T(8,128)(4,1)}, pred[32,1,128]{2,0,1:T(8,128)(4,1)S(1)}, u32[]{:S(2)}) copy-start(pred[32,1,128]{2,0,1:T(8,128)(4,1)S(1)} %copy.21) | copy-start | bytes 12292
  39.9 20.2 %copy-start.38 = (f32[4096]{0:T(1024)}, f32[4096]{0:T(1024)S(1)}, u32[]{:S(2)}) copy-start(f32[4096]{0:T(1024)S(1)} %broadcast_subtract_fusion.4) | copy-start | bytes 49156
  56.7 3.5 %copy-start.6 = (f32[4096,60]{0,1:T(8,128)S(1)}, f32[4096,60]{0,1:T(8,128)}, u32[]{:S(2)}) copy-start(f32[4096,60]{0,1:T(8,128)} %mul.1044) | copy-start | bytes 2949124
  62.2 2.9 %collective-permute-start.6 = (f32[3,6,10,3]{3,2,1,0:T(8,128)S(1)}, f32[3,6,10,3]{3,2,1,0:T(8,128)S(1)}, u32[]{:S(2)}, u32[]{:S(2)}) collective-permute-start(f32[3,6,10,3]{3,2,1,0:T(8,128)S(1)} %get-tuple-element.130), channel_id=1, source_target_pairs={{1,0},{2,1},{3,2},{0,3},{5,4},{6,5},{7,6},{4,7},{9,8},{10,9},{11,1... | collective-permute-start | bytes 6488 | tf_op jit(solution)/shard_map/ppermute | solution.py:43
  62.5 7.3 %collective-permute-start.5 = (f32[3,6,10,3]{3,2,1,0:T(8,128)S(1)}, f32[3,6,10,3]{3,2,1,0:T(8,128)S(1)}, u32[]{:S(2)}, u32[]{:S(2)}) collective-permute-start(f32[3,6,10,3]{3,2,1,0:T(8,128)S(1)} %get-tuple-element.129), channel_id=1, source_target_pairs={{0,1},{1,2},{2,3},{3,0},{4,5},{5,6},{6,7},{7,4},{8,9},{9,10},{10,1... | collective-permute-start | bytes 6488 | tf_op jit(solution)/shard_map/ppermute | solution.py:42
  70.0 9.1 %collective-permute-start.8 = (f32[3,3,10,132]{3,2,1,0:T(8,128)S(1)}, f32[3,3,10,132]{3,2,1,0:T(8,128)S(1)}, u32[]{:S(2)}, u32[]{:S(2)}) collective-permute-start(f32[3,3,10,132]{3,2,1,0:T(8,128)S(1)} %get-tuple-element.128), channel_id=1, source_target_pairs={{8,0},{16,8},{24,16},{0,24},{9,1},{17,9},{25,17},{1,25},{10,2},{18... | collective-permute-start | bytes 142568 | tf_op jit(solution)/shard_map/ppermute | solution.py:43
  71.4 7.7 %collective-permute-start.7 = (f32[3,3,10,132]{3,2,1,0:T(8,128)S(1)}, f32[3,3,10,132]{3,2,1,0:T(8,128)S(1)}, u32[]{:S(2)}, u32[]{:S(2)}) collective-permute-start(f32[3,3,10,132]{3,2,1,0:T(8,128)S(1)} %get-tuple-element.127), channel_id=1, source_target_pairs={{0,8},{8,16},{16,24},{24,0},{1,9},{9,17},{17,25},{25,1},{2,10},{10... | collective-permute-start | bytes 142568 | tf_op jit(solution)/shard_map/ppermute | solution.py:42
  79.2 5.8 %collective-permute-start.9 = (f32[2,3,8,3,132]{4,3,2,1,0:T(4,128)S(1)}, f32[2,3,8,3,132]{4,3,2,1,0:T(4,128)S(1)}, u32[]{:S(2)}, u32[]{:S(2)}) collective-permute-start(f32[2,3,8,3,132]{4,3,2,1,0:T(4,128)S(1)} %pad_maximum_fusion.11), channel_id=1, source_target_pairs={{0,4},{4,0},{1,5},{5,1},{2,6},{6,2},{3,7},{7,3},{8,12},{12,8},{9,1... | collective-permute-start | bytes 228104 | tf_op jit(solution)/shard_map/ppermute | solution.py:39
  81.3 3.9 %copy-start.8 = (f32[8,12,132]{2,1,0:T(8,128)S(1)}, f32[8,12,132]{2,1,0:T(8,128)}, u32[]{:S(2)}) copy-start(f32[8,12,132]{2,1,0:T(8,128)} %get-tuple-element.62) | copy-start | bytes 152068
  81.3 3.9 %copy-start.9 = (f32[8,12,132]{2,1,0:T(8,128)S(1)}, f32[8,12,132]{2,1,0:T(8,128)}, u32[]{:S(2)}) copy-start(f32[8,12,132]{2,1,0:T(8,128)} %get-tuple-element.64) | copy-start | bytes 152068
  81.3 3.9 %copy-start.10 = (f32[8,12,132]{2,1,0:T(8,128)S(1)}, f32[8,12,132]{2,1,0:T(8,128)}, u32[]{:S(2)}) copy-start(f32[8,12,132]{2,1,0:T(8,128)} %get-tuple-element.65) | copy-start | bytes 152068
  81.3 3.9 %copy-start.11 = (f32[8,12,132]{2,1,0:T(8,128)S(1)}, f32[8,12,132]{2,1,0:T(8,128)}, u32[]{:S(2)}) copy-start(f32[8,12,132]{2,1,0:T(8,128)} %get-tuple-element.66) | copy-start | bytes 152068
  81.3 3.9 %copy-start.12 = (f32[8,12,132]{2,1,0:T(8,128)S(1)}, f32[8,12,132]{2,1,0:T(8,128)}, u32[]{:S(2)}) copy-start(f32[8,12,132]{2,1,0:T(8,128)} %get-tuple-element.67) | copy-start | bytes 152068
  81.3 3.9 %copy-start.13 = (f32[8,12,132]{2,1,0:T(8,128)S(1)}, f32[8,12,132]{2,1,0:T(8,128)}, u32[]{:S(2)}) copy-start(f32[8,12,132]{2,1,0:T(8,128)} %get-tuple-element.68) | copy-start | bytes 152068
  81.4 3.9 %copy-start.14 = (f32[8,12,132]{2,1,0:T(8,128)S(1)}, f32[8,12,132]{2,1,0:T(8,128)}, u32[]{:S(2)}) copy-start(f32[8,12,132]{2,1,0:T(8,128)} %get-tuple-element.69) | copy-start | bytes 152068
  81.4 3.9 %copy-start.15 = (f32[8,12,132]{2,1,0:T(8,128)S(1)}, f32[8,12,132]{2,1,0:T(8,128)}, u32[]{:S(2)}) copy-start(f32[8,12,132]{2,1,0:T(8,128)} %get-tuple-element.70) | copy-start | bytes 152068
  81.4 3.9 %copy-start.16 = (f32[8,12,132]{2,1,0:T(8,128)S(1)}, f32[8,12,132]{2,1,0:T(8,128)}, u32[]{:S(2)}) copy-start(f32[8,12,132]{2,1,0:T(8,128)} %get-tuple-element.52) | copy-start | bytes 152068
  81.4 3.9 %copy-start.17 = (f32[8,12,132]{2,1,0:T(8,128)S(1)}, f32[8,12,132]{2,1,0:T(8,128)}, u32[]{:S(2)}) copy-start(f32[8,12,132]{2,1,0:T(8,128)} %get-tuple-element.54) | copy-start | bytes 152068
  81.4 3.9 %copy-start.18 = (f32[8,12,132]{2,1,0:T(8,128)S(1)}, f32[8,12,132]{2,1,0:T(8,128)}, u32[]{:S(2)}) copy-start(f32[8,12,132]{2,1,0:T(8,128)} %get-tuple-element.55) | copy-start | bytes 152068
  81.4 3.9 %copy-start.19 = (f32[8,12,132]{2,1,0:T(8,128)S(1)}, f32[8,12,132]{2,1,0:T(8,128)}, u32[]{:S(2)}) copy-start(f32[8,12,132]{2,1,0:T(8,128)} %get-tuple-element.56) | copy-start | bytes 152068
  81.4 3.9 %copy-start.20 = (f32[8,12,132]{2,1,0:T(8,128)S(1)}, f32[8,12,132]{2,1,0:T(8,128)}, u32[]{:S(2)}) copy-start(f32[8,12,132]{2,1,0:T(8,128)} %get-tuple-element.57) | copy-start | bytes 152068
  81.4 3.9 %copy-start.21 = (f32[8,12,132]{2,1,0:T(8,128)S(1)}, f32[8,12,132]{2,1,0:T(8,128)}, u32[]{:S(2)}) copy-start(f32[8,12,132]{2,1,0:T(8,128)} %get-tuple-element.58) | copy-start | bytes 152068
  81.4 3.9 %copy-start.22 = (f32[8,12,132]{2,1,0:T(8,128)S(1)}, f32[8,12,132]{2,1,0:T(8,128)}, u32[]{:S(2)}) copy-start(f32[8,12,132]{2,1,0:T(8,128)} %get-tuple-element.59) | copy-start | bytes 152068
  81.4 3.9 %copy-start.23 = (f32[8,12,132]{2,1,0:T(8,128)S(1)}, f32[8,12,132]{2,1,0:T(8,128)}, u32[]{:S(2)}) copy-start(f32[8,12,132]{2,1,0:T(8,128)} %get-tuple-element.60) | copy-start | bytes 152068
  81.5 3.9 %copy-start.24 = (f32[8,12,132]{2,1,0:T(8,128)S(1)}, f32[8,12,132]{2,1,0:T(8,128)}, u32[]{:S(2)}) copy-start(f32[8,12,132]{2,1,0:T(8,128)} %get-tuple-element.61) | copy-start | bytes 152068
  81.5 3.9 %copy-start.25 = (f32[8,12,132]{2,1,0:T(8,128)S(1)}, f32[8,12,132]{2,1,0:T(8,128)}, u32[]{:S(2)}) copy-start(f32[8,12,132]{2,1,0:T(8,128)} %get-tuple-element.73) | copy-start | bytes 152068
  81.5 3.9 %copy-start.26 = (f32[8,12,132]{2,1,0:T(8,128)S(1)}, f32[8,12,132]{2,1,0:T(8,128)}, u32[]{:S(2)}) copy-start(f32[8,12,132]{2,1,0:T(8,128)} %get-tuple-element.71) | copy-start | bytes 152068
  85.4 3.5 %copy-start.7 = (f32[4096,60]{0,1:T(8,128)S(1)}, f32[4096,60]{0,1:T(8,128)}, u32[]{:S(2)}) copy-start(f32[4096,60]{0,1:T(8,128)} %mul.1044) | copy-start | bytes 2949124
  85.4 3.5 %copy-start.30 = (f32[32,1,128]{2,1,0:T(1,128)S(1)}, f32[32,1,128]{2,1,0:T(1,128)}, u32[]{:S(2)}) copy-start(f32[32,1,128]{2,1,0:T(1,128)} %copy-done.29) | copy-start | bytes 49156
  85.4 3.5 %copy-start.34 = (s32[4096]{0:T(1024)S(1)}, s32[4096]{0:T(1024)}, u32[]{:S(2)}) copy-start(s32[4096]{0:T(1024)} %copy-done.33) | copy-start | bytes 49156
  85.4 3.5 %copy-start.36 = (s32[4096]{0:T(1024)S(1)}, s32[4096]{0:T(1024)}, u32[]{:S(2)}) copy-start(s32[4096]{0:T(1024)} %copy-done.35) | copy-start | bytes 49156
  85.4 3.5 %copy-start.39 = (f32[4096]{0:T(1024)S(1)}, f32[4096]{0:T(1024)}, u32[]{:S(2)}) copy-start(f32[4096]{0:T(1024)} %copy-done.38) | copy-start | bytes 49156
  88.9 2.0 %copy-start.5 = (f32[32,8,128]{2,1,0:T(8,128)S(1)}, f32[32,8,128]{2,1,0:T(8,128)}, u32[]{:S(2)}) copy-start(f32[32,8,128]{2,1,0:T(8,128)} %copy-done.4) | copy-start | bytes 393220
  88.9 2.0 %copy-start.28 = (f32[32,1,128]{2,1,0:T(1,128)S(1)}, f32[32,1,128]{2,1,0:T(1,128)}, u32[]{:S(2)}) copy-start(f32[32,1,128]{2,1,0:T(1,128)} %copy-done.27) | copy-start | bytes 49156
  88.9 2.0 %copy-start.32 = (pred[32,1,128]{2,0,1:T(8,128)(4,1)S(1)}, pred[32,1,128]{2,0,1:T(8,128)(4,1)}, u32[]{:S(2)}) copy-start(pred[32,1,128]{2,0,1:T(8,128)(4,1)} %copy-done.31) | copy-start | bytes 12292
  88.9 2.1 %copy-start.37 = (s32[4096]{0:T(1024)S(1)}, s32[4096]{0:T(1024)}, u32[]{:S(2)}) copy-start(s32[4096]{0:T(1024)} %copy-done.35) | copy-start | bytes 49156
  88.9 2.1 %copy-start.40 = (f32[4096]{0:T(1024)S(1)}, f32[4096]{0:T(1024)}, u32[]{:S(2)}) copy-start(f32[4096]{0:T(1024)} %copy-done.38) | copy-start | bytes 49156
  93.0 4.1 %collective-permute-start.11 = (f32[3,6,10,2]{3,2,1,0:T(8,128)S(1)}, f32[3,6,10,2]{3,2,1,0:T(8,128)S(1)}, u32[]{:S(2)}, u32[]{:S(2)}) collective-permute-start(f32[3,6,10,2]{3,2,1,0:T(8,128)S(1)} %get-tuple-element.126), channel_id=1, source_target_pairs={{1,0},{2,1},{3,2},{0,3},{5,4},{6,5},{7,6},{4,7},{9,8},{10,9},{11,1... | collective-permute-start | bytes 4328 | tf_op jit(solution)/shard_map/ppermute | solution.py:43
  93.0 4.6 %collective-permute-start.10 = (f32[3,6,10,2]{3,2,1,0:T(8,128)S(1)}, f32[3,6,10,2]{3,2,1,0:T(8,128)S(1)}, u32[]{:S(2)}, u32[]{:S(2)}) collective-permute-start(f32[3,6,10,2]{3,2,1,0:T(8,128)S(1)} %get-tuple-element.125), channel_id=1, source_target_pairs={{0,1},{1,2},{2,3},{3,0},{4,5},{5,6},{6,7},{7,4},{8,9},{9,10},{10,1... | collective-permute-start | bytes 4328 | tf_op jit(solution)/shard_map/ppermute | solution.py:42
  97.7 5.6 %collective-permute-start.13 = (f32[3,2,10,130]{3,2,1,0:T(8,128)S(1)}, f32[3,2,10,130]{3,2,1,0:T(8,128)S(1)}, u32[]{:S(2)}, u32[]{:S(2)}) collective-permute-start(f32[3,2,10,130]{3,2,1,0:T(8,128)S(1)} %get-tuple-element.124), channel_id=1, source_target_pairs={{8,0},{16,8},{24,16},{0,24},{9,1},{17,9},{25,17},{1,25},{10,2},{18... | collective-permute-start | bytes 93608 | tf_op jit(solution)/shard_map/ppermute | solution.py:43
  100.8 6.9 %collective-permute-start.12 = (f32[3,2,10,130]{3,2,1,0:T(8,128)S(1)}, f32[3,2,10,130]{3,2,1,0:T(8,128)S(1)}, u32[]{:S(2)}, u32[]{:S(2)}) collective-permute-start(f32[3,2,10,130]{3,2,1,0:T(8,128)S(1)} %get-tuple-element.123), channel_id=1, source_target_pairs={{0,8},{8,16},{16,24},{24,0},{1,9},{9,17},{17,25},{25,1},{2,10},{10... | collective-permute-start | bytes 93608 | tf_op jit(solution)/shard_map/ppermute | solution.py:42
  107.8 4.4 %collective-permute-start.14 = (f32[2,3,6,2,130]{4,3,2,1,0:T(2,128)S(1)}, f32[2,3,6,2,130]{4,3,2,1,0:T(2,128)S(1)}, u32[]{:S(2)}, u32[]{:S(2)}) collective-permute-start(f32[2,3,6,2,130]{4,3,2,1,0:T(2,128)S(1)} %pad_maximum_fusion.12), channel_id=1, source_target_pairs={{0,4},{4,0},{1,5},{5,1},{2,6},{6,2},{3,7},{7,3},{8,12},{12,8},{9,1... | collective-permute-start | bytes 112328 | tf_op jit(solution)/shard_map/ppermute | solution.py:39

commit v3 on v2

--- a/solution.py
+++ b/solution.py
@@ -1,6 +1,10 @@
+import functools
+
 import jax
 import jax.numpy as jnp
 from jax import lax
+from jax.experimental import pallas as pl
+from jax.experimental.pallas import tpu as pltpu
 from jax.sharding import PartitionSpec as P
 
 STEPS = 2
@@ -33,41 +37,151 @@
 speed_unit = 0.05
 
 
-def swap(axis, onward, backward):
+AXES = ("gx", "gy", "gz")
+MESH = pl.DeviceIdType.MESH
+
+
+def neighbour(axis, step):
+    place = [lax.axis_index(name) for name in AXES]
     count = lax.axis_size(axis)
-    if count == 2:
-        both = lax.ppermute(jnp.stack([onward, backward]), axis, [(0, 1), (1, 0)])
-        return (both[0], both[1])
-    return (
-        lax.ppermute(onward, axis, [(i, (i + 1) % count) for i in range(count)]),
-        lax.ppermute(backward, axis, [((i + 1) % count, i) for i in range(count)]),
-    )
-
-
-def with_halo(cells, sides, width):
-    for axis, dim in sides:
-        length = cells.shape[dim]
-        head = lax.slice_in_dim(cells, 0, width, axis=dim)
-        tail = lax.slice_in_dim(cells, length - width, length, axis=dim)
-        before, after = swap(axis, tail, head)
-        cells = jnp.concatenate([before, cells, after], axis=dim)
-    return cells
-
-
-def spread_sums(ghosts, sides, width):
-    for axis, dim in sides:
-        length = ghosts.shape[dim]
-        head = lax.slice_in_dim(ghosts, 0, width + 1, axis=dim)
-        tail = lax.slice_in_dim(ghosts, length - width - 1, length, axis=dim)
-        before, after = swap(axis, tail, head)
-        around = [(0, 0)] * 4
-        around[dim] = (width - 1, width - 1)
-        low, high = list(around), list(around)
-        rest = length + 2 * (width - 1) - (width + 1)
-        low[dim] = (0, rest)
-        high[dim] = (rest, 0)
-        ghosts = jnp.pad(ghosts, around) + jnp.pad(before, low) + jnp.pad(after, high)
-    return ghosts
+    where = AXES.index(axis)
+    place[where] = lax.rem(place[where] + count + step, count)
+    return tuple(place)
+
+
+def greet():
+    barrier = pltpu.get_barrier_semaphore()
+    for axis in AXES:
+        for step in (1, -1):
+            pl.semaphore_signal(barrier, inc=1, device_id=neighbour(axis, step), device_id_type=MESH)
+    pl.semaphore_wait(barrier, 6)
+
+
+def swap(axis, sources, targets, send_sems, recv_sems):
+    copies = []
+    for k, step in enumerate((1, -1)):
+        number = 2 * AXES.index(axis) + k
+        copy = pltpu.make_async_remote_copy(
+            src_ref=sources[k],
+            dst_ref=targets[k],
+            send_sem=send_sems.at[number],
+            recv_sem=recv_sems.at[number],
+            device_id=neighbour(axis, step),
+            device_id_type=MESH,
+        )
+        copy.start()
+        copies.append(copy)
+    for copy in copies:
+        copy.wait()
+
+
+def widen_kernel(width, cells, out, y_out, y_in, mid, z_out, z_in, send_sems, recv_sems):
+    fields, size_x, size_y, size_z = cells.shape
+    greet()
+    y_out[0] = cells[:, :, size_y - width :, :]
+    y_out[1] = cells[:, :, :width, :]
+    swap("gy", (y_out.at[0], y_out.at[1]), (y_in.at[0], y_in.at[1]), send_sems, recv_sems)
+    mid[:, width : width + size_x] = jnp.concatenate([y_in[0], cells[...], y_in[1]], axis=2)
+    swap(
+        "gx",
+        (mid.at[:, pl.ds(size_x, width)], mid.at[:, pl.ds(width, width)]),
+        (mid.at[:, pl.ds(0, width)], mid.at[:, pl.ds(size_x + width, width)]),
+        send_sems,
+        recv_sems,
+    )
+    z_out[0] = jnp.concatenate([mid[c, :, :, size_z - width :] for c in range(fields)], axis=-1)
+    z_out[1] = jnp.concatenate([mid[c, :, :, :width] for c in range(fields)], axis=-1)
+    swap("gz", (z_out.at[0], z_out.at[1]), (z_in.at[0], z_in.at[1]), send_sems, recv_sems)
+    for c in range(fields):
+        cut = slice(c * width, (c + 1) * width)
+        out[c] = jnp.concatenate([z_in[0, :, :, cut], mid[c], z_in[1, :, :, cut]], axis=-1)
+
+
+def call_kernel(kernel, operand, out_shape, scratch, number):
+    return pl.pallas_call(
+        kernel,
+        out_shape=jax.ShapeDtypeStruct(out_shape, jnp.float32),
+        in_specs=[pl.BlockSpec(memory_space=pltpu.VMEM)],
+        out_specs=pl.BlockSpec(memory_space=pltpu.VMEM),
+        scratch_shapes=[pltpu.VMEM(shape, jnp.float32) for shape in scratch]
+        + [pltpu.SemaphoreType.DMA((6,)), pltpu.SemaphoreType.DMA((6,))],
+        compiler_params=pltpu.CompilerParams(
+            collective_id=number, has_side_effects=True, vmem_limit_bytes=40 * 1024 * 1024
+        ),
+    )(operand)
+
+
+def with_halo(cells, width):
+    fields, size_x, size_y, size_z = cells.shape
+    wide_x, wide_y, wide_z = (size_x + 2 * width, size_y + 2 * width, size_z + 2 * width)
+    y_slab = (2, fields, size_x, width, size_z)
+    z_slab = (2, wide_x, wide_y, fields * width)
+    return call_kernel(
+        functools.partial(widen_kernel, width),
+        cells,
+        (fields, wide_x, wide_y, wide_z),
+        [y_slab, y_slab, (fields, wide_x, wide_y, size_z), z_slab, z_slab],
+        0,
+    )
+
+
+def add_ends(middle, before, after, dim, width):
+    length = middle.shape[dim]
+    part = functools.partial(lax.slice_in_dim, axis=dim)
+    if width == 1:
+        pieces = [
+            part(middle, 0, 2) + before,
+            part(middle, 2, length - 2),
+            part(middle, length - 2, length) + after,
+        ]
+    else:
+        pieces = [
+            part(before, 0, width - 1),
+            part(middle, 0, 2) + part(before, width - 1, width + 1),
+            part(middle, 2, length - 2),
+            part(middle, length - 2, length) + part(after, 0, 2),
+            part(after, 2, width + 1),
+        ]
+    return jnp.concatenate(pieces, axis=dim)
+
+
+def spread_kernel(width, ghosts, out, z_out, z_in, mid, x_in, y_out, y_in, send_sems, recv_sems):
+    _, size_x, size_y, size_z = ghosts.shape
+    layers = width + 1
+    greet()
+    z_out[0] = jnp.concatenate([ghosts[d, :, :, size_z - layers :] for d in range(3)], axis=-1)
+    z_out[1] = jnp.concatenate([ghosts[d, :, :, :layers] for d in range(3)], axis=-1)
+    swap("gz", (z_out.at[0], z_out.at[1]), (z_in.at[0], z_in.at[1]), send_sems, recv_sems)
+    for d in range(3):
+        cut = slice(d * layers, (d + 1) * layers)
+        mid[d] = add_ends(ghosts[d], z_in[0, :, :, cut], z_in[1, :, :, cut], 2, width)
+    swap(
+        "gx",
+        (mid.at[:, pl.ds(size_x - layers, layers)], mid.at[:, pl.ds(0, layers)]),
+        (x_in.at[0], x_in.at[1]),
+        send_sems,
+        recv_sems,
+    )
+    summed = add_ends(mid[...], x_in[0], x_in[1], 1, width)
+    y_out[0] = summed[:, :, size_y - layers :, :]
+    y_out[1] = summed[:, :, :layers, :]
+    swap("gy", (y_out.at[0], y_out.at[1]), (y_in.at[0], y_in.at[1]), send_sems, recv_sems)
+    out[...] = add_ends(summed, y_in[0], y_in[1], 2, width)
+
+
+def spread_sums(ghosts, width):
+    _, size_x, size_y, size_z = ghosts.shape
+    more = 2 * (width - 1)
+    z_slab = (2, size_x, size_y, 3 * (width + 1))
+    x_slab = (2, 3, width + 1, size_y, size_z + more)
+    y_slab = (2, 3, size_x + more, width + 1, size_z + more)
+    return call_kernel(
+        functools.partial(spread_kernel, width),
+        ghosts,
+        (3, size_x + more, size_y + more, size_z + more),
+        [z_slab, z_slab, (3, size_x, size_y, size_z + more), x_slab, y_slab, y_slab],
+        width,
+    )
 
 
 def project(vector, direction):
@@ -174,9 +288,8 @@
             + jnp.where(grid == farther[:, None], jnp.abs(displace)[:, None], 0.0)
         )
     across = (tables[0][:, :, None] * tables[1][:, None, :]).reshape(slots * rows_block, -1)
-    sides = (("gz", 3), ("gx", 1), ("gy", 2))
     gray = solid_class.astype(jnp.float32) * 0.25
-    wide = with_halo(jnp.concatenate([populations, gray[None]]), sides, STEPS)
+    wide = with_halo(jnp.concatenate([populations, gray[None]]), STEPS)
     fields = [wide[i] for i in range(19)]
     gray_fraction = wide[19]
     for repeat in range(STEPS):
@@ -199,7 +312,7 @@
             precision=lax.Precision.HIGH,
         )
         ghosts = ghosts.reshape(3, size_x + 2, size_y + 2, size_z + 2)
-        cell_force = spread_sums(ghosts, sides, reach)
+        cell_force = spread_sums(ghosts, reach)
         post_list = collide(fields, density, flow, cell_force, gray_fraction)
         fields = propagate(post_list)
         gray_fraction = gray_fraction[1:-1, 1:-1, 1:-1]

time: 116 us -> 106 us (0.914)
  Pallas kernels: 0 us -> 58.1 us
  waiting for transfers between devices: 53.4 us -> 0.01 us
  starting transfers between devices: 22.1 us -> 6.32 us
    pallas_call x0 -> x3, Pallas kernels: none -> 58.1 us  [call_kernel(): pl.pallas_call(kernel, out_shape=jax.ShapeDtypeStruct(out_shape, jnp.floa...]
    ppermute x15 -> x0, waiting for transfers between devices: 53.4 us -> none  [the longest x6 19.2 us: swap(): lax.ppermute(backward, axis, [((i + 1) % count, i) for i in range(count)])]
    ppermute x15 -> x0, starting transfers between devices: 17 us -> none  [the longest x6 10.9 us: swap(): lax.ppermute(backward, axis, [((i + 1) % count, i) for i in range(count)])]
    mul x4, other arithmetic: 4.55 us -> 9.48 us  [collide(): equilibrium = weights[i] * baseline]
    concatenate x3 -> x1, other arithmetic: 4.67 us -> 0.99 us  [per_device(): wide = with_halo(jnp.concatenate([populations, gray[None]]), STEPS)]
    another operation x4 -> x0, other arithmetic: 1.92 us -> none  [swap(): both = lax.ppermute(jnp.stack([onward, backward]), axis, [(0, 1), (1, 0)])]
    another operation x4, other arithmetic: 2.71 us -> 4.01 us  [moments(): return (density, jnp.stack(components))]
    all_to_all x1, starting transfers between devices: 5.09 us -> 6.32 us  [per_device(): lax.all_to_all(send_floats, 'gx', split_axis=0, concat_axis=0, tiled=True)]
  transfers between devices with their start and end apart: 16 -> 1, of which waited for: 14 -> 0; matrix products, arithmetic and copies ran while one was open for 11% -> 9% of each run, Pallas kernels for 0% -> 23%
where the time goes in v3:
time: 106 us; the launch traced here: 105 us
  Pallas kernels  58.1 us (55%)
  other arithmetic  24.2 us (23%)
  matrix products  9.3 us (9%)
  starting transfers between devices  6.32 us (6%)
  local copies, waits for them, and re-layouts  5.99 us (6%)
  between operations  1.38 us (1%)
    pallas_call x3, Pallas kernels, call_kernel(): pl.pallas_call(kernel, out_shape=jax.ShapeDtypeStruct(out_shape, jnp.floa...  58.1 us
    mul x4, other arithmetic, collide(): equilibrium = weights[i] * baseline  9.48 us
    all_to_all x1, starting transfers between devices, per_device(): lax.all_to_all(send_floats, 'gx', split_axis=0, concat_axis=0, tiled=True)  6.32 us
    dot_general x2, matrix products, per_device(): jnp.einsum('nz,dkz->dnk', tables[2], lines, precision=lax.Precision.HIGH)  4.84 us
    dot_general x2, matrix products, per_device(): jnp.einsum('dnk,nz->dkz', pushed[:, :, None] * across[None], tables[2], p...  4.47 us
    another operation x4, other arithmetic, moments(): return (density, jnp.stack(components))  4.01 us
    unnamed x68, local copies, waits for them, and re-layouts  3.37 us
    squeeze x2, other arithmetic, per_device(): fields = [wide[i] for i in range(19)]  2.13 us
  transfers between devices with their start and end apart: 1, of which 0 were waited for; matrix products, arithmetic and copies ran while one was open for 9% of the time, Pallas kernels for 23%

profile of v3, /device:TPU:0, one launch (start us, length us, event | category | flops | bytes accessed | tf_op | source)
XLA Modules:
  0.0 105.3 jit_solution(6789619658784421640)
XLA Ops:
  0.6 0.7 fusion.356
  1.4 0.8 select_reduce_fusion.1
  2.2 0.7 multiply_add_fusion
  2.9 0.1 select_reduce_fusion
  3.0 0.1 fusion.355
  3.1 0.8 copy.17
  3.9 0.8 copy.16
  4.6 0.8 select_convert_fusion
  5.4 0.7 pad_maximum_fusion.3
  6.1 0.6 gather_fusion
  6.7 0.8 select_select_fusion
  7.5 6.3 %all-to-all-start = ((f32[32,8,128]{2,1,0:T(8,128)}), f32[32,8,128]{2,1,0:T(8,128)S(1)}, u32[]{:S(2)}, u32[]{:S(2)}) async-start(f32[32,8,128]{2,1,0:T(8,128)} %select_select_fusion), calls=%async_computation | async-start | bytes 262144 | tf_op jit(solution)/shard_map/all_to_all | solution.py:270
  13.9 0.7 multiply_bitcast_fusion
  14.6 1.0 pad_maximum_fusion.cells
  15.6 24.5 %shard_map.95 = f32[20,8,12,132]{3,2,1,0:T(8,128)S(1)} custom-call(f32[20,4,8,128]{3,2,1,0:T(8,128)S(1)} %pad_maximum_fusion.cells), custom_call_target="tpu_custom_call" | custom-call | tf_op jit(solution)/shard_map/pallas_call | solution.py:101
  40.0 0.8 add_add_fusion
  40.8 1.2 %fusion.48 = (f32[8,12,132]{2,1,0:T(8,128)}, f32[8,12,132]{2,1,0:T(8,128)S(1)}, f32[8,12,132]{2,1,0:T(8,128)}, f32[8,12,132]{2,1,0:T(8,128)}, f32[8,12,132]{2,1,0:T(8,128)}) fusion(f32[20,8,12,132]{3,2,1,0:T(8,128)S(1)} %shard_map.95), kind=kLoop, calls=%fused_computation.93 | loop fusion | flops 899712 | bytes 1216512 | tf_op jit(solution)/shard_map/mul | solution.py:220
  42.0 1.1 %slice_bitcast_fusion.5 = (f32[8,12,132]{2,1,0:T(8,128)}, f32[1,8,12,132]{3,2,1,0:T(8,128)S(1)}, f32[8,12,132]{2,1,0:T(8,128)}, f32[8,12,132]{2,1,0:T(8,128)}, f...) fusion(f32[20,8,12,132]{3,2,1,0:T(8,128)S(1)} %shard_map.95), kind=kLoop, calls=%fused_computation.142 | loop fusion | flops 177408 | bytes 1216512 | tf_op jit(solution)/shard_map/squeeze | solution.py:293
  43.1 1.1 %slice_bitcast_fusion.11 = (f32[8,12,132]{2,1,0:T(8,128)}, f32[1,8,12,132]{3,2,1,0:T(8,128)S(1)}, f32[8,12,132]{2,1,0:T(8,128)}, f32[8,12,132]{2,1,0:T(8,128)}, ...) fusion(f32[20,8,12,132]{3,2,1,0:T(8,128)S(1)} %shard_map.95), kind=kLoop, calls=%fused_computation.148 | loop fusion | flops 177408 | bytes 1216512 | tf_op jit(solution)/shard_map/squeeze | solution.py:293
  44.2 0.1 pad_maximum_fusion.1
  44.3 0.7 reshape.363
  45.0 0.0 copy-done
  45.0 2.6 %fusion.78 = (f32[8,12,132]{2,1,0:T(8,128)}, f32[8,12,132]{2,1,0:T(8,128)}, f32[8,12,132]{2,1,0:T(8,128)}, f32[8,12,132]{2,1,0:T(8,128)}, f32[8,12,132]{2,1,0:T(...) fusion(f32[8,12,132]{2,1,0:T(8,128)S(1)} %get-tuple-element.46,, ...), kind=kLoop, calls=%fused_computation.123 | loop fusion | flops 1495296 | bytes 1165824 | tf_op jit(solution)/shard_map/mul | solution.py:220
  47.7 0.1 broadcast_subtract_fusion.1
  47.8 0.0 all-to-all-done
  47.8 0.1 fusion.404
  47.9 0.1 compare_select_fusion.2
  48.0 0.0 copy-start.26
  48.0 0.0 copy-start.28
  48.1 0.0 copy-start.25
  48.1 0.1 broadcast_multiply_fusion
  48.3 0.1 mul.1044
  48.4 0.0 copy-start.30
  48.5 0.6 copy-done.25
  49.1 1.9 %fusion.14 = f32[3,4096]{1,0:T(4,128)S(1)} fusion(f32[4096,60]{0,1:T(8,128)S(1)} %mul.1044, f32[3,60,130]{2,1,0:T(8,128)S(1)} %copy-done.25, f32[4096]{0:T(1024)S(1)} %bitcast.310, s32[4096]{0:T(1024)S(1)} %get-tuple-element.154, f32[4096]{0:T(1024)S(1)} %broadcast_subtract_fusion.4, s32[4096]{0:T(1024)S(1)} %get-tuple-element.153), kind=kOutput, calls=%fused_computation.20 | convolution fusion | flops 579203072 | bytes 1191328 | tf_op jit(solution)/shard_map/nz,dkz->dnk/dot_general | solution.py:302
  51.0 0.0 copy-start.23
  51.1 0.0 copy-done.26
  51.1 0.0 copy-done.28
  51.1 0.0 copy-done.30
  51.1 0.5 copy-done.23
  51.6 2.6 %fusion.4 = f32[3,60,130]{2,1,0:T(8,128)} fusion(f32[3,4096]{1,0:T(4,128)S(1)} %negate_bitcast_fusion.1, f32[4096,60]{0,1:T(8,128)S(1)} %mul.1044, f32[4096]{0:T(1024)S(1)} %bitcast.311, s32[4096]{0:T(1024)S(1)} %get-tuple-element.154, f32[4096]{0:T(1024)S(1)} %broadcast_subtract_fusion.4, s32[4096]{0:T(1024)S(1)} %get-tuple-element.153), kind=kOutput, calls=%fused_computation.7 | convolution fusion | flops 578478080 | bytes 1191328 | tf_op jit(solution)/shard_map/dnk,nz->dkz/dot_general | solution.py:310
  54.2 0.0 copy-start.5
  54.2 0.0 copy-start.6
  54.2 0.0 copy-start.7
  54.2 0.0 copy-start.8
  54.3 0.0 copy-start.9
  54.3 0.0 copy-start.10
  54.3 0.0 copy-start.11
  54.3 0.0 copy-start.20
  54.3 1.1 %reshape.365.ghosts = f32[3,6,10,130]{3,2,1,0:T(8,128)S(1)} reshape(f32[3,60,130]{2,1,0:T(8,128)} %fusion.4) | data formatting | bytes 187200 | tf_op jit(solution)/shard_map/reshape | solution.py:314
  55.5 19.8 %shard_map.96 = f32[3,8,12,132]{3,2,1,0:T(8,128)S(1)} custom-call(f32[3,6,10,130]{3,2,1,0:T(8,128)S(1)} %reshape.365.ghosts), custom_call_target="tpu_custom_call" | custom-call | tf_op jit(solution)/shard_map/pallas_call | solution.py:101
  75.6 5.2 %fusion.82 = (f32[6,10,130]{2,1,0:T(8,128)}, f32[6,10,130]{2,1,0:T(8,128)}, f32[6,10,130]{2,1,0:T(8,128)S(1)}, f32[6,10,130]{2,1,0:T(8,128)}, f32[6,10,130]{2,1,...) fusion(f32[8,12,132]{2,1,0:T(8,128)S(1)} %get-tuple-element.74,, ...), kind=kLoop, calls=%fused_computation.161 | loop fusion | flops 1817400 | bytes 4586400 | tf_op jit(solution)/shard_map/mul | solution.py:220
  80.9 0.0 copy-start.29
  80.9 0.0 copy-start.31
  80.9 2.9 %fusion.17 = f32[3,4096]{1,0:T(4,128)S(1)} fusion(f32[4096,60]{0,1:T(8,128)S(1)} %mul.1044, f32[4096]{0:T(1024)S(1)} %bitcast.312, s32[4096]{0:T(1024)} %copy-done.28, f32[4096]{0:T(1024)} %copy-done.30, s32[4096]{0:T(1024)} %copy-done.26, f32[1,60,130]{2,1,0:T(8,128)S(1)} %stack.33, f32[1,60,130]{2,1,0:T(8,128)S(1)} %stack.32, f32[1,60,130]{2,1,0:T(8,128)S(1)} %stack.31), kind=kOutput, calls=%fused_computation.21 | convolution fusion | flops 579249856 | bytes 1191328 | tf_op jit(solution)/shard_map/nz,dkz->dnk/dot_general | solution.py:302
  83.8 0.1 multiply_select_fusion
  83.9 1.9 %fusion.2 = f32[3,60,130]{2,1,0:T(8,128)S(1)} fusion(f32[3,4096]{1,0:T(4,128)S(1)} %get-tuple-element.112, f32[4096,60]{0,1:T(8,128)S(1)} %mul.1044, f32[4096]{0:T(1024)S(1)} %bitcast.313, s32[4096]{0:T(1024)S(1)} %copy-done.29, f32[4096]{0:T(1024)S(1)} %copy-done.31, s32[4096]{0:T(1024)S(1)} %copy-done.27), kind=kOutput, calls=%fused_computation.5 | convolution fusion | flops 578478080 | bytes 1191328 | tf_op jit(solution)/shard_map/dnk,nz->dkz/dot_general | solution.py:310
  85.9 13.8 %shard_map.97 = f32[3,6,10,130]{3,2,1,0:T(8,128)S(1)} custom-call(f32[3,6,10,130]{3,2,1,0:T(8,128)S(1)} %reshape.367.ghosts), custom_call_target="tpu_custom_call" | custom-call | tf_op jit(solution)/shard_map/pallas_call | solution.py:101
  99.8 0.4 fusion.114
  100.2 0.6 copy.18
  100.8 1.6 %fusion.345 = (f32[1,4,8,128]{3,2,1,0:T(8,128)S(1)}, f32[4,8,128]{2,1,0:T(8,128)S(1)}, f32[4,8,128]{2,1,0:T(8,128)S(1)}, f32[4,8,128]{2,1,0:T(8,128)S(1)}, f32[4...) fusion(f32[6,10,130]{2,1,0:T(8,128)} %get-tuple-element.21, ...), kind=kLoop, calls=%fused_computation.593 | loop fusion | flops 417792 | bytes 1261568 | tf_op jit(solution)/shard_map/stack | solution.py:208
  102.4 1.3 %fusion.284 = (f32[1,4,8,128]{3,2,1,0:T(8,128)S(1)}, f32[4,8,128]{2,1,0:T(8,128)S(1)}, f32[4,8,128]{2,1,0:T(8,128)S(1)}, f32[4,8,128]{2,1,0:T(8,128)S(1)}, f32[4,8,128]{2,1,0:T(8,128)S(1)}) fusion(f32[4,8,128]{2,1,0:T(8,128)S(1)} %get-tuple-element.12, f32[4,8,128]{2,1,0:T(8,128)S(1)} %get-tuple-element.11, f32[4,8,128]{2,1,0:T(8,128)S(1)} %get-tuple-element.10, ...), kind=kLoop, calls=%fused_computation.492 | loop fusion | flops 266240 | bytes 802816 | tf_op jit(solution)/shard_map/stack | solution.py:208
  103.6 1.0 fusion.244
  104.7 0.6 maximum_multiply_fusion
  (65 shorter events, 0.5 us)
Async XLA Ops:
  7.5 40.2 %all-to-all-start = ((f32[32,8,128]{2,1,0:T(8,128)}), f32[32,8,128]{2,1,0:T(8,128)S(1)}, u32[]{:S(2)}, u32[]{:S(2)}) async-start(f32[32,8,128]{2,1,0:T(8,128)} %select_select_fusion), calls=%async_computation | async-start | bytes 262144 | tf_op jit(solution)/shard_map/all_to_all | solution.py:270
  42.0 3.0 %copy-start = (f32[8,12,132]{2,1,0:T(8,128)}, f32[8,12,132]{2,1,0:T(8,128)S(1)}, u32[]{:S(2)}) copy-start(f32[8,12,132]{2,1,0:T(8,128)S(1)} %get-tuple-element.46) | copy-start | bytes 152068
  48.0 3.1 %copy-start.26 = (s32[4096]{0:T(1024)}, s32[4096]{0:T(1024)S(1)}, u32[]{:S(2)}) copy-start(s32[4096]{0:T(1024)S(1)} %get-tuple-element.153) | copy-start | bytes 49156
  48.0 3.1 %copy-start.28 = (s32[4096]{0:T(1024)}, s32[4096]{0:T(1024)S(1)}, u32[]{:S(2)}) copy-start(s32[4096]{0:T(1024)S(1)} %get-tuple-element.154) | copy-start | bytes 49156
  48.1 0.9 copy-start.25
  48.4 2.6 %copy-start.30 = (f32[4096]{0:T(1024)}, f32[4096]{0:T(1024)S(1)}, u32[]{:S(2)}) copy-start(f32[4096]{0:T(1024)S(1)} %broadcast_subtract_fusion.4) | copy-start | bytes 49156
  51.0 0.6 copy-start.23
  54.2 21.1 %copy-start.1 = (f32[8,12,132]{2,1,0:T(8,128)S(1)}, f32[8,12,132]{2,1,0:T(8,128)}, u32[]{:S(2)}) copy-start(f32[8,12,132]{2,1,0:T(8,128)} %copy-done) | copy-start | bytes 152068
  54.2 21.1 %copy-start.2 = (f32[8,12,132]{2,1,0:T(8,128)S(1)}, f32[8,12,132]{2,1,0:T(8,128)}, u32[]{:S(2)}) copy-start(f32[8,12,132]{2,1,0:T(8,128)} %get-tuple-element.62) | copy-start | bytes 152068
  54.2 21.2 %copy-start.3 = (f32[8,12,132]{2,1,0:T(8,128)S(1)}, f32[8,12,132]{2,1,0:T(8,128)}, u32[]{:S(2)}) copy-start(f32[8,12,132]{2,1,0:T(8,128)} %get-tuple-element.64) | copy-start | bytes 152068
  54.2 21.2 %copy-start.4 = (f32[8,12,132]{2,1,0:T(8,128)S(1)}, f32[8,12,132]{2,1,0:T(8,128)}, u32[]{:S(2)}) copy-start(f32[8,12,132]{2,1,0:T(8,128)} %get-tuple-element.65) | copy-start | bytes 152068
  54.2 21.2 %copy-start.5 = (f32[8,12,132]{2,1,0:T(8,128)S(1)}, f32[8,12,132]{2,1,0:T(8,128)}, u32[]{:S(2)}) copy-start(f32[8,12,132]{2,1,0:T(8,128)} %get-tuple-element.66) | copy-start | bytes 152068
  54.2 21.2 %copy-start.6 = (f32[8,12,132]{2,1,0:T(8,128)S(1)}, f32[8,12,132]{2,1,0:T(8,128)}, u32[]{:S(2)}) copy-start(f32[8,12,132]{2,1,0:T(8,128)} %get-tuple-element.67) | copy-start | bytes 152068
  54.2 21.2 %copy-start.7 = (f32[8,12,132]{2,1,0:T(8,128)S(1)}, f32[8,12,132]{2,1,0:T(8,128)}, u32[]{:S(2)}) copy-start(f32[8,12,132]{2,1,0:T(8,128)} %get-tuple-element.68) | copy-start | bytes 152068
  54.2 21.2 %copy-start.8 = (f32[8,12,132]{2,1,0:T(8,128)S(1)}, f32[8,12,132]{2,1,0:T(8,128)}, u32[]{:S(2)}) copy-start(f32[8,12,132]{2,1,0:T(8,128)} %get-tuple-element.69) | copy-start | bytes 152068
  54.3 21.2 %copy-start.9 = (f32[8,12,132]{2,1,0:T(8,128)S(1)}, f32[8,12,132]{2,1,0:T(8,128)}, u32[]{:S(2)}) copy-start(f32[8,12,132]{2,1,0:T(8,128)} %get-tuple-element.70) | copy-start | bytes 152068
  54.3 21.2 %copy-start.10 = (f32[8,12,132]{2,1,0:T(8,128)S(1)}, f32[8,12,132]{2,1,0:T(8,128)}, u32[]{:S(2)}) copy-start(f32[8,12,132]{2,1,0:T(8,128)} %get-tuple-element.52) | copy-start | bytes 152068
  54.3 21.2 %copy-start.11 = (f32[8,12,132]{2,1,0:T(8,128)S(1)}, f32[8,12,132]{2,1,0:T(8,128)}, u32[]{:S(2)}) copy-start(f32[8,12,132]{2,1,0:T(8,128)} %get-tuple-element.54) | copy-start | bytes 152068
  54.3 21.2 %copy-start.20 = (f32[8,12,132]{2,1,0:T(8,128)S(1)}, f32[8,12,132]{2,1,0:T(8,128)}, u32[]{:S(2)}) copy-start(f32[8,12,132]{2,1,0:T(8,128)} %get-tuple-element.45) | copy-start | bytes 152068
  55.4 20.1 %copy-start.12 = (f32[8,12,132]{2,1,0:T(8,128)S(1)}, f32[8,12,132]{2,1,0:T(8,128)}, u32[]{:S(2)}) copy-start(f32[8,12,132]{2,1,0:T(8,128)} %get-tuple-element.55) | copy-start | bytes 152068
  55.4 20.1 %copy-start.13 = (f32[8,12,132]{2,1,0:T(8,128)S(1)}, f32[8,12,132]{2,1,0:T(8,128)}, u32[]{:S(2)}) copy-start(f32[8,12,132]{2,1,0:T(8,128)} %get-tuple-element.56) | copy-start | bytes 152068
  55.4 20.1 %copy-start.14 = (f32[8,12,132]{2,1,0:T(8,128)S(1)}, f32[8,12,132]{2,1,0:T(8,128)}, u32[]{:S(2)}) copy-start(f32[8,12,132]{2,1,0:T(8,128)} %get-tuple-element.57) | copy-start | bytes 152068
  55.4 20.1 %copy-start.15 = (f32[8,12,132]{2,1,0:T(8,128)S(1)}, f32[8,12,132]{2,1,0:T(8,128)}, u32[]{:S(2)}) copy-start(f32[8,12,132]{2,1,0:T(8,128)} %get-tuple-element.58) | copy-start | bytes 152068
  55.4 20.1 %copy-start.16 = (f32[8,12,132]{2,1,0:T(8,128)S(1)}, f32[8,12,132]{2,1,0:T(8,128)}, u32[]{:S(2)}) copy-start(f32[8,12,132]{2,1,0:T(8,128)} %get-tuple-element.59) | copy-start | bytes 152068
  55.4 20.1 %copy-start.17 = (f32[8,12,132]{2,1,0:T(8,128)S(1)}, f32[8,12,132]{2,1,0:T(8,128)}, u32[]{:S(2)}) copy-start(f32[8,12,132]{2,1,0:T(8,128)} %get-tuple-element.60) | copy-start | bytes 152068
  55.4 20.1 %copy-start.18 = (f32[8,12,132]{2,1,0:T(8,128)S(1)}, f32[8,12,132]{2,1,0:T(8,128)}, u32[]{:S(2)}) copy-start(f32[8,12,132]{2,1,0:T(8,128)} %get-tuple-element.61) | copy-start | bytes 152068
  55.4 20.1 %copy-start.19 = (f32[8,12,132]{2,1,0:T(8,128)S(1)}, f32[8,12,132]{2,1,0:T(8,128)}, u32[]{:S(2)}) copy-start(f32[8,12,132]{2,1,0:T(8,128)} %get-tuple-element.73) | copy-start | bytes 152068
  55.5 20.1 %copy-start.21 = (f32[8,12,132]{2,1,0:T(8,128)S(1)}, f32[8,12,132]{2,1,0:T(8,128)}, u32[]{:S(2)}) copy-start(f32[8,12,132]{2,1,0:T(8,128)} %get-tuple-element.71) | copy-start | bytes 152068
  80.9 3.0 %copy-start.24 = (f32[3,4096]{1,0:T(4,128)S(1)}, f32[3,4096]{1,0:T(4,128)}, u32[]{:S(2)}) copy-start(f32[3,4096]{1,0:T(4,128)} %copy-done.23) | copy-start | bytes 147460
  80.9 3.0 %copy-start.27 = (s32[4096]{0:T(1024)S(1)}, s32[4096]{0:T(1024)}, u32[]{:S(2)}) copy-start(s32[4096]{0:T(1024)} %copy-done.26) | copy-start | bytes 49156
  80.9 3.0 %copy-start.29 = (s32[4096]{0:T(1024)S(1)}, s32[4096]{0:T(1024)}, u32[]{:S(2)}) copy-start(s32[4096]{0:T(1024)} %copy-done.28) | copy-start | bytes 49156
  80.9 3.0 %copy-start.31 = (f32[4096]{0:T(1024)S(1)}, f32[4096]{0:T(1024)}, u32[]{:S(2)}) copy-start(f32[4096]{0:T(1024)} %copy-done.30) | copy-start | bytes 49156
  85.8 14.0 %copy-start.22 = (f32[6,10,130]{2,1,0:T(8,128)S(1)}, f32[6,10,130]{2,1,0:T(8,128)}, u32[]{:S(2)}) copy-start(f32[6,10,130]{2,1,0:T(8,128)} %get-tuple-element.18) | copy-start | bytes 93604

commit v4 on v3

--- a/solution.py
+++ b/solution.py
@@ -57,10 +57,10 @@
     pl.semaphore_wait(barrier, 6)
 
 
-def swap(axis, sources, targets, send_sems, recv_sems):
+def send(axis, sources, targets, send_sems, recv_sems, offset=0):
     copies = []
     for k, step in enumerate((1, -1)):
-        number = 2 * AXES.index(axis) + k
+        number = 2 * AXES.index(axis) + k + offset
         copy = pltpu.make_async_remote_copy(
             src_ref=sources[k],
             dst_ref=targets[k],
@@ -71,24 +71,66 @@
         )
         copy.start()
         copies.append(copy)
-    for copy in copies:
+    return copies
+
+
+def swap(axis, sources, targets, send_sems, recv_sems, offset=0):
+    for copy in send(axis, sources, targets, send_sems, recv_sems, offset):
         copy.wait()
 
 
-def widen_kernel(width, cells, out, y_out, y_in, mid, z_out, z_in, send_sems, recv_sems):
+def stack_rows(cells, groups):
+    per = cells.shape[0] // groups
+    return jnp.concatenate([cells[g * per : (g + 1) * per] for g in range(groups)], axis=2)
+
+
+def part_rows(packed, groups, width):
+    return jnp.concatenate(
+        [packed[:, :, g * width : (g + 1) * width] for g in range(groups)], axis=0
+    )
+
+
+def widen_kernel(
+    width, groups, cells, out, x_in, y_out, y_in, e_out, e_in, mid, z_out, z_in,
+    send_sems, recv_sems,
+):
     fields, size_x, size_y, size_z = cells.shape
     greet()
-    y_out[0] = cells[:, :, size_y - width :, :]
-    y_out[1] = cells[:, :, :width, :]
-    swap("gy", (y_out.at[0], y_out.at[1]), (y_in.at[0], y_in.at[1]), send_sems, recv_sems)
-    mid[:, width : width + size_x] = jnp.concatenate([y_in[0], cells[...], y_in[1]], axis=2)
-    swap(
+    x_copies = send(
         "gx",
-        (mid.at[:, pl.ds(size_x, width)], mid.at[:, pl.ds(width, width)]),
-        (mid.at[:, pl.ds(0, width)], mid.at[:, pl.ds(size_x + width, width)]),
+        (cells.at[:, pl.ds(size_x - width, width)], cells.at[:, pl.ds(0, width)]),
+        (x_in.at[0], x_in.at[1]),
         send_sems,
         recv_sems,
     )
+    y_out[0] = stack_rows(cells[:, :, size_y - width :, :], groups)
+    y_out[1] = stack_rows(cells[:, :, :width, :], groups)
+    y_copies = send("gy", (y_out.at[0], y_out.at[1]), (y_in.at[0], y_in.at[1]), send_sems, recv_sems)
+    for copy in x_copies:
+        copy.wait()
+    for k in range(2):
+        e_out[0, :, k * width : (k + 1) * width] = stack_rows(x_in[k, :, :, size_y - width :, :], groups)
+        e_out[1, :, k * width : (k + 1) * width] = stack_rows(x_in[k, :, :, :width, :], groups)
+    e_copies = send(
+        "gy", (e_out.at[0], e_out.at[1]), (e_in.at[0], e_in.at[1]), send_sems, recv_sems, 4
+    )
+    for copy in y_copies:
+        copy.wait()
+    mid[:, width : width + size_x] = jnp.concatenate(
+        [part_rows(y_in[0], groups, width), cells[...], part_rows(y_in[1], groups, width)], axis=2
+    )
+    for copy in e_copies:
+        copy.wait()
+    for k, start in ((0, 0), (1, width + size_x)):
+        rows = slice(k * width, (k + 1) * width)
+        mid[:, start : start + width] = jnp.concatenate(
+            [
+                part_rows(e_in[0, :, rows], groups, width),
+                x_in[k],
+                part_rows(e_in[1, :, rows], groups, width),
+            ],
+            axis=2,
+        )
     z_out[0] = jnp.concatenate([mid[c, :, :, size_z - width :] for c in range(fields)], axis=-1)
     z_out[1] = jnp.concatenate([mid[c, :, :, :width] for c in range(fields)], axis=-1)
     swap("gz", (z_out.at[0], z_out.at[1]), (z_in.at[0], z_in.at[1]), send_sems, recv_sems)
@@ -104,7 +146,7 @@
         in_specs=[pl.BlockSpec(memory_space=pltpu.VMEM)],
         out_specs=pl.BlockSpec(memory_space=pltpu.VMEM),
         scratch_shapes=[pltpu.VMEM(shape, jnp.float32) for shape in scratch]
-        + [pltpu.SemaphoreType.DMA((6,)), pltpu.SemaphoreType.DMA((6,))],
+        + [pltpu.SemaphoreType.DMA((8,)), pltpu.SemaphoreType.DMA((8,))],
         compiler_params=pltpu.CompilerParams(
             collective_id=number, has_side_effects=True, vmem_limit_bytes=40 * 1024 * 1024
         ),
@@ -114,15 +156,41 @@
 def with_halo(cells, width):
     fields, size_x, size_y, size_z = cells.shape
     wide_x, wide_y, wide_z = (size_x + 2 * width, size_y + 2 * width, size_z + 2 * width)
-    y_slab = (2, fields, size_x, width, size_z)
+    groups = 4 if fields % 4 == 0 else 1
+    x_slab = (2, fields, width, size_y, size_z)
+    y_slab = (2, fields // groups, size_x, groups * width, size_z)
+    e_slab = (2, fields // groups, 2 * width, groups * width, size_z)
     z_slab = (2, wide_x, wide_y, fields * width)
     return call_kernel(
-        functools.partial(widen_kernel, width),
+        functools.partial(widen_kernel, width, groups),
         cells,
         (fields, wide_x, wide_y, wide_z),
-        [y_slab, y_slab, (fields, wide_x, wide_y, size_z), z_slab, z_slab],
+        [x_slab, y_slab, y_slab, e_slab, e_slab, (fields, wide_x, wide_y, size_z), z_slab, z_slab],
         0,
     )
+
+
+def pack(slab, lanes):
+    planes = [slab[d, k] for d in range(slab.shape[0]) for k in range(slab.shape[1])]
+    rest = [plane[:, lanes:] for plane in planes]
+    free = lanes - len(planes) * rest[0].shape[1]
+    rest.append(jnp.zeros((planes[0].shape[0], free), jnp.float32))
+    return jnp.concatenate(
+        [plane[:, :lanes] for plane in planes] + [jnp.concatenate(rest, axis=1)], axis=0
+    )
+
+
+def unpack(packed, shape, lanes):
+    outer, inner, rows, width = shape
+    extra, total = width - lanes, outer * inner
+    rest = packed[total * rows :]
+    planes = [
+        jnp.concatenate(
+            [packed[i * rows : (i + 1) * rows], rest[:, i * extra : (i + 1) * extra]], axis=1
+        )
+        for i in range(total)
+    ]
+    return jnp.stack([jnp.stack(planes[d * inner : (d + 1) * inner]) for d in range(outer)])
 
 
 def add_ends(middle, before, after, dim, width):
@@ -145,41 +213,47 @@
     return jnp.concatenate(pieces, axis=dim)
 
 
-def spread_kernel(width, ghosts, out, z_out, z_in, mid, x_in, y_out, y_in, send_sems, recv_sems):
+def spread_kernel(
+    width, ghosts, out, z_out, z_in, x_out, x_in, y_out, y_in, send_sems, recv_sems
+):
     _, size_x, size_y, size_z = ghosts.shape
-    layers = width + 1
+    layers, lanes = width + 1, size_z - 2
     greet()
     z_out[0] = jnp.concatenate([ghosts[d, :, :, size_z - layers :] for d in range(3)], axis=-1)
     z_out[1] = jnp.concatenate([ghosts[d, :, :, :layers] for d in range(3)], axis=-1)
     swap("gz", (z_out.at[0], z_out.at[1]), (z_in.at[0], z_in.at[1]), send_sems, recv_sems)
+    parts = []
     for d in range(3):
         cut = slice(d * layers, (d + 1) * layers)
-        mid[d] = add_ends(ghosts[d], z_in[0, :, :, cut], z_in[1, :, :, cut], 2, width)
-    swap(
-        "gx",
-        (mid.at[:, pl.ds(size_x - layers, layers)], mid.at[:, pl.ds(0, layers)]),
-        (x_in.at[0], x_in.at[1]),
-        send_sems,
-        recv_sems,
-    )
-    summed = add_ends(mid[...], x_in[0], x_in[1], 1, width)
-    y_out[0] = summed[:, :, size_y - layers :, :]
-    y_out[1] = summed[:, :, :layers, :]
+        parts.append(add_ends(ghosts[d], z_in[0, :, :, cut], z_in[1, :, :, cut], 2, width))
+    summed = jnp.stack(parts)
+    x_out[0] = pack(summed[:, size_x - layers :], lanes)
+    x_out[1] = pack(summed[:, :layers], lanes)
+    swap("gx", (x_out.at[0], x_out.at[1]), (x_in.at[0], x_in.at[1]), send_sems, recv_sems)
+    shape = (3, layers, size_y, summed.shape[3])
+    summed = add_ends(
+        summed, unpack(x_in[0], shape, lanes), unpack(x_in[1], shape, lanes), 1, width
+    )
+    y_out[0] = pack(summed[:, :, size_y - layers :, :], lanes)
+    y_out[1] = pack(summed[:, :, :layers, :], lanes)
     swap("gy", (y_out.at[0], y_out.at[1]), (y_in.at[0], y_in.at[1]), send_sems, recv_sems)
-    out[...] = add_ends(summed, y_in[0], y_in[1], 2, width)
+    shape = (3, summed.shape[1], layers, summed.shape[3])
+    out[...] = add_ends(
+        summed, unpack(y_in[0], shape, lanes), unpack(y_in[1], shape, lanes), 2, width
+    )
 
 
 def spread_sums(ghosts, width):
     _, size_x, size_y, size_z = ghosts.shape
     more = 2 * (width - 1)
     z_slab = (2, size_x, size_y, 3 * (width + 1))
-    x_slab = (2, 3, width + 1, size_y, size_z + more)
-    y_slab = (2, 3, size_x + more, width + 1, size_z + more)
+    x_slab = (2, (3 * (width + 1) + 1) * size_y, size_z - 2)
+    y_slab = (2, (3 * (size_x + more) + 1) * (width + 1), size_z - 2)
     return call_kernel(
         functools.partial(spread_kernel, width),
         ghosts,
         (3, size_x + more, size_y + more, size_z + more),
-        [z_slab, z_slab, (3, size_x, size_y, size_z + more), x_slab, y_slab, y_slab],
+        [z_slab, z_slab, x_slab, x_slab, y_slab, y_slab],
         width,
     )
 

time: 106 us -> 95.1 us (0.90)
  Pallas kernels: 58.1 us -> 47 us
    pallas_call x3, Pallas kernels: 58.1 us -> 47 us  [call_kernel(): pl.pallas_call(kernel, out_shape=jax.ShapeDtypeStruct(out_shape, jnp.floa...]
  transfers between devices with their start and end apart: 1 -> 1, of which waited for: 0 -> 0; matrix products, arithmetic and copies ran while one was open for 9% -> 10% of each run, Pallas kernels for 23% -> 22%
where the time goes in v4:
time: 95.1 us; the launch traced here: 94.2 us
  Pallas kernels  47 us (49%)
  other arithmetic  24.2 us (25%)
  matrix products  9.11 us (10%)
  starting transfers between devices  6.32 us (7%)
  local copies, waits for them, and re-layouts  6.17 us (6%)
  between operations  1.38 us (1%)
    pallas_call x3, Pallas kernels, call_kernel(): pl.pallas_call(kernel, out_shape=jax.ShapeDtypeStruct(out_shape, jnp.floa...  47 us
    mul x4, other arithmetic, collide(): equilibrium = weights[i] * baseline  9.48 us
    all_to_all x1, starting transfers between devices, per_device(): lax.all_to_all(send_floats, 'gx', split_axis=0, concat_axis=0, tiled=True)  6.32 us
    dot_general x2, matrix products, per_device(): jnp.einsum('nz,dkz->dnk', tables[2], lines, precision=lax.Precision.HIGH)  4.64 us
    dot_general x2, matrix products, per_device(): jnp.einsum('dnk,nz->dkz', pushed[:, :, None] * across[None], tables[2], p...  4.47 us
    another operation x4, other arithmetic, moments(): return (density, jnp.stack(components))  4.01 us
    unnamed x68, local copies, waits for them, and re-layouts  3.37 us
    squeeze x2, other arithmetic, per_device(): fields = [wide[i] for i in range(19)]  2.13 us
  transfers between devices with their start and end apart: 1, of which 0 were waited for; matrix products, arithmetic and copies ran while one was open for 10% of the time, Pallas kernels for 22%

profile of v4, /device:TPU:0, one launch (start us, length us, event | category | flops | bytes accessed | tf_op | source)
XLA Modules:
  0.0 94.2 jit_solution(8747767399196591476)
XLA Ops:
  0.6 0.7 fusion.356
  1.4 0.8 select_reduce_fusion.1
  2.2 0.7 multiply_add_fusion
  2.9 0.1 select_reduce_fusion
  3.0 0.1 fusion.355
  3.1 0.8 copy.17
  3.9 0.8 copy.16
  4.6 0.8 select_convert_fusion
  5.4 0.7 pad_maximum_fusion.3
  6.1 0.6 gather_fusion
  6.7 0.8 select_select_fusion
  7.5 6.3 %all-to-all-start = ((f32[32,8,128]{2,1,0:T(8,128)}), f32[32,8,128]{2,1,0:T(8,128)S(1)}, u32[]{:S(2)}, u32[]{:S(2)}) async-start(f32[32,8,128]{2,1,0:T(8,128)} %select_select_fusion), calls=%async_computation | async-start | bytes 262144 | tf_op jit(solution)/shard_map/all_to_all | solution.py:344
  13.9 0.7 multiply_bitcast_fusion
  14.6 1.0 %pad_maximum_fusion.cells = f32[20,4,8,128]{3,2,1,0:T(8,128)S(1)} fusion(f32[1,4,8,128]{3,2,1,0:T(8,128)S(1)} %multiply_bitcast_fusion, f32[19,4,8,128]{3,2,1,0:T(8,128)} %param.8), kind=kLoop, calls=%fused_computation.43 | loop fusion | flops 81920 | bytes 655360 | tf_op jit(solution)/shard_map/concatenate | solution.py:366
  15.6 20.9 %shard_map.95 = f32[20,8,12,132]{3,2,1,0:T(8,128)S(1)} custom-call(f32[20,4,8,128]{3,2,1,0:T(8,128)S(1)} %pad_maximum_fusion.cells), custom_call_target="tpu_custom_call" | custom-call | tf_op jit(solution)/shard_map/pallas_call | solution.py:143
  36.5 0.8 add_add_fusion
  37.3 1.2 %fusion.48 = (f32[8,12,132]{2,1,0:T(8,128)}, f32[8,12,132]{2,1,0:T(8,128)S(1)}, f32[8,12,132]{2,1,0:T(8,128)}, f32[8,12,132]{2,1,0:T(8,128)}, f32[8,12,132]{2,1,0:T(8,128)}) fusion(f32[20,8,12,132]{3,2,1,0:T(8,128)S(1)} %shard_map.95), kind=kLoop, calls=%fused_computation.93 | loop fusion | flops 899712 | bytes 1216512 | tf_op jit(solution)/shard_map/mul | solution.py:294
  38.5 1.1 %slice_bitcast_fusion.5 = (f32[8,12,132]{2,1,0:T(8,128)}, f32[1,8,12,132]{3,2,1,0:T(8,128)S(1)}, f32[8,12,132]{2,1,0:T(8,128)}, f32[8,12,132]{2,1,0:T(8,128)}, f...) fusion(f32[20,8,12,132]{3,2,1,0:T(8,128)S(1)} %shard_map.95), kind=kLoop, calls=%fused_computation.142 | loop fusion | flops 177408 | bytes 1216512 | tf_op jit(solution)/shard_map/squeeze | solution.py:367
  39.6 1.1 %slice_bitcast_fusion.11 = (f32[8,12,132]{2,1,0:T(8,128)}, f32[1,8,12,132]{3,2,1,0:T(8,128)S(1)}, f32[8,12,132]{2,1,0:T(8,128)}, f32[8,12,132]{2,1,0:T(8,128)}, ...) fusion(f32[20,8,12,132]{3,2,1,0:T(8,128)S(1)} %shard_map.95), kind=kLoop, calls=%fused_computation.148 | loop fusion | flops 177408 | bytes 1216512 | tf_op jit(solution)/shard_map/squeeze | solution.py:367
  40.6 0.1 pad_maximum_fusion.1
  40.8 0.7 reshape.363
  41.5 0.0 copy-done
  41.5 2.6 %fusion.78 = (f32[8,12,132]{2,1,0:T(8,128)}, f32[8,12,132]{2,1,0:T(8,128)}, f32[8,12,132]{2,1,0:T(8,128)}, f32[8,12,132]{2,1,0:T(8,128)}, f32[8,12,132]{2,1,0:T(...) fusion(f32[8,12,132]{2,1,0:T(8,128)S(1)} %get-tuple-element.46,, ...), kind=kLoop, calls=%fused_computation.123 | loop fusion | flops 1495296 | bytes 1165824 | tf_op jit(solution)/shard_map/mul | solution.py:294
  44.1 0.1 broadcast_subtract_fusion.1
  44.2 0.0 all-to-all-done
  44.2 0.1 fusion.404
  44.3 0.1 compare_select_fusion.2
  44.4 0.0 copy-start.26
  44.5 0.0 copy-start.28
  44.6 0.0 copy-start.25
  44.6 0.1 broadcast_multiply_fusion
  44.7 0.1 mul.1044
  44.9 0.0 copy-start.30
  44.9 0.6 copy-done.25
  45.5 1.9 %fusion.14 = f32[3,4096]{1,0:T(4,128)S(1)} fusion(f32[4096,60]{0,1:T(8,128)S(1)} %mul.1044, f32[3,60,130]{2,1,0:T(8,128)S(1)} %copy-done.25, f32[4096]{0:T(1024)S(1)} %bitcast.310, s32[4096]{0:T(1024)S(1)} %get-tuple-element.154, f32[4096]{0:T(1024)S(1)} %broadcast_subtract_fusion.4, s32[4096]{0:T(1024)S(1)} %get-tuple-element.153), kind=kOutput, calls=%fused_computation.20 | convolution fusion | flops 579203072 | bytes 1191328 | tf_op jit(solution)/shard_map/nz,dkz->dnk/dot_general | solution.py:376
  47.4 0.0 copy-start.23
  47.5 0.0 copy-done.26
  47.5 0.5 copy-done.23
  48.1 2.6 %fusion.4 = f32[3,60,130]{2,1,0:T(8,128)} fusion(f32[3,4096]{1,0:T(4,128)S(1)} %negate_bitcast_fusion.1, f32[4096,60]{0,1:T(8,128)S(1)} %mul.1044, f32[4096]{0:T(1024)S(1)} %bitcast.311, s32[4096]{0:T(1024)S(1)} %get-tuple-element.154, f32[4096]{0:T(1024)S(1)} %broadcast_subtract_fusion.4, s32[4096]{0:T(1024)S(1)} %get-tuple-element.153), kind=kOutput, calls=%fused_computation.7 | convolution fusion | flops 578478080 | bytes 1191328 | tf_op jit(solution)/shard_map/dnk,nz->dkz/dot_general | solution.py:384
  50.7 1.1 %reshape.365.ghosts = f32[3,6,10,130]{3,2,1,0:T(8,128)S(1)} reshape(f32[3,60,130]{2,1,0:T(8,128)} %fusion.4) | data formatting | bytes 187200 | tf_op jit(solution)/shard_map/reshape | solution.py:388
  51.8 0.0 copy-start.12
  51.8 0.0 copy-start.13
  51.8 0.0 copy-start.14
  51.9 0.0 copy-start.15
  51.9 0.0 copy-start.16
  51.9 0.0 copy-start.17
  51.9 0.0 copy-start.18
  51.9 0.0 copy-start.19
  51.9 0.0 copy-start.21
  51.9 13.4 %shard_map.96 = f32[3,8,12,132]{3,2,1,0:T(8,128)S(1)} custom-call(f32[3,6,10,130]{3,2,1,0:T(8,128)S(1)} %reshape.365.ghosts), custom_call_target="tpu_custom_call" | custom-call | tf_op jit(solution)/shard_map/pallas_call | solution.py:143
  65.7 5.2 %fusion.82 = (f32[6,10,130]{2,1,0:T(8,128)}, f32[6,10,130]{2,1,0:T(8,128)}, f32[6,10,130]{2,1,0:T(8,128)S(1)}, f32[6,10,130]{2,1,0:T(8,128)}, f32[6,10,130]{2,1,...) fusion(f32[8,12,132]{2,1,0:T(8,128)S(1)} %get-tuple-element.74,, ...), kind=kLoop, calls=%fused_computation.161 | loop fusion | flops 1817400 | bytes 4586400 | tf_op jit(solution)/shard_map/mul | solution.py:294
  70.9 0.2 stack.32
  71.2 0.0 copy-start.29
  71.2 0.0 copy-start.31
  71.2 2.7 %fusion.17 = f32[3,4096]{1,0:T(4,128)S(1)} fusion(f32[4096,60]{0,1:T(8,128)S(1)} %mul.1044, f32[4096]{0:T(1024)S(1)} %bitcast.312, s32[4096]{0:T(1024)} %copy-done.28, f32[4096]{0:T(1024)} %copy-done.30, s32[4096]{0:T(1024)} %copy-done.26, f32[1,60,130]{2,1,0:T(8,128)S(1)} %stack.33, f32[1,60,130]{2,1,0:T(8,128)S(1)} %stack.32, f32[1,60,130]{2,1,0:T(8,128)S(1)} %stack.31), kind=kOutput, calls=%fused_computation.21 | convolution fusion | flops 579249856 | bytes 1191328 | tf_op jit(solution)/shard_map/nz,dkz->dnk/dot_general | solution.py:376
  73.9 0.1 multiply_select_fusion
  74.0 1.9 %fusion.2 = f32[3,60,130]{2,1,0:T(8,128)S(1)} fusion(f32[3,4096]{1,0:T(4,128)S(1)} %get-tuple-element.112, f32[4096,60]{0,1:T(8,128)S(1)} %mul.1044, f32[4096]{0:T(1024)S(1)} %bitcast.313, s32[4096]{0:T(1024)S(1)} %copy-done.29, f32[4096]{0:T(1024)S(1)} %copy-done.31, s32[4096]{0:T(1024)S(1)} %copy-done.27), kind=kOutput, calls=%fused_computation.5 | convolution fusion | flops 578478080 | bytes 1191328 | tf_op jit(solution)/shard_map/dnk,nz->dkz/dot_general | solution.py:384
  76.0 12.6 %shard_map.97 = f32[3,6,10,130]{3,2,1,0:T(8,128)S(1)} custom-call(f32[3,6,10,130]{3,2,1,0:T(8,128)S(1)} %reshape.367.ghosts), custom_call_target="tpu_custom_call" | custom-call | tf_op jit(solution)/shard_map/pallas_call | solution.py:143
  88.7 0.4 fusion.114
  89.1 0.6 copy.18
  89.7 1.6 %fusion.345 = (f32[1,4,8,128]{3,2,1,0:T(8,128)S(1)}, f32[4,8,128]{2,1,0:T(8,128)S(1)}, f32[4,8,128]{2,1,0:T(8,128)S(1)}, f32[4,8,128]{2,1,0:T(8,128)S(1)}, f32[4...) fusion(f32[6,10,130]{2,1,0:T(8,128)} %get-tuple-element.21, ...), kind=kLoop, calls=%fused_computation.593 | loop fusion | flops 417792 | bytes 1261568 | tf_op jit(solution)/shard_map/stack | solution.py:282
  91.3 1.3 %fusion.284 = (f32[1,4,8,128]{3,2,1,0:T(8,128)S(1)}, f32[4,8,128]{2,1,0:T(8,128)S(1)}, f32[4,8,128]{2,1,0:T(8,128)S(1)}, f32[4,8,128]{2,1,0:T(8,128)S(1)}, f32[4,8,128]{2,1,0:T(8,128)S(1)}) fusion(f32[4,8,128]{2,1,0:T(8,128)S(1)} %get-tuple-element.12, f32[4,8,128]{2,1,0:T(8,128)S(1)} %get-tuple-element.11, f32[4,8,128]{2,1,0:T(8,128)S(1)} %get-tuple-element.10, ...), kind=kLoop, calls=%fused_computation.492 | loop fusion | flops 266240 | bytes 802816 | tf_op jit(solution)/shard_map/stack | solution.py:282
  92.5 1.0 %fusion.244 = f32[1,4,8,128]{3,2,1,0:T(8,128)S(1)} fusion(f32[4,8,128]{2,1,0:T(8,128)S(1)} %get-tuple-element.44, f32[4,8,128]{2,1,0:T(8,128)S(1)} %get-tuple-element.43, f32[4,8,128]{2,1,0:T(8,128)S(1)} %get-tuple-element.42, f32[4,8,128]{2,1,0:T(8,128)S(1)} %get-tuple-element.16, f32[4,8,128]{2,1,0:T(8,128)S(1)} %get-tuple-element.15, ...), kind=kLoop, calls=%fused_computation.428 | loop fusion | flops 114688 | bytes 344064 | tf_op jit(solution)/shard_map/stack | solution.py:282
  93.6 0.6 maximum_multiply_fusion
  (65 shorter events, 0.5 us)
Async XLA Ops:
  7.5 36.7 %all-to-all-start = ((f32[32,8,128]{2,1,0:T(8,128)}), f32[32,8,128]{2,1,0:T(8,128)S(1)}, u32[]{:S(2)}, u32[]{:S(2)}) async-start(f32[32,8,128]{2,1,0:T(8,128)} %select_select_fusion), calls=%async_computation | async-start | bytes 262144 | tf_op jit(solution)/shard_map/all_to_all | solution.py:344
  38.5 3.0 %copy-start = (f32[8,12,132]{2,1,0:T(8,128)}, f32[8,12,132]{2,1,0:T(8,128)S(1)}, u32[]{:S(2)}) copy-start(f32[8,12,132]{2,1,0:T(8,128)S(1)} %get-tuple-element.46) | copy-start | bytes 152068
  44.4 3.1 %copy-start.26 = (s32[4096]{0:T(1024)}, s32[4096]{0:T(1024)S(1)}, u32[]{:S(2)}) copy-start(s32[4096]{0:T(1024)S(1)} %get-tuple-element.153) | copy-start | bytes 49156
  44.5 3.1 %copy-start.28 = (s32[4096]{0:T(1024)}, s32[4096]{0:T(1024)S(1)}, u32[]{:S(2)}) copy-start(s32[4096]{0:T(1024)S(1)} %get-tuple-element.154) | copy-start | bytes 49156
  44.6 0.9 copy-start.25
  44.9 2.6 %copy-start.30 = (f32[4096]{0:T(1024)}, f32[4096]{0:T(1024)S(1)}, u32[]{:S(2)}) copy-start(f32[4096]{0:T(1024)S(1)} %broadcast_subtract_fusion.4) | copy-start | bytes 49156
  47.4 0.6 copy-start.23
  50.6 14.8 %copy-start.1 = (f32[8,12,132]{2,1,0:T(8,128)S(1)}, f32[8,12,132]{2,1,0:T(8,128)}, u32[]{:S(2)}) copy-start(f32[8,12,132]{2,1,0:T(8,128)} %copy-done) | copy-start | bytes 152068
  50.7 14.8 %copy-start.2 = (f32[8,12,132]{2,1,0:T(8,128)S(1)}, f32[8,12,132]{2,1,0:T(8,128)}, u32[]{:S(2)}) copy-start(f32[8,12,132]{2,1,0:T(8,128)} %get-tuple-element.62) | copy-start | bytes 152068
  50.7 14.8 %copy-start.3 = (f32[8,12,132]{2,1,0:T(8,128)S(1)}, f32[8,12,132]{2,1,0:T(8,128)}, u32[]{:S(2)}) copy-start(f32[8,12,132]{2,1,0:T(8,128)} %get-tuple-element.64) | copy-start | bytes 152068
  50.7 14.8 %copy-start.4 = (f32[8,12,132]{2,1,0:T(8,128)S(1)}, f32[8,12,132]{2,1,0:T(8,128)}, u32[]{:S(2)}) copy-start(f32[8,12,132]{2,1,0:T(8,128)} %get-tuple-element.65) | copy-start | bytes 152068
  50.7 14.8 %copy-start.5 = (f32[8,12,132]{2,1,0:T(8,128)S(1)}, f32[8,12,132]{2,1,0:T(8,128)}, u32[]{:S(2)}) copy-start(f32[8,12,132]{2,1,0:T(8,128)} %get-tuple-element.66) | copy-start | bytes 152068
  50.7 14.8 %copy-start.6 = (f32[8,12,132]{2,1,0:T(8,128)S(1)}, f32[8,12,132]{2,1,0:T(8,128)}, u32[]{:S(2)}) copy-start(f32[8,12,132]{2,1,0:T(8,128)} %get-tuple-element.67) | copy-start | bytes 152068
  50.7 14.8 %copy-start.7 = (f32[8,12,132]{2,1,0:T(8,128)S(1)}, f32[8,12,132]{2,1,0:T(8,128)}, u32[]{:S(2)}) copy-start(f32[8,12,132]{2,1,0:T(8,128)} %get-tuple-element.68) | copy-start | bytes 152068
  50.7 14.8 %copy-start.8 = (f32[8,12,132]{2,1,0:T(8,128)S(1)}, f32[8,12,132]{2,1,0:T(8,128)}, u32[]{:S(2)}) copy-start(f32[8,12,132]{2,1,0:T(8,128)} %get-tuple-element.69) | copy-start | bytes 152068
  50.7 14.8 %copy-start.9 = (f32[8,12,132]{2,1,0:T(8,128)S(1)}, f32[8,12,132]{2,1,0:T(8,128)}, u32[]{:S(2)}) copy-start(f32[8,12,132]{2,1,0:T(8,128)} %get-tuple-element.70) | copy-start | bytes 152068
  50.7 14.8 %copy-start.10 = (f32[8,12,132]{2,1,0:T(8,128)S(1)}, f32[8,12,132]{2,1,0:T(8,128)}, u32[]{:S(2)}) copy-start(f32[8,12,132]{2,1,0:T(8,128)} %get-tuple-element.52) | copy-start | bytes 152068
  50.7 14.8 %copy-start.11 = (f32[8,12,132]{2,1,0:T(8,128)S(1)}, f32[8,12,132]{2,1,0:T(8,128)}, u32[]{:S(2)}) copy-start(f32[8,12,132]{2,1,0:T(8,128)} %get-tuple-element.54) | copy-start | bytes 152068
  50.7 14.8 %copy-start.20 = (f32[8,12,132]{2,1,0:T(8,128)S(1)}, f32[8,12,132]{2,1,0:T(8,128)}, u32[]{:S(2)}) copy-start(f32[8,12,132]{2,1,0:T(8,128)} %get-tuple-element.45) | copy-start | bytes 152068
  51.8 13.7 %copy-start.12 = (f32[8,12,132]{2,1,0:T(8,128)S(1)}, f32[8,12,132]{2,1,0:T(8,128)}, u32[]{:S(2)}) copy-start(f32[8,12,132]{2,1,0:T(8,128)} %get-tuple-element.55) | copy-start | bytes 152068
  51.8 13.7 %copy-start.13 = (f32[8,12,132]{2,1,0:T(8,128)S(1)}, f32[8,12,132]{2,1,0:T(8,128)}, u32[]{:S(2)}) copy-start(f32[8,12,132]{2,1,0:T(8,128)} %get-tuple-element.56) | copy-start | bytes 152068
  51.8 13.7 %copy-start.14 = (f32[8,12,132]{2,1,0:T(8,128)S(1)}, f32[8,12,132]{2,1,0:T(8,128)}, u32[]{:S(2)}) copy-start(f32[8,12,132]{2,1,0:T(8,128)} %get-tuple-element.57) | copy-start | bytes 152068
  51.9 13.7 %copy-start.15 = (f32[8,12,132]{2,1,0:T(8,128)S(1)}, f32[8,12,132]{2,1,0:T(8,128)}, u32[]{:S(2)}) copy-start(f32[8,12,132]{2,1,0:T(8,128)} %get-tuple-element.58) | copy-start | bytes 152068
  51.9 13.7 %copy-start.16 = (f32[8,12,132]{2,1,0:T(8,128)S(1)}, f32[8,12,132]{2,1,0:T(8,128)}, u32[]{:S(2)}) copy-start(f32[8,12,132]{2,1,0:T(8,128)} %get-tuple-element.59) | copy-start | bytes 152068
  51.9 13.7 %copy-start.17 = (f32[8,12,132]{2,1,0:T(8,128)S(1)}, f32[8,12,132]{2,1,0:T(8,128)}, u32[]{:S(2)}) copy-start(f32[8,12,132]{2,1,0:T(8,128)} %get-tuple-element.60) | copy-start | bytes 152068
  51.9 13.7 %copy-start.18 = (f32[8,12,132]{2,1,0:T(8,128)S(1)}, f32[8,12,132]{2,1,0:T(8,128)}, u32[]{:S(2)}) copy-start(f32[8,12,132]{2,1,0:T(8,128)} %get-tuple-element.61) | copy-start | bytes 152068
  51.9 13.7 %copy-start.19 = (f32[8,12,132]{2,1,0:T(8,128)S(1)}, f32[8,12,132]{2,1,0:T(8,128)}, u32[]{:S(2)}) copy-start(f32[8,12,132]{2,1,0:T(8,128)} %get-tuple-element.73) | copy-start | bytes 152068
  51.9 13.7 %copy-start.21 = (f32[8,12,132]{2,1,0:T(8,128)S(1)}, f32[8,12,132]{2,1,0:T(8,128)}, u32[]{:S(2)}) copy-start(f32[8,12,132]{2,1,0:T(8,128)} %get-tuple-element.71) | copy-start | bytes 152068
  71.1 2.8 %copy-start.24 = (f32[3,4096]{1,0:T(4,128)S(1)}, f32[3,4096]{1,0:T(4,128)}, u32[]{:S(2)}) copy-start(f32[3,4096]{1,0:T(4,128)} %copy-done.23) | copy-start | bytes 147460
  71.1 2.8 %copy-start.27 = (s32[4096]{0:T(1024)S(1)}, s32[4096]{0:T(1024)}, u32[]{:S(2)}) copy-start(s32[4096]{0:T(1024)} %copy-done.26) | copy-start | bytes 49156
  71.2 2.8 %copy-start.29 = (s32[4096]{0:T(1024)S(1)}, s32[4096]{0:T(1024)}, u32[]{:S(2)}) copy-start(s32[4096]{0:T(1024)} %copy-done.28) | copy-start | bytes 49156
  71.2 2.8 %copy-start.31 = (f32[4096]{0:T(1024)S(1)}, f32[4096]{0:T(1024)}, u32[]{:S(2)}) copy-start(f32[4096]{0:T(1024)} %copy-done.30) | copy-start | bytes 49156
  75.9 12.8 %copy-start.22 = (f32[6,10,130]{2,1,0:T(8,128)S(1)}, f32[6,10,130]{2,1,0:T(8,128)}, u32[]{:S(2)}) copy-start(f32[6,10,130]{2,1,0:T(8,128)} %get-tuple-element.18) | copy-start | bytes 93604

commit v5 on v4

--- a/solution.py
+++ b/solution.py
@@ -49,12 +49,14 @@
     return tuple(place)
 
 
-def greet():
+def greet(peers=1):
     barrier = pltpu.get_barrier_semaphore()
+    for step in range(1, peers):
+        pl.semaphore_signal(barrier, inc=1, device_id=neighbour("gx", step), device_id_type=MESH)
     for axis in AXES:
         for step in (1, -1):
             pl.semaphore_signal(barrier, inc=1, device_id=neighbour(axis, step), device_id_type=MESH)
-    pl.semaphore_wait(barrier, 6)
+    pl.semaphore_wait(barrier, 5 + peers)
 
 
 def send(axis, sources, targets, send_sems, recv_sems, offset=0):
@@ -91,11 +93,13 @@
 
 
 def widen_kernel(
-    width, groups, cells, out, x_in, y_out, y_in, e_out, e_in, mid, z_out, z_in,
-    send_sems, recv_sems,
+    width, groups, peers, cells, blocks, out, got, x_in, y_out, y_in, e_out, e_in, mid, z_out,
+    z_in, arrived, send_sems, recv_sems, give_sems, take_sems,
 ):
     fields, size_x, size_y, size_z = cells.shape
-    greet()
+    capacity = blocks.shape[0] // peers
+    me = lax.axis_index("gx")
+    greet(peers)
     x_copies = send(
         "gx",
         (cells.at[:, pl.ds(size_x - width, width)], cells.at[:, pl.ds(0, width)]),
@@ -103,6 +107,19 @@
         send_sems,
         recv_sems,
     )
+    block_copies = []
+    for step in range(1, peers):
+        copy = pltpu.make_async_remote_copy(
+            src_ref=blocks.at[pl.ds(lax.rem(me + step, peers) * capacity, capacity)],
+            dst_ref=arrived.at[pl.ds(me * capacity, capacity)],
+            send_sem=give_sems.at[step - 1],
+            recv_sem=take_sems.at[step - 1],
+            device_id=neighbour("gx", step),
+            device_id_type=MESH,
+        )
+        copy.start()
+        block_copies.append(copy)
+    arrived[pl.ds(me * capacity, capacity)] = blocks[pl.ds(me * capacity, capacity)]
     y_out[0] = stack_rows(cells[:, :, size_y - width :, :], groups)
     y_out[1] = stack_rows(cells[:, :, :width, :], groups)
     y_copies = send("gy", (y_out.at[0], y_out.at[1]), (y_in.at[0], y_in.at[1]), send_sems, recv_sems)
@@ -137,23 +154,28 @@
     for c in range(fields):
         cut = slice(c * width, (c + 1) * width)
         out[c] = jnp.concatenate([z_in[0, :, :, cut], mid[c], z_in[1, :, :, cut]], axis=-1)
-
-
-def call_kernel(kernel, operand, out_shape, scratch, number):
+    for copy in block_copies:
+        copy.wait()
+    got[...] = arrived[...]
+
+
+def call_kernel(kernel, operands, out_shapes, scratch, number, peers=1):
+    vmem = pl.BlockSpec(memory_space=pltpu.VMEM)
+    counts = (8, 8) + ((peers - 1,) * 2 if peers > 1 else ())
     return pl.pallas_call(
         kernel,
-        out_shape=jax.ShapeDtypeStruct(out_shape, jnp.float32),
-        in_specs=[pl.BlockSpec(memory_space=pltpu.VMEM)],
-        out_specs=pl.BlockSpec(memory_space=pltpu.VMEM),
+        out_shape=[jax.ShapeDtypeStruct(shape, jnp.float32) for shape in out_shapes],
+        in_specs=[vmem for _ in operands],
+        out_specs=[vmem for _ in out_shapes],
         scratch_shapes=[pltpu.VMEM(shape, jnp.float32) for shape in scratch]
-        + [pltpu.SemaphoreType.DMA((8,)), pltpu.SemaphoreType.DMA((8,))],
+        + [pltpu.SemaphoreType.DMA((count,)) for count in counts],
         compiler_params=pltpu.CompilerParams(
             collective_id=number, has_side_effects=True, vmem_limit_bytes=40 * 1024 * 1024
         ),
-    )(operand)
-
-
-def with_halo(cells, width):
+    )(*operands)
+
+
+def with_halo(cells, blocks, peers, width):
     fields, size_x, size_y, size_z = cells.shape
     wide_x, wide_y, wide_z = (size_x + 2 * width, size_y + 2 * width, size_z + 2 * width)
     groups = 4 if fields % 4 == 0 else 1
@@ -162,11 +184,13 @@
     e_slab = (2, fields // groups, 2 * width, groups * width, size_z)
     z_slab = (2, wide_x, wide_y, fields * width)
     return call_kernel(
-        functools.partial(widen_kernel, width, groups),
-        cells,
-        (fields, wide_x, wide_y, wide_z),
-        [x_slab, y_slab, y_slab, e_slab, e_slab, (fields, wide_x, wide_y, size_z), z_slab, z_slab],
+        functools.partial(widen_kernel, width, groups, peers),
+        (cells, blocks),
+        ((fields, wide_x, wide_y, wide_z), blocks.shape),
+        [x_slab, y_slab, y_slab, e_slab, e_slab, (fields, wide_x, wide_y, size_z), z_slab, z_slab]
+        + [blocks.shape],
         0,
+        peers,
     )
 
 
@@ -251,11 +275,11 @@
     y_slab = (2, (3 * (size_x + more) + 1) * (width + 1), size_z - 2)
     return call_kernel(
         functools.partial(spread_kernel, width),
-        ghosts,
-        (3, size_x + more, size_y + more, size_z + more),
+        (ghosts,),
+        ((3, size_x + more, size_y + more, size_z + more),),
         [z_slab, z_slab, x_slab, x_slab, y_slab, y_slab],
         width,
-    )
+    )[0]
 
 
 def project(vector, direction):
@@ -341,7 +365,10 @@
     )
     empty = jnp.where(jnp.arange(8) == 7, -1.0, 0.0).astype(jnp.float32)[None, :, None]
     send_floats = jnp.where(filled[:, None, None], jnp.take(floats, source, axis=0), empty)
-    got_floats = lax.all_to_all(send_floats, "gx", split_axis=0, concat_axis=0, tiled=True)
+    gray = solid_class.astype(jnp.float32) * 0.25
+    wide, got_floats = with_halo(
+        jnp.concatenate([populations, gray[None]]), send_floats, peers, STEPS
+    )
     offset = got_floats[:, 0:3, :]
     velocity = got_floats[:, 3:6, :]
     drag_rate = got_floats[:, 6, :]
@@ -362,8 +389,6 @@
             + jnp.where(grid == farther[:, None], jnp.abs(displace)[:, None], 0.0)
         )
     across = (tables[0][:, :, None] * tables[1][:, None, :]).reshape(slots * rows_block, -1)
-    gray = solid_class.astype(jnp.float32) * 0.25
-    wide = with_halo(jnp.concatenate([populations, gray[None]]), STEPS)
     fields = [wide[i] for i in range(19)]
     gray_fraction = wide[19]
     for repeat in range(STEPS):

time: 95.1 us -> 95.6 us (level)
  starting transfers between devices: 6.32 us -> 0 us
  Pallas kernels: 47 us -> 50.2 us
  matrix products: 9.11 us -> 10.5 us
  other arithmetic: 24.2 us -> 25.5 us
  local copies, waits for them, and re-layouts: 6.17 us -> 7.27 us
    all_to_all x1 -> x0, starting transfers between devices: 6.32 us -> none  [per_device(): lax.all_to_all(send_floats, 'gx', split_axis=0, concat_axis=0, tiled=True)]
    pallas_call x3, Pallas kernels: 47 us -> 50.2 us  [call_kernel(): pl.pallas_call(kernel, out_shape=[jax.ShapeDtypeStruct(shape, jnp.float32...]
    mul x1, local copies, waits for them, and re-layouts: 0.14 us -> 2.53 us  [per_device(): tables[0][:, :, None] * tables[1][:, None, :]]
    dot_general x2, matrix products: 4.64 us -> 6.02 us  [per_device(): jnp.einsum('nz,dkz->dnk', tables[2], lines, precision=lax.Precision.HIGH)]
    mul x4, other arithmetic: 9.48 us -> 8.18 us  [collide(): equilibrium = weights[i] * baseline]
    mul x1, other arithmetic: 0.13 us -> 1.33 us  [per_device(): tables[0][:, :, None] * tables[1][:, None, :]]
    unnamed x68 -> x80, local copies, waits for them, and re-layouts: 3.37 us -> 2.98 us
  transfers between devices with their start and end apart: 1 -> 0, of which waited for: 0 -> 0; matrix products, arithmetic and copies ran while one was open for 10% -> 0% of each run, Pallas kernels for 22% -> 0%
where the time goes in v5:
time: 95.6 us; the launch traced here: 94.8 us
  Pallas kernels  50.2 us (53%)
  other arithmetic  25.5 us (27%)
  matrix products  10.5 us (11%)
  local copies, waits for them, and re-layouts  7.27 us (8%)
  between operations  1.4 us (1%)
    pallas_call x3, Pallas kernels, call_kernel(): pl.pallas_call(kernel, out_shape=[jax.ShapeDtypeStruct(shape, jnp.float32...  50.2 us
    mul x4, other arithmetic, collide(): equilibrium = weights[i] * baseline  8.18 us
    dot_general x2, matrix products, per_device(): jnp.einsum('nz,dkz->dnk', tables[2], lines, precision=lax.Precision.HIGH)  6.02 us
    dot_general x2, matrix products, per_device(): jnp.einsum('dnk,nz->dkz', pushed[:, :, None] * across[None], tables[2], p...  4.47 us
    another operation x4, other arithmetic, moments(): return (density, jnp.stack(components))  4.1 us
    unnamed x80, local copies, waits for them, and re-layouts  2.98 us
    mul x1, local copies, waits for them, and re-layouts, per_device(): tables[0][:, :, None] * tables[1][:, None, :]  2.53 us
    squeeze x2, other arithmetic, per_device(): fields = [wide[i] for i in range(19)]  2.07 us

profile of v5, /device:TPU:0, one launch (start us, length us, event | category | flops | bytes accessed | tf_op | source)
XLA Modules:
  0.0 94.8 jit_solution(591203189282614324)
XLA Ops:
  0.6 0.7 multiply_bitcast_fusion
  1.4 1.0 %pad_maximum_fusion.cells = f32[20,4,8,128]{3,2,1,0:T(8,128)S(1)} fusion(f32[1,4,8,128]{3,2,1,0:T(8,128)S(1)} %multiply_bitcast_fusion, f32[19,4,8,128]{3,2,1,0:T(8,128)} %param.8), kind=kLoop, calls=%fused_computation.43 | loop fusion | flops 81920 | bytes 655360 | tf_op jit(solution)/shard_map/concatenate | solution.py:370
  2.3 0.8 select_convert_fusion
  3.1 0.8 copy.15
  3.9 0.8 copy.14
  4.6 0.7 pad_maximum_fusion.3
  5.4 0.7 fusion.356
  6.1 0.8 select_reduce_fusion.1
  7.0 0.7 multiply_add_fusion
  7.6 0.1 select_reduce_fusion
  7.7 0.6 gather_fusion
  8.4 0.1 fusion.355
  8.5 0.1 select_select_fusion.blocks
  8.6 22.4 %shard_map.95 = (f32[20,8,12,132]{3,2,1,0:T(8,128)S(1)}, f32[32,8,128]{2,1,0:T(8,128)S(1)}) custom-call(f32[20,4,8,128]{3,2,1,0:T(8,128)S(1)} %pad_maximum_fusion.cells, f32[32,8,128]{2,1,0:T(8,128)S(1)} %select_select_fusion.blocks), custom_call_target="tpu_custom_call" | custom-call | tf_op jit(solution)/shard_map/pallas_call | solution.py:165
  31.0 0.9 add_add_fusion
  31.8 1.0 %fusion.48 = (f32[8,12,132]{2,1,0:T(8,128)}, f32[8,12,132]{2,1,0:T(8,128)S(1)}, f32[8,12,132]{2,1,0:T(8,128)S(1)}, f32[8,12,132]{2,1,0:T(8,128)S(1)}, f32[8,12,132]{2,1,0:T(8,128)S(1)}) fusion(f32[20,8,12,132]{3,2,1,0:T(8,128)S(1)} %get-tuple-element.4), kind=kLoop, calls=%fused_computation.93 | loop fusion | flops 899712 | bytes 1216512 | tf_op jit(solution)/shard_map/mul | solution.py:318
  32.8 1.0 %slice_bitcast_fusion.5 = (f32[8,12,132]{2,1,0:T(8,128)S(1)}, f32[1,8,12,132]{3,2,1,0:T(8,128)}, f32[8,12,132]{2,1,0:T(8,128)S(1)}, f32[8,12,132]{2,1,0:T(8,128)...) fusion(f32[20,8,12,132]{3,2,1,0:T(8,128)S(1)} %get-tuple-element.4), kind=kLoop, calls=%fused_computation.142 | loop fusion | flops 177408 | bytes 1216512 | tf_op jit(solution)/shard_map/squeeze | solution.py:392
  33.8 1.6 %fusion.78 = (f32[8,12,132]{2,1,0:T(8,128)}, f32[8,12,132]{2,1,0:T(8,128)}, f32[8,12,132]{2,1,0:T(8,128)}, f32[8,12,132]{2,1,0:T(8,128)}, f32[8,12,132]{2,1,0:T(...) fusion(f32[8,12,132]{2,1,0:T(8,128)S(1)} %get-tuple-element.50,, ...), kind=kLoop, calls=%fused_computation.123 | loop fusion | flops 1495296 | bytes 1165824 | tf_op jit(solution)/shard_map/mul | solution.py:318
  35.3 0.7 fusion.404
  36.0 0.1 compare_select_fusion.2
  36.1 0.6 fusion.228
  36.8 1.3 %broadcast_multiply_fusion = f32[4096,6,10]{0,2,1:T(8,128)} fusion(f32[4096,10]{0,1:T(8,128)S(1)} %select_add_fusion.5, f32[4096,6]{0,1:T(8,128)S(1)} %select_add_fusion.6), kind=kLoop, calls=%fused_computation.42 | loop fusion | flops 245760 | bytes 1245184 | tf_op jit(solution)/shard_map/mul | solution.py:391
  38.2 2.5 %mul.1044 = f32[4096,60]{0,1:T(8,128)} reshape(f32[4096,6,10]{0,2,1:T(8,128)} %broadcast_multiply_fusion) | data formatting | bytes 1966080 | tf_op jit(solution)/shard_map/mul | solution.py:391
  40.7 1.1 %slice_bitcast_fusion.11 = (f32[8,12,132]{2,1,0:T(8,128)}, f32[1,8,12,132]{3,2,1,0:T(8,128)S(1)}, f32[8,12,132]{2,1,0:T(8,128)}, f32[8,12,132]{2,1,0:T(8,128)}, ...) fusion(f32[20,8,12,132]{3,2,1,0:T(8,128)S(1)} %get-tuple-element.4), kind=kLoop, calls=%fused_computation.148 | loop fusion | flops 177408 | bytes 1216512 | tf_op jit(solution)/shard_map/squeeze | solution.py:392
  41.8 0.0 copy-done.16
  41.8 0.1 copy-done.17
  41.9 0.1 pad_maximum_fusion.1
  42.1 0.7 broadcast_subtract_fusion.4
  42.8 0.0 copy-start.32
  42.8 0.0 copy-start.34
  42.8 3.3 %fusion.14 = f32[3,4096]{1,0:T(4,128)S(1)} fusion(f32[4096,60]{0,1:T(8,128)} %mul.1044, f32[3,60,130]{2,1,0:T(8,128)S(1)} %reshape.363, f32[4096]{0:T(1024)} %bitcast.310, s32[4096]{0:T(1024)} %get-tuple-element.158, f32[4096]{0:T(1024)S(1)} %broadcast_subtract_fusion.4, s32[4096]{0:T(1024)} %get-tuple-element.157), kind=kOutput, calls=%fused_computation.20 | convolution fusion | flops 579203072 | bytes 1191328 | tf_op jit(solution)/shard_map/nz,dkz->dnk/dot_general | solution.py:401
  46.1 0.0 copy-start.26
  46.2 0.0 copy-start.30
  46.2 0.6 copy-done.30
  46.8 0.0 copy-done.36
  46.8 0.0 copy-done.26
  46.9 0.0 copy-done
  46.9 0.0 copy-done.28
  46.9 0.0 copy-done.32
  46.9 0.0 copy-done.34
  46.9 0.0 copy-start.24
  46.9 0.0 copy-start.25
  46.9 2.6 %fusion.4 = f32[3,60,130]{2,1,0:T(8,128)} fusion(f32[3,4096]{1,0:T(4,128)S(1)} %negate_bitcast_fusion.1, f32[4096,60]{0,1:T(8,128)S(1)} %copy-done, f32[4096]{0:T(1024)S(1)} %bitcast.312, s32[4096]{0:T(1024)S(1)} %copy-done.34, f32[4096]{0:T(1024)S(1)} %broadcast_subtract_fusion.4, s32[4096]{0:T(1024)S(1)} %copy-done.32), kind=kOutput, calls=%fused_computation.7 | convolution fusion | flops 578478080 | bytes 1191328 | tf_op jit(solution)/shard_map/dnk,nz->dkz/dot_general | solution.py:409
  49.5 0.0 copy-start.5
  49.5 0.0 copy-start.6
  49.5 0.0 copy-start.7
  49.5 1.0 %reshape.365.ghosts = f32[3,6,10,130]{3,2,1,0:T(8,128)S(1)} reshape(f32[3,60,130]{2,1,0:T(8,128)} %fusion.4) | data formatting | bytes 187200 | tf_op jit(solution)/shard_map/reshape | solution.py:413
  50.7 15.0 %shard_map.96 = f32[3,8,12,132]{3,2,1,0:T(8,128)S(1)} custom-call(f32[3,6,10,130]{3,2,1,0:T(8,128)S(1)} %reshape.365.ghosts), custom_call_target="tpu_custom_call" | custom-call | tf_op jit(solution)/shard_map/pallas_call | solution.py:165
  66.0 5.2 %fusion.82 = (f32[6,10,130]{2,1,0:T(8,128)}, f32[6,10,130]{2,1,0:T(8,128)S(1)}, f32[6,10,130]{2,1,0:T(8,128)S(1)}, f32[6,10,130]{2,1,0:T(8,128)}, f32[6,10,130]{...) fusion(f32[8,12,132]{2,1,0:T(8,128)S(1)} %get-tuple-element.78,, ...), kind=kLoop, calls=%fused_computation.161 | loop fusion | flops 1817400 | bytes 4586400 | tf_op jit(solution)/shard_map/mul | solution.py:318
  71.3 0.1 broadcast_subtract_fusion.1
  71.4 0.0 copy-start.27
  71.4 0.0 copy-start.31
  71.4 0.0 copy-start.29
  71.5 0.0 copy-start.33
  71.5 2.7 %fusion.17 = f32[3,4096]{1,0:T(4,128)S(1)} fusion(f32[4096,60]{0,1:T(8,128)S(1)} %copy-done, f32[4096]{0:T(1024)} %bitcast.311, s32[4096]{0:T(1024)} %get-tuple-element.158, f32[4096]{0:T(1024)} %copy-done.36, s32[4096]{0:T(1024)} %get-tuple-element.157, f32[1,60,130]{2,1,0:T(8,128)S(1)} %stack.33, f32[1,60,130]{2,1,0:T(8,128)S(1)} %stack.32, ...), kind=kOutput, calls=%fused_computation.21 | convolution fusion | flops 579249856 | bytes 1191328 | tf_op jit(solution)/shard_map/nz,dkz->dnk/dot_general | solution.py:401
  74.2 0.1 multiply_select_fusion
  74.4 1.9 %fusion.2 = f32[3,60,130]{2,1,0:T(8,128)S(1)} fusion(f32[3,4096]{1,0:T(4,128)S(1)} %get-tuple-element.116, f32[4096,60]{0,1:T(8,128)S(1)} %copy-done, f32[4096]{0:T(1024)S(1)} %bitcast.313, s32[4096]{0:T(1024)S(1)} %copy-done.35, f32[4096]{0:T(1024)S(1)} %copy-done.37, s32[4096]{0:T(1024)S(1)} %copy-done.33), kind=kOutput, calls=%fused_computation.5 | convolution fusion | flops 578478080 | bytes 1191328 | tf_op jit(solution)/shard_map/dnk,nz->dkz/dot_general | solution.py:409
  76.3 12.8 %shard_map.97 = f32[3,6,10,130]{3,2,1,0:T(8,128)S(1)} custom-call(f32[3,6,10,130]{3,2,1,0:T(8,128)S(1)} %reshape.367.ghosts), custom_call_target="tpu_custom_call" | custom-call | tf_op jit(solution)/shard_map/pallas_call | solution.py:165
  89.1 0.4 fusion.114
  89.6 1.7 %fusion.345 = (f32[1,4,8,128]{3,2,1,0:T(8,128)S(1)}, f32[4,8,128]{2,1,0:T(8,128)S(1)}, f32[4,8,128]{2,1,0:T(8,128)S(1)}, f32[4,8,128]{2,1,0:T(8,128)S(1)}, f32[4...) fusion(f32[6,10,130]{2,1,0:T(8,128)} %get-tuple-element.25, ...), kind=kLoop, calls=%fused_computation.593 | loop fusion | flops 417792 | bytes 1261568 | tf_op jit(solution)/shard_map/stack | solution.py:306
  91.2 1.3 %fusion.284 = (f32[1,4,8,128]{3,2,1,0:T(8,128)S(1)}, f32[4,8,128]{2,1,0:T(8,128)S(1)}, f32[4,8,128]{2,1,0:T(8,128)S(1)}, f32[4,8,128]{2,1,0:T(8,128)S(1)}, f32[4,8,128]{2,1,0:T(8,128)S(1)}) fusion(f32[4,8,128]{2,1,0:T(8,128)S(1)} %get-tuple-element.16, f32[4,8,128]{2,1,0:T(8,128)S(1)} %get-tuple-element.15, f32[4,8,128]{2,1,0:T(8,128)S(1)} %get-tuple-element.14, ...), kind=kLoop, calls=%fused_computation.492 | loop fusion | flops 266240 | bytes 802816 | tf_op jit(solution)/shard_map/stack | solution.py:306
  92.5 1.0 %fusion.244 = f32[1,4,8,128]{3,2,1,0:T(8,128)S(1)} fusion(f32[4,8,128]{2,1,0:T(8,128)S(1)} %get-tuple-element.48, f32[4,8,128]{2,1,0:T(8,128)S(1)} %get-tuple-element.47, f32[4,8,128]{2,1,0:T(8,128)S(1)} %get-tuple-element.46, f32[4,8,128]{2,1,0:T(8,128)S(1)} %get-tuple-element.20, f32[4,8,128]{2,1,0:T(8,128)S(1)} %get-tuple-element.19, ...), kind=kLoop, calls=%fused_computation.428 | loop fusion | flops 114688 | bytes 344064 | tf_op jit(solution)/shard_map/stack | solution.py:306
  93.5 0.6 maximum_multiply_fusion
  94.2 0.6 copy.16
  (75 shorter events, 0.5 us)
Async XLA Ops:
  40.7 1.1 %copy-start.16 = (f32[1,8,12,132]{3,2,1,0:T(8,128)S(1)}, f32[1,8,12,132]{3,2,1,0:T(8,128)}, u32[]{:S(2)}) copy-start(f32[1,8,12,132]{3,2,1,0:T(8,128)} %get-tuple-element.67) | copy-start | bytes 152068
  40.7 1.2 %copy-start.17 = (f32[1,8,12,132]{3,2,1,0:T(8,128)S(1)}, f32[1,8,12,132]{3,2,1,0:T(8,128)}, u32[]{:S(2)}) copy-start(f32[1,8,12,132]{3,2,1,0:T(8,128)} %get-tuple-element.76) | copy-start | bytes 152068
  42.8 4.0 %copy-start.36 = (f32[4096]{0:T(1024)}, f32[4096]{0:T(1024)S(1)}, u32[]{:S(2)}) copy-start(f32[4096]{0:T(1024)S(1)} %broadcast_subtract_fusion.4) | copy-start | bytes 49156
  42.8 4.0 %copy-start = (f32[4096,60]{0,1:T(8,128)S(1)}, f32[4096,60]{0,1:T(8,128)}, u32[]{:S(2)}) copy-start(f32[4096,60]{0,1:T(8,128)} %mul.1044) | copy-start | bytes 2949124
  42.8 4.1 %copy-start.28 = (f32[32,1,128]{2,1,0:T(1,128)S(1)}, f32[32,1,128]{2,1,0:T(1,128)}, u32[]{:S(2)}) copy-start(f32[32,1,128]{2,1,0:T(1,128)} %get-tuple-element.153) | copy-start | bytes 49156
  42.8 4.1 %copy-start.32 = (s32[4096]{0:T(1024)S(1)}, s32[4096]{0:T(1024)}, u32[]{:S(2)}) copy-start(s32[4096]{0:T(1024)} %get-tuple-element.157) | copy-start | bytes 49156
  42.8 4.1 %copy-start.34 = (s32[4096]{0:T(1024)S(1)}, s32[4096]{0:T(1024)}, u32[]{:S(2)}) copy-start(s32[4096]{0:T(1024)} %get-tuple-element.158) | copy-start | bytes 49156
  46.1 0.7 copy-start.26
  46.2 0.6 copy-start.30
  46.9 18.9 %copy-start.24 = (f32[8,12,132]{2,1,0:T(8,128)S(1)}, f32[8,12,132]{2,1,0:T(8,128)}, u32[]{:S(2)}) copy-start(f32[8,12,132]{2,1,0:T(8,128)} %get-tuple-element.117) | copy-start | bytes 152068
  46.9 18.9 %copy-start.25 = (f32[8,12,132]{2,1,0:T(8,128)S(1)}, f32[8,12,132]{2,1,0:T(8,128)}, u32[]{:S(2)}) copy-start(f32[8,12,132]{2,1,0:T(8,128)} %get-tuple-element.118) | copy-start | bytes 152068
  49.5 16.3 %copy-start.1 = (f32[8,12,132]{2,1,0:T(8,128)S(1)}, f32[8,12,132]{2,1,0:T(8,128)}, u32[]{:S(2)}) copy-start(f32[8,12,132]{2,1,0:T(8,128)} %get-tuple-element.70) | copy-start | bytes 152068
  49.5 16.3 %copy-start.2 = (f32[8,12,132]{2,1,0:T(8,128)S(1)}, f32[8,12,132]{2,1,0:T(8,128)}, u32[]{:S(2)}) copy-start(f32[8,12,132]{2,1,0:T(8,128)} %get-tuple-element.71) | copy-start | bytes 152068
  49.5 16.3 %copy-start.3 = (f32[8,12,132]{2,1,0:T(8,128)S(1)}, f32[8,12,132]{2,1,0:T(8,128)}, u32[]{:S(2)}) copy-start(f32[8,12,132]{2,1,0:T(8,128)} %get-tuple-element.72) | copy-start | bytes 152068
  49.5 16.3 %copy-start.4 = (f32[8,12,132]{2,1,0:T(8,128)S(1)}, f32[8,12,132]{2,1,0:T(8,128)}, u32[]{:S(2)}) copy-start(f32[8,12,132]{2,1,0:T(8,128)} %get-tuple-element.73) | copy-start | bytes 152068
  49.5 16.4 %copy-start.5 = (f32[8,12,132]{2,1,0:T(8,128)S(1)}, f32[8,12,132]{2,1,0:T(8,128)}, u32[]{:S(2)}) copy-start(f32[8,12,132]{2,1,0:T(8,128)} %get-tuple-element.74) | copy-start | bytes 152068
  49.5 16.4 %copy-start.6 = (f32[8,12,132]{2,1,0:T(8,128)S(1)}, f32[8,12,132]{2,1,0:T(8,128)}, u32[]{:S(2)}) copy-start(f32[8,12,132]{2,1,0:T(8,128)} %get-tuple-element.56) | copy-start | bytes 152068
  49.5 16.4 %copy-start.7 = (f32[8,12,132]{2,1,0:T(8,128)S(1)}, f32[8,12,132]{2,1,0:T(8,128)}, u32[]{:S(2)}) copy-start(f32[8,12,132]{2,1,0:T(8,128)} %get-tuple-element.58) | copy-start | bytes 152068
  50.6 15.3 %copy-start.8 = (f32[8,12,132]{2,1,0:T(8,128)S(1)}, f32[8,12,132]{2,1,0:T(8,128)}, u32[]{:S(2)}) copy-start(f32[8,12,132]{2,1,0:T(8,128)} %get-tuple-element.59) | copy-start | bytes 152068
  50.6 15.3 %copy-start.9 = (f32[8,12,132]{2,1,0:T(8,128)S(1)}, f32[8,12,132]{2,1,0:T(8,128)}, u32[]{:S(2)}) copy-start(f32[8,12,132]{2,1,0:T(8,128)} %get-tuple-element.60) | copy-start | bytes 152068
  50.6 15.3 %copy-start.10 = (f32[8,12,132]{2,1,0:T(8,128)S(1)}, f32[8,12,132]{2,1,0:T(8,128)}, u32[]{:S(2)}) copy-start(f32[8,12,132]{2,1,0:T(8,128)} %get-tuple-element.61) | copy-start | bytes 152068
  50.6 15.3 %copy-start.11 = (f32[8,12,132]{2,1,0:T(8,128)S(1)}, f32[8,12,132]{2,1,0:T(8,128)}, u32[]{:S(2)}) copy-start(f32[8,12,132]{2,1,0:T(8,128)} %get-tuple-element.62) | copy-start | bytes 152068
  50.6 15.3 %copy-start.12 = (f32[8,12,132]{2,1,0:T(8,128)S(1)}, f32[8,12,132]{2,1,0:T(8,128)}, u32[]{:S(2)}) copy-start(f32[8,12,132]{2,1,0:T(8,128)} %get-tuple-element.63) | copy-start | bytes 152068
  50.6 15.3 %copy-start.13 = (f32[8,12,132]{2,1,0:T(8,128)S(1)}, f32[8,12,132]{2,1,0:T(8,128)}, u32[]{:S(2)}) copy-start(f32[8,12,132]{2,1,0:T(8,128)} %get-tuple-element.64) | copy-start | bytes 152068
  50.6 15.3 %copy-start.14 = (f32[8,12,132]{2,1,0:T(8,128)S(1)}, f32[8,12,132]{2,1,0:T(8,128)}, u32[]{:S(2)}) copy-start(f32[8,12,132]{2,1,0:T(8,128)} %get-tuple-element.65) | copy-start | bytes 152068
  50.6 15.3 %copy-start.15 = (f32[8,12,132]{2,1,0:T(8,128)S(1)}, f32[8,12,132]{2,1,0:T(8,128)}, u32[]{:S(2)}) copy-start(f32[8,12,132]{2,1,0:T(8,128)} %get-tuple-element.77) | copy-start | bytes 152068
  50.6 15.3 %copy-start.18 = (f32[8,12,132]{2,1,0:T(8,128)S(1)}, f32[8,12,132]{2,1,0:T(8,128)}, u32[]{:S(2)}) copy-start(f32[8,12,132]{2,1,0:T(8,128)} %get-tuple-element.49) | copy-start | bytes 152068
  50.7 15.3 %copy-start.19 = (f32[8,12,132]{2,1,0:T(8,128)S(1)}, f32[8,12,132]{2,1,0:T(8,128)}, u32[]{:S(2)}) copy-start(f32[8,12,132]{2,1,0:T(8,128)} %get-tuple-element.75) | copy-start | bytes 152068
  50.7 15.3 %copy-start.20 = (f32[8,12,132]{2,1,0:T(8,128)S(1)}, f32[8,12,132]{2,1,0:T(8,128)}, u32[]{:S(2)}) copy-start(f32[8,12,132]{2,1,0:T(8,128)} %get-tuple-element.79) | copy-start | bytes 152068
  50.7 15.3 %copy-start.21 = (f32[8,12,132]{2,1,0:T(8,128)S(1)}, f32[8,12,132]{2,1,0:T(8,128)}, u32[]{:S(2)}) copy-start(f32[8,12,132]{2,1,0:T(8,128)} %get-tuple-element.80) | copy-start | bytes 152068
  50.7 15.3 %copy-start.22 = (f32[8,12,132]{2,1,0:T(8,128)S(1)}, f32[8,12,132]{2,1,0:T(8,128)}, u32[]{:S(2)}) copy-start(f32[8,12,132]{2,1,0:T(8,128)} %get-tuple-element.81) | copy-start | bytes 152068
  50.7 15.3 %copy-start.23 = (f32[8,12,132]{2,1,0:T(8,128)S(1)}, f32[8,12,132]{2,1,0:T(8,128)}, u32[]{:S(2)}) copy-start(f32[8,12,132]{2,1,0:T(8,128)} %get-tuple-element.82) | copy-start | bytes 152068
  71.4 2.8 %copy-start.27 = (f32[3,4096]{1,0:T(4,128)S(1)}, f32[3,4096]{1,0:T(4,128)}, u32[]{:S(2)}) copy-start(f32[3,4096]{1,0:T(4,128)} %copy-done.26) | copy-start | bytes 147460
  71.4 2.8 %copy-start.31 = (pred[32,1,128]{2,0,1:T(8,128)(4,1)S(1)}, pred[32,1,128]{2,0,1:T(8,128)(4,1)}, u32[]{:S(2)}) copy-start(pred[32,1,128]{2,0,1:T(8,128)(4,1)} %copy-done.30) | copy-start | bytes 12292
  71.4 2.9 %copy-start.29 = (f32[32,1,128]{2,1,0:T(1,128)S(1)}, f32[32,1,128]{2,1,0:T(1,128)}, u32[]{:S(2)}) copy-start(f32[32,1,128]{2,1,0:T(1,128)} %get-tuple-element.153) | copy-start | bytes 49156
  71.5 2.9 %copy-start.33 = (s32[4096]{0:T(1024)S(1)}, s32[4096]{0:T(1024)}, u32[]{:S(2)}) copy-start(s32[4096]{0:T(1024)} %get-tuple-element.157) | copy-start | bytes 49156
  71.5 2.9 %copy-start.35 = (s32[4096]{0:T(1024)S(1)}, s32[4096]{0:T(1024)}, u32[]{:S(2)}) copy-start(s32[4096]{0:T(1024)} %get-tuple-element.158) | copy-start | bytes 49156
  71.5 2.9 %copy-start.37 = (f32[4096]{0:T(1024)S(1)}, f32[4096]{0:T(1024)}, u32[]{:S(2)}) copy-start(f32[4096]{0:T(1024)} %copy-done.36) | copy-start | bytes 49156

commit v6 on v5

--- a/solution.py
+++ b/solution.py
@@ -93,12 +93,14 @@
 
 
 def widen_kernel(
-    width, groups, peers, cells, blocks, out, got, x_in, y_out, y_in, e_out, e_in, mid, z_out,
+    width, groups, peers, given, solid, blocks, out, got, cells, x_in, y_out, y_in, e_out, e_in, mid, z_out,
     z_in, arrived, send_sems, recv_sems, give_sems, take_sems,
 ):
     fields, size_x, size_y, size_z = cells.shape
     capacity = blocks.shape[0] // peers
     me = lax.axis_index("gx")
+    cells[: fields - 1] = given[...]
+    cells[fields - 1] = solid[...].astype(jnp.float32) * 0.25
     greet(peers)
     x_copies = send(
         "gx",
@@ -175,8 +177,8 @@
     )(*operands)
 
 
-def with_halo(cells, blocks, peers, width):
-    fields, size_x, size_y, size_z = cells.shape
+def with_halo(populations, solid, blocks, peers, width):
+    fields, size_x, size_y, size_z = (populations.shape[0] + 1,) + populations.shape[1:]
     wide_x, wide_y, wide_z = (size_x + 2 * width, size_y + 2 * width, size_z + 2 * width)
     groups = 4 if fields % 4 == 0 else 1
     x_slab = (2, fields, width, size_y, size_z)
@@ -185,9 +187,10 @@
     z_slab = (2, wide_x, wide_y, fields * width)
     return call_kernel(
         functools.partial(widen_kernel, width, groups, peers),
-        (cells, blocks),
+        (populations, solid, blocks),
         ((fields, wide_x, wide_y, wide_z), blocks.shape),
-        [x_slab, y_slab, y_slab, e_slab, e_slab, (fields, wide_x, wide_y, size_z), z_slab, z_slab]
+        [(fields, size_x, size_y, size_z)]
+        + [x_slab, y_slab, y_slab, e_slab, e_slab, (fields, wide_x, wide_y, size_z), z_slab, z_slab]
         + [blocks.shape],
         0,
         peers,
@@ -365,10 +368,7 @@
     )
     empty = jnp.where(jnp.arange(8) == 7, -1.0, 0.0).astype(jnp.float32)[None, :, None]
     send_floats = jnp.where(filled[:, None, None], jnp.take(floats, source, axis=0), empty)
-    gray = solid_class.astype(jnp.float32) * 0.25
-    wide, got_floats = with_halo(
-        jnp.concatenate([populations, gray[None]]), send_floats, peers, STEPS
-    )
+    wide, got_floats = with_halo(populations, solid_class, send_floats, peers, STEPS)
     offset = got_floats[:, 0:3, :]
     velocity = got_floats[:, 3:6, :]
     drag_rate = got_floats[:, 6, :]

time: 95.6 us -> 95.6 us (level)
  other arithmetic: 25.5 us -> 23.7 us
  local copies, waits for them, and re-layouts: 7.27 us -> 8.93 us
    unnamed x80 -> x84, local copies, waits for them, and re-layouts: 2.98 us -> 4.65 us
    concatenate x1 -> x0, other arithmetic: 0.99 us -> none  [per_device(): jnp.concatenate([populations, gray[None]])]
where the time goes in v6:
time: 95.6 us; the launch traced here: 94.7 us
  Pallas kernels  50.1 us (52%)
  other arithmetic  23.7 us (25%)
  matrix products  10.5 us (11%)
  local copies, waits for them, and re-layouts  8.93 us (9%)
  between operations  1.41 us (1%)
    pallas_call x3, Pallas kernels, call_kernel(): pl.pallas_call(kernel, out_shape=[jax.ShapeDtypeStruct(shape, jnp.float32...  50.1 us
    mul x4, other arithmetic, collide(): equilibrium = weights[i] * baseline  8.17 us
    dot_general x2, matrix products, per_device(): jnp.einsum('nz,dkz->dnk', tables[2], lines, precision=lax.Precision.HIGH)  6.02 us
    unnamed x84, local copies, waits for them, and re-layouts  4.65 us
    dot_general x2, matrix products, per_device(): jnp.einsum('dnk,nz->dkz', pushed[:, :, None] * across[None], tables[2], p...  4.47 us
    another operation x4, other arithmetic, moments(): return (density, jnp.stack(components))  4.1 us
    mul x1, local copies, waits for them, and re-layouts, per_device(): tables[0][:, :, None] * tables[1][:, None, :]  2.53 us
    squeeze x2, other arithmetic, per_device(): fields = [wide[i] for i in range(19)]  2.08 us

profile of v6, /device:TPU:0, one launch (start us, length us, event | category | flops | bytes accessed | tf_op | source)
XLA Modules:
  0.0 94.7 jit_solution(10856529105101340967)
XLA Ops:
  0.6 0.8 select_convert_fusion
  1.4 0.8 copy.15
  2.2 0.8 copy.14
  2.9 0.7 pad_maximum_fusion.2
  3.7 0.7 fusion.356
  4.4 0.8 select_reduce_fusion.1
  5.3 0.7 multiply_add_fusion
  5.9 0.1 select_reduce_fusion
  6.0 0.6 gather_fusion
  6.6 0.1 fusion.355
  6.7 0.1 select_select_fusion.blocks
  6.9 0.0 copy-start
  6.9 1.0 %copy-done = f32[19,4,8,128]{3,2,1,0:T(8,128)S(1)} copy-done((f32[19,4,8,128]{3,2,1,0:T(8,128)S(1)}, f32[19,4,8,128]{3,2,1,0:T(8,128)}, u32[]{:S(2)}) %copy-start) | copy-done | bytes 311320
  7.9 0.7 copy-done.1
  8.6 22.3 %shard_map.95 = (f32[20,8,12,132]{3,2,1,0:T(8,128)S(1)}, f32[32,8,128]{2,1,0:T(8,128)S(1)}) custom-call(f32[19,4,8,128]{3,2,1,0:T(8,128)S(1)} %copy-done, s32[4,8,128]{2,1,0:T(8,128)S(1)} %copy-done.1, f32[32,8,128]{2,1,0:T(8,128)S(1)} %select_select_fusion.blocks), custom_call_target="tpu_custom_call" | custom-call | tf_op jit(solution)/shard_map/pallas_call | solution.py:167
  30.9 0.9 add_add_fusion
  31.8 1.0 %fusion.48 = (f32[8,12,132]{2,1,0:T(8,128)}, f32[8,12,132]{2,1,0:T(8,128)S(1)}, f32[8,12,132]{2,1,0:T(8,128)S(1)}, f32[8,12,132]{2,1,0:T(8,128)S(1)}, f32[8,12,132]{2,1,0:T(8,128)S(1)}) fusion(f32[20,8,12,132]{3,2,1,0:T(8,128)S(1)} %get-tuple-element.4), kind=kLoop, calls=%fused_computation.92 | loop fusion | flops 899712 | bytes 1216512 | tf_op jit(solution)/shard_map/mul | solution.py:321
  32.7 1.0 %slice_bitcast_fusion.5 = (f32[8,12,132]{2,1,0:T(8,128)S(1)}, f32[1,8,12,132]{3,2,1,0:T(8,128)}, f32[8,12,132]{2,1,0:T(8,128)S(1)}, f32[8,12,132]{2,1,0:T(8,128)...) fusion(f32[20,8,12,132]{3,2,1,0:T(8,128)S(1)} %get-tuple-element.4), kind=kLoop, calls=%fused_computation.141 | loop fusion | flops 177408 | bytes 1216512 | tf_op jit(solution)/shard_map/squeeze | solution.py:392
  33.7 1.6 %fusion.78 = (f32[8,12,132]{2,1,0:T(8,128)}, f32[8,12,132]{2,1,0:T(8,128)}, f32[8,12,132]{2,1,0:T(8,128)}, f32[8,12,132]{2,1,0:T(8,128)}, f32[8,12,132]{2,1,0:T(...) fusion(f32[8,12,132]{2,1,0:T(8,128)S(1)} %get-tuple-element.50,, ...), kind=kLoop, calls=%fused_computation.122 | loop fusion | flops 1495296 | bytes 1165824 | tf_op jit(solution)/shard_map/mul | solution.py:321
  35.3 0.7 fusion.404
  36.0 0.1 compare_select_fusion.2
  36.0 0.6 fusion.228
  36.8 1.3 %broadcast_multiply_fusion = f32[4096,6,10]{0,2,1:T(8,128)} fusion(f32[4096,10]{0,1:T(8,128)S(1)} %select_add_fusion.5, f32[4096,6]{0,1:T(8,128)S(1)} %select_add_fusion.6), kind=kLoop, calls=%fused_computation.42 | loop fusion | flops 245760 | bytes 1245184 | tf_op jit(solution)/shard_map/mul | solution.py:391
  38.1 2.5 %mul.1036 = f32[4096,60]{0,1:T(8,128)} reshape(f32[4096,6,10]{0,2,1:T(8,128)} %broadcast_multiply_fusion) | data formatting | bytes 1966080 | tf_op jit(solution)/shard_map/mul | solution.py:391
  40.6 1.1 %slice_bitcast_fusion.11 = (f32[8,12,132]{2,1,0:T(8,128)}, f32[1,8,12,132]{3,2,1,0:T(8,128)S(1)}, f32[8,12,132]{2,1,0:T(8,128)}, f32[8,12,132]{2,1,0:T(8,128)}, ...) fusion(f32[20,8,12,132]{3,2,1,0:T(8,128)S(1)} %get-tuple-element.4), kind=kLoop, calls=%fused_computation.147 | loop fusion | flops 177408 | bytes 1216512 | tf_op jit(solution)/shard_map/squeeze | solution.py:392
  41.7 0.1 copy-done.19
  41.8 0.1 pad_maximum_fusion
  42.0 0.7 broadcast_subtract_fusion.4
  42.8 0.0 copy-start.34
  42.8 3.3 %fusion.14 = f32[3,4096]{1,0:T(4,128)S(1)} fusion(f32[4096,60]{0,1:T(8,128)} %mul.1036, f32[3,60,130]{2,1,0:T(8,128)S(1)} %reshape.363, f32[4096]{0:T(1024)} %bitcast.308, s32[4096]{0:T(1024)} %get-tuple-element.158, f32[4096]{0:T(1024)S(1)} %broadcast_subtract_fusion.4, s32[4096]{0:T(1024)} %get-tuple-element.157), kind=kOutput, calls=%fused_computation.20 | convolution fusion | flops 579203072 | bytes 1191328 | tf_op jit(solution)/shard_map/nz,dkz->dnk/dot_general | solution.py:401
  46.1 0.0 copy-start.32
  46.2 0.6 copy-done.32
  46.8 0.0 copy-done.38
  46.8 0.0 copy-done.28
  46.8 0.0 copy-done.2
  46.8 0.0 copy-done.30
  46.8 0.0 copy-done.34
  46.8 0.0 copy-done.36
  46.8 0.0 copy-start.26
  46.8 0.0 copy-start.27
  46.8 2.6 %fusion.4 = f32[3,60,130]{2,1,0:T(8,128)} fusion(f32[3,4096]{1,0:T(4,128)S(1)} %negate_bitcast_fusion.1, f32[4096,60]{0,1:T(8,128)S(1)} %copy-done.2, f32[4096]{0:T(1024)S(1)} %bitcast.310, s32[4096]{0:T(1024)S(1)} %copy-done.36, f32[4096]{0:T(1024)S(1)} %broadcast_subtract_fusion.4, s32[4096]{0:T(1024)S(1)} %copy-done.34), kind=kOutput, calls=%fused_computation.7 | convolution fusion | flops 578478080 | bytes 1191328 | tf_op jit(solution)/shard_map/dnk,nz->dkz/dot_general | solution.py:409
  49.4 0.0 copy-start.7
  49.4 0.0 copy-start.8
  49.4 0.0 copy-start.9
  49.5 1.0 %reshape.365.ghosts = f32[3,6,10,130]{3,2,1,0:T(8,128)S(1)} reshape(f32[3,60,130]{2,1,0:T(8,128)} %fusion.4) | data formatting | bytes 187200 | tf_op jit(solution)/shard_map/reshape | solution.py:413
  50.5 0.0 copy-start.10
  50.5 0.0 copy-start.11
  50.5 0.0 copy-start.12
  50.5 0.0 copy-start.13
  50.6 15.0 %shard_map.96 = f32[3,8,12,132]{3,2,1,0:T(8,128)S(1)} custom-call(f32[3,6,10,130]{3,2,1,0:T(8,128)S(1)} %reshape.365.ghosts), custom_call_target="tpu_custom_call" | custom-call | tf_op jit(solution)/shard_map/pallas_call | solution.py:167
  65.9 5.3 %fusion.82 = (f32[6,10,130]{2,1,0:T(8,128)}, f32[6,10,130]{2,1,0:T(8,128)S(1)}, f32[6,10,130]{2,1,0:T(8,128)S(1)}, f32[6,10,130]{2,1,0:T(8,128)}, f32[6,10,130]{...) fusion(f32[8,12,132]{2,1,0:T(8,128)S(1)} %get-tuple-element.78,, ...), kind=kLoop, calls=%fused_computation.160 | loop fusion | flops 1817400 | bytes 4586400 | tf_op jit(solution)/shard_map/mul | solution.py:321
  71.2 0.1 broadcast_subtract_fusion.1
  71.4 0.0 copy-start.31
  71.4 0.0 copy-start.35
  71.4 2.7 %fusion.17 = f32[3,4096]{1,0:T(4,128)S(1)} fusion(f32[4096,60]{0,1:T(8,128)S(1)} %copy-done.2, f32[4096]{0:T(1024)} %bitcast.309, s32[4096]{0:T(1024)} %get-tuple-element.158, f32[4096]{0:T(1024)} %copy-done.38, s32[4096]{0:T(1024)} %get-tuple-element.157, f32[1,60,130]{2,1,0:T(8,128)S(1)} %stack.33, f32[1,60,130]{2,1,0:T(8,128)S(1)} %stack.32, ...), kind=kOutput, calls=%fused_computation.21 | convolution fusion | flops 579249856 | bytes 1191328 | tf_op jit(solution)/shard_map/nz,dkz->dnk/dot_general | solution.py:401
  74.2 0.1 multiply_select_fusion
  74.3 1.9 %fusion.2 = f32[3,60,130]{2,1,0:T(8,128)S(1)} fusion(f32[3,4096]{1,0:T(4,128)S(1)} %get-tuple-element.116, f32[4096,60]{0,1:T(8,128)S(1)} %copy-done.2, f32[4096]{0:T(1024)S(1)} %bitcast.311, s32[4096]{0:T(1024)S(1)} %copy-done.37, f32[4096]{0:T(1024)S(1)} %copy-done.39, s32[4096]{0:T(1024)S(1)} %copy-done.35), kind=kOutput, calls=%fused_computation.5 | convolution fusion | flops 578478080 | bytes 1191328 | tf_op jit(solution)/shard_map/dnk,nz->dkz/dot_general | solution.py:409
  76.2 12.8 %shard_map.97 = f32[3,6,10,130]{3,2,1,0:T(8,128)S(1)} custom-call(f32[3,6,10,130]{3,2,1,0:T(8,128)S(1)} %reshape.367.ghosts), custom_call_target="tpu_custom_call" | custom-call | tf_op jit(solution)/shard_map/pallas_call | solution.py:167
  89.1 0.4 fusion.114
  89.5 1.7 %fusion.345 = (f32[1,4,8,128]{3,2,1,0:T(8,128)S(1)}, f32[4,8,128]{2,1,0:T(8,128)S(1)}, f32[4,8,128]{2,1,0:T(8,128)S(1)}, f32[4,8,128]{2,1,0:T(8,128)S(1)}, f32[4...) fusion(f32[6,10,130]{2,1,0:T(8,128)} %get-tuple-element.25, ...), kind=kLoop, calls=%fused_computation.592 | loop fusion | flops 417792 | bytes 1261568 | tf_op jit(solution)/shard_map/stack | solution.py:309
  91.1 1.3 %fusion.284 = (f32[1,4,8,128]{3,2,1,0:T(8,128)S(1)}, f32[4,8,128]{2,1,0:T(8,128)S(1)}, f32[4,8,128]{2,1,0:T(8,128)S(1)}, f32[4,8,128]{2,1,0:T(8,128)S(1)}, f32[4,8,128]{2,1,0:T(8,128)S(1)}) fusion(f32[4,8,128]{2,1,0:T(8,128)S(1)} %get-tuple-element.16, f32[4,8,128]{2,1,0:T(8,128)S(1)} %get-tuple-element.15, f32[4,8,128]{2,1,0:T(8,128)S(1)} %get-tuple-element.14, ...), kind=kLoop, calls=%fused_computation.491 | loop fusion | flops 266240 | bytes 802816 | tf_op jit(solution)/shard_map/stack | solution.py:309
  92.4 1.0 %fusion.244 = f32[1,4,8,128]{3,2,1,0:T(8,128)S(1)} fusion(f32[4,8,128]{2,1,0:T(8,128)S(1)} %get-tuple-element.48, f32[4,8,128]{2,1,0:T(8,128)S(1)} %get-tuple-element.47, f32[4,8,128]{2,1,0:T(8,128)S(1)} %get-tuple-element.46, f32[4,8,128]{2,1,0:T(8,128)S(1)} %get-tuple-element.20, f32[4,8,128]{2,1,0:T(8,128)S(1)} %get-tuple-element.19, ...), kind=kLoop, calls=%fused_computation.427 | loop fusion | flops 114688 | bytes 344064 | tf_op jit(solution)/shard_map/stack | solution.py:309
  93.4 0.6 maximum_multiply_fusion
  94.1 0.6 copy.16
  (77 shorter events, 0.5 us)
Async XLA Ops:
  6.9 1.0 %copy-start = (f32[19,4,8,128]{3,2,1,0:T(8,128)S(1)}, f32[19,4,8,128]{3,2,1,0:T(8,128)}, u32[]{:S(2)}) copy-start(f32[19,4,8,128]{3,2,1,0:T(8,128)} %given.1) | copy-start | bytes 933892
  7.9 0.7 copy-start.1
  40.6 1.1 %copy-start.18 = (f32[1,8,12,132]{3,2,1,0:T(8,128)S(1)}, f32[1,8,12,132]{3,2,1,0:T(8,128)}, u32[]{:S(2)}) copy-start(f32[1,8,12,132]{3,2,1,0:T(8,128)} %get-tuple-element.67) | copy-start | bytes 152068
  40.6 1.2 %copy-start.19 = (f32[1,8,12,132]{3,2,1,0:T(8,128)S(1)}, f32[1,8,12,132]{3,2,1,0:T(8,128)}, u32[]{:S(2)}) copy-start(f32[1,8,12,132]{3,2,1,0:T(8,128)} %get-tuple-element.76) | copy-start | bytes 152068
  42.8 4.0 %copy-start.38 = (f32[4096]{0:T(1024)}, f32[4096]{0:T(1024)S(1)}, u32[]{:S(2)}) copy-start(f32[4096]{0:T(1024)S(1)} %broadcast_subtract_fusion.4) | copy-start | bytes 49156
  42.8 4.0 %copy-start.2 = (f32[4096,60]{0,1:T(8,128)S(1)}, f32[4096,60]{0,1:T(8,128)}, u32[]{:S(2)}) copy-start(f32[4096,60]{0,1:T(8,128)} %mul.1036) | copy-start | bytes 2949124
  42.8 4.0 %copy-start.30 = (f32[32,1,128]{2,1,0:T(1,128)S(1)}, f32[32,1,128]{2,1,0:T(1,128)}, u32[]{:S(2)}) copy-start(f32[32,1,128]{2,1,0:T(1,128)} %get-tuple-element.153) | copy-start | bytes 49156
  42.8 4.0 %copy-start.34 = (s32[4096]{0:T(1024)S(1)}, s32[4096]{0:T(1024)}, u32[]{:S(2)}) copy-start(s32[4096]{0:T(1024)} %get-tuple-element.157) | copy-start | bytes 49156
  42.8 4.0 %copy-start.36 = (s32[4096]{0:T(1024)S(1)}, s32[4096]{0:T(1024)}, u32[]{:S(2)}) copy-start(s32[4096]{0:T(1024)} %get-tuple-element.158) | copy-start | bytes 49156
  46.1 0.7 copy-start.28
  46.1 0.6 copy-start.32
  46.8 18.9 %copy-start.26 = (f32[8,12,132]{2,1,0:T(8,128)S(1)}, f32[8,12,132]{2,1,0:T(8,128)}, u32[]{:S(2)}) copy-start(f32[8,12,132]{2,1,0:T(8,128)} %get-tuple-element.117) | copy-start | bytes 152068
  46.8 18.9 %copy-start.27 = (f32[8,12,132]{2,1,0:T(8,128)S(1)}, f32[8,12,132]{2,1,0:T(8,128)}, u32[]{:S(2)}) copy-start(f32[8,12,132]{2,1,0:T(8,128)} %get-tuple-element.118) | copy-start | bytes 152068
  49.4 16.3 %copy-start.3 = (f32[8,12,132]{2,1,0:T(8,128)S(1)}, f32[8,12,132]{2,1,0:T(8,128)}, u32[]{:S(2)}) copy-start(f32[8,12,132]{2,1,0:T(8,128)} %get-tuple-element.70) | copy-start | bytes 152068
  49.4 16.3 %copy-start.4 = (f32[8,12,132]{2,1,0:T(8,128)S(1)}, f32[8,12,132]{2,1,0:T(8,128)}, u32[]{:S(2)}) copy-start(f32[8,12,132]{2,1,0:T(8,128)} %get-tuple-element.71) | copy-start | bytes 152068
  49.4 16.3 %copy-start.5 = (f32[8,12,132]{2,1,0:T(8,128)S(1)}, f32[8,12,132]{2,1,0:T(8,128)}, u32[]{:S(2)}) copy-start(f32[8,12,132]{2,1,0:T(8,128)} %get-tuple-element.72) | copy-start | bytes 152068
  49.4 16.3 %copy-start.6 = (f32[8,12,132]{2,1,0:T(8,128)S(1)}, f32[8,12,132]{2,1,0:T(8,128)}, u32[]{:S(2)}) copy-start(f32[8,12,132]{2,1,0:T(8,128)} %get-tuple-element.73) | copy-start | bytes 152068
  49.4 16.4 %copy-start.7 = (f32[8,12,132]{2,1,0:T(8,128)S(1)}, f32[8,12,132]{2,1,0:T(8,128)}, u32[]{:S(2)}) copy-start(f32[8,12,132]{2,1,0:T(8,128)} %get-tuple-element.74) | copy-start | bytes 152068
  49.4 16.4 %copy-start.8 = (f32[8,12,132]{2,1,0:T(8,128)S(1)}, f32[8,12,132]{2,1,0:T(8,128)}, u32[]{:S(2)}) copy-start(f32[8,12,132]{2,1,0:T(8,128)} %get-tuple-element.56) | copy-start | bytes 152068
  49.4 16.4 %copy-start.9 = (f32[8,12,132]{2,1,0:T(8,128)S(1)}, f32[8,12,132]{2,1,0:T(8,128)}, u32[]{:S(2)}) copy-start(f32[8,12,132]{2,1,0:T(8,128)} %get-tuple-element.58) | copy-start | bytes 152068
  50.5 15.3 %copy-start.10 = (f32[8,12,132]{2,1,0:T(8,128)S(1)}, f32[8,12,132]{2,1,0:T(8,128)}, u32[]{:S(2)}) copy-start(f32[8,12,132]{2,1,0:T(8,128)} %get-tuple-element.59) | copy-start | bytes 152068
  50.5 15.3 %copy-start.11 = (f32[8,12,132]{2,1,0:T(8,128)S(1)}, f32[8,12,132]{2,1,0:T(8,128)}, u32[]{:S(2)}) copy-start(f32[8,12,132]{2,1,0:T(8,128)} %get-tuple-element.60) | copy-start | bytes 152068
  50.5 15.3 %copy-start.12 = (f32[8,12,132]{2,1,0:T(8,128)S(1)}, f32[8,12,132]{2,1,0:T(8,128)}, u32[]{:S(2)}) copy-start(f32[8,12,132]{2,1,0:T(8,128)} %get-tuple-element.61) | copy-start | bytes 152068
  50.5 15.3 %copy-start.13 = (f32[8,12,132]{2,1,0:T(8,128)S(1)}, f32[8,12,132]{2,1,0:T(8,128)}, u32[]{:S(2)}) copy-start(f32[8,12,132]{2,1,0:T(8,128)} %get-tuple-element.62) | copy-start | bytes 152068
  50.5 15.3 %copy-start.14 = (f32[8,12,132]{2,1,0:T(8,128)S(1)}, f32[8,12,132]{2,1,0:T(8,128)}, u32[]{:S(2)}) copy-start(f32[8,12,132]{2,1,0:T(8,128)} %get-tuple-element.63) | copy-start | bytes 152068
  50.5 15.3 %copy-start.15 = (f32[8,12,132]{2,1,0:T(8,128)S(1)}, f32[8,12,132]{2,1,0:T(8,128)}, u32[]{:S(2)}) copy-start(f32[8,12,132]{2,1,0:T(8,128)} %get-tuple-element.64) | copy-start | bytes 152068
  50.5 15.3 %copy-start.16 = (f32[8,12,132]{2,1,0:T(8,128)S(1)}, f32[8,12,132]{2,1,0:T(8,128)}, u32[]{:S(2)}) copy-start(f32[8,12,132]{2,1,0:T(8,128)} %get-tuple-element.65) | copy-start | bytes 152068
  50.6 15.3 %copy-start.17 = (f32[8,12,132]{2,1,0:T(8,128)S(1)}, f32[8,12,132]{2,1,0:T(8,128)}, u32[]{:S(2)}) copy-start(f32[8,12,132]{2,1,0:T(8,128)} %get-tuple-element.77) | copy-start | bytes 152068
  50.6 15.3 %copy-start.20 = (f32[8,12,132]{2,1,0:T(8,128)S(1)}, f32[8,12,132]{2,1,0:T(8,128)}, u32[]{:S(2)}) copy-start(f32[8,12,132]{2,1,0:T(8,128)} %get-tuple-element.49) | copy-start | bytes 152068
  50.6 15.3 %copy-start.21 = (f32[8,12,132]{2,1,0:T(8,128)S(1)}, f32[8,12,132]{2,1,0:T(8,128)}, u32[]{:S(2)}) copy-start(f32[8,12,132]{2,1,0:T(8,128)} %get-tuple-element.75) | copy-start | bytes 152068
  50.6 15.3 %copy-start.22 = (f32[8,12,132]{2,1,0:T(8,128)S(1)}, f32[8,12,132]{2,1,0:T(8,128)}, u32[]{:S(2)}) copy-start(f32[8,12,132]{2,1,0:T(8,128)} %get-tuple-element.79) | copy-start | bytes 152068
  50.6 15.3 %copy-start.23 = (f32[8,12,132]{2,1,0:T(8,128)S(1)}, f32[8,12,132]{2,1,0:T(8,128)}, u32[]{:S(2)}) copy-start(f32[8,12,132]{2,1,0:T(8,128)} %get-tuple-element.80) | copy-start | bytes 152068
  50.6 15.3 %copy-start.24 = (f32[8,12,132]{2,1,0:T(8,128)S(1)}, f32[8,12,132]{2,1,0:T(8,128)}, u32[]{:S(2)}) copy-start(f32[8,12,132]{2,1,0:T(8,128)} %get-tuple-element.81) | copy-start | bytes 152068
  50.6 15.3 %copy-start.25 = (f32[8,12,132]{2,1,0:T(8,128)S(1)}, f32[8,12,132]{2,1,0:T(8,128)}, u32[]{:S(2)}) copy-start(f32[8,12,132]{2,1,0:T(8,128)} %get-tuple-element.82) | copy-start | bytes 152068
  71.4 2.8 %copy-start.29 = (f32[3,4096]{1,0:T(4,128)S(1)}, f32[3,4096]{1,0:T(4,128)}, u32[]{:S(2)}) copy-start(f32[3,4096]{1,0:T(4,128)} %copy-done.28) | copy-start | bytes 147460
  71.4 2.8 %copy-start.33 = (pred[32,1,128]{2,0,1:T(8,128)(4,1)S(1)}, pred[32,1,128]{2,0,1:T(8,128)(4,1)}, u32[]{:S(2)}) copy-start(pred[32,1,128]{2,0,1:T(8,128)(4,1)} %copy-done.32) | copy-start | bytes 12292
  71.4 2.9 %copy-start.31 = (f32[32,1,128]{2,1,0:T(1,128)S(1)}, f32[32,1,128]{2,1,0:T(1,128)}, u32[]{:S(2)}) copy-start(f32[32,1,128]{2,1,0:T(1,128)} %get-tuple-element.153) | copy-start | bytes 49156
  71.4 2.9 %copy-start.35 = (s32[4096]{0:T(1024)S(1)}, s32[4096]{0:T(1024)}, u32[]{:S(2)}) copy-start(s32[4096]{0:T(1024)} %get-tuple-element.157) | copy-start | bytes 49156
  71.4 2.9 %copy-start.37 = (s32[4096]{0:T(1024)S(1)}, s32[4096]{0:T(1024)}, u32[]{:S(2)}) copy-start(s32[4096]{0:T(1024)} %get-tuple-element.158) | copy-start | bytes 49156
  71.4 2.9 %copy-start.39 = (f32[4096]{0:T(1024)S(1)}, f32[4096]{0:T(1024)}, u32[]{:S(2)}) copy-start(f32[4096]{0:T(1024)} %copy-done.38) | copy-start | bytes 49156
